TPU v7x, 256 devices: a whole 4x4x8 slice. The times are simulated.
256 devices in a mesh: gx: 32 (over y, z), gy: 8 (over x, core).
Axes of the slice: x: 4, y: 4, z: 8, core: 2. Of those that a mesh axis runs over, the one named last changes fastest.
Arguments:
- features: bfloat16 [32, 4, 256, 1024], P(None, None, 'gx', 'gy'), may hold values from -8 to 8
- vessel_label: int32 [4, 256, 1024], P(None, 'gx', 'gy'), may hold values from 0 to 1, as said below
- conv_weight: bfloat16 [27, 32], replicated, may hold values from -0.21875 to 0.21875
- conv_bias: float32 [1], replicated, may hold values from -1.5 to 1.5
Outputs:
- cldice_loss: float32 [], replicated
- weight_grad: float32 [27, 32], replicated
- bias_grad: float32 [1], replicated
- feature_grad: bfloat16 [32, 4, 256, 1024], P(None, None, 'gx', 'gy')
Inputs may be any that keep to these rules, and one draw needn't show every extreme that they name: `vessel_label`: 1 marks a vessel voxel, 0 the background.
All inputs are finite; a program needn't handle non-finite values.
Results may differ from a plain program's by a relative error of at most 0.012.
Values may be sent and summed in bfloat16 or wider, within the bound.
No kernel may reach another device: no remote copies, remote signals or barrier semaphores. Data moves between devices by JAX's collectives and lax.ppermute only.
A program may use at most 64 MiB of HBM per device.

v0:
```python
import jax
import jax.numpy as jnp
from jax import lax
from jax.sharding import PartitionSpec as P

ITERS = 5


softmin_sharpness = 0.1
softness = 0.05


def padded_2(x, sides, width):
    for axis, dim in sides:
        size, length = (lax.axis_size(axis), x.shape[dim])
        up = [(i, (i + 1) % size) for i in range(size - 1)]
        down = [(j, i) for i, j in up]
        last = lax.slice_in_dim(x, length - width, length, axis=dim)
        initial = lax.slice_in_dim(x, 0, width, axis=dim)
        before = lax.ppermute(last, axis, up)
        after = lax.ppermute(initial, axis, down)
        x = jnp.concatenate([before, x, after], axis=dim)
    return x


def passed_along(value, axis, steps):
    count = lax.axis_size(axis)
    initial, last = (max(0, -steps), min(count, count - steps))
    return lax.ppermute(value, axis, [(source, source + steps) for source in range(initial, last)])


def soft_relu(source_grid):
    return softness * jax.nn.softplus(source_grid / softness)


def crop_cycle(array, amount):
    if amount == 0:
        return array
    return array[..., amount : array.shape[-2] - amount, amount : array.shape[-1] - amount]


def border_thickness(source_grid):
    widths = [(0, 0)] * (source_grid.ndim - 3) + [(1, 1), (0, 0), (0, 0)]
    return jnp.pad(source_grid, widths)


def soft_dilate(source_grid, cell_neighbourhood):
    scaled_powers = jnp.exp(border_thickness(source_grid) / softmin_sharpness)
    collapsed_aggregate = scaled_powers[:-2] + scaled_powers[1:-1] + scaled_powers[2:]
    collapsed_aggregate = (
        collapsed_aggregate[:, :-2] + collapsed_aggregate[:, 1:-1] + collapsed_aggregate[:, 2:]
    )
    collapsed_aggregate = (
        collapsed_aggregate[:, :, :-2]
        + collapsed_aggregate[:, :, 1:-1]
        + collapsed_aggregate[:, :, 2:]
    )
    return softmin_sharpness * jnp.log(collapsed_aggregate / 27.0) * cell_neighbourhood


def soft_erode(source_grid, cell_neighbourhood):
    scaled_powers = jnp.exp(-border_thickness(source_grid) / softmin_sharpness)
    middle_cell = scaled_powers[1:-1, 1:-1, 1:-1]
    neighbouring_cells = (
        scaled_powers[2:, 1:-1, 1:-1]
        + scaled_powers[:-2, 1:-1, 1:-1]
        + scaled_powers[1:-1, 2:, 1:-1]
        + scaled_powers[1:-1, :-2, 1:-1]
        + scaled_powers[1:-1, 1:-1, 2:]
        + scaled_powers[1:-1, 1:-1, :-2]
    )
    return (
        -softmin_sharpness
        * jnp.log(middle_cell / 3.0 + neighbouring_cells / 9.0)
        * cell_neighbourhood
    )


def soft_open(source_grid, cell_neighbourhood):
    return soft_dilate(
        soft_erode(source_grid, crop_cycle(cell_neighbourhood, 1)),
        crop_cycle(cell_neighbourhood, 2),
    )


def skeleton(source_grid, cell_neighbourhood, cycle_width):
    current = source_grid
    mask_now = cell_neighbourhood
    opened = soft_open(crop_cycle(current, cycle_width - 2), crop_cycle(mask_now, cycle_width - 2))
    skeleton_sum = soft_relu(crop_cycle(current, cycle_width) - opened)
    for erosion in range(1, cycle_width - 1):
        mask_now = crop_cycle(mask_now, 1)
        current = soft_erode(current, mask_now)
        cycle_now = cycle_width - erosion
        opened = soft_open(crop_cycle(current, cycle_now - 2), crop_cycle(mask_now, cycle_now - 2))
        change_term = soft_relu(crop_cycle(current, cycle_now) - opened)
        skeleton_sum = skeleton_sum + soft_relu(change_term - skeleton_sum * change_term)
    return skeleton_sum


def topology_loss(totals):
    precision = (totals[0] + 1.0) / (totals[1] + 1.0)
    sensitivity = (totals[2] + 1.0) / (totals[3] + 1.0)
    return 1.0 - 2.0 * precision * sensitivity / (precision + sensitivity)


def inside_mask(cycle_width, tile_rows, tile_cols):
    row_start = lax.axis_index("gx") * tile_rows - cycle_width
    col_start = lax.axis_index("gy") * tile_cols - cycle_width
    row_ids = row_start + jnp.arange(tile_rows + 2 * cycle_width, dtype=jnp.int32)
    col_ids = col_start + jnp.arange(tile_cols + 2 * cycle_width, dtype=jnp.int32)
    row_inside = (row_ids >= 0) & (row_ids < tile_rows * lax.axis_size("gx"))
    col_inside = (col_ids >= 0) & (col_ids < tile_cols * lax.axis_size("gy"))
    return (row_inside[:, None] & col_inside[None, :]).astype(jnp.float32)


def intersection_sums(prob_cycle, label_cycle, label_skeleton, cell_neighbourhood, cycle_width):
    pred_skeleton = skeleton(prob_cycle, cell_neighbourhood, cycle_width)
    prob_own = crop_cycle(prob_cycle, cycle_width)
    label_own = crop_cycle(label_cycle, cycle_width)
    return (
        jnp.sum(pred_skeleton * label_own),
        jnp.sum(pred_skeleton),
        jnp.sum(label_skeleton * prob_own),
        jnp.sum(label_skeleton),
    )


def extend(block, halo_width):
    return padded_2(block, (("gx", 2), ("gy", 3)), halo_width)


def convolve(feature_cycle, conv_weight, conv_bias):
    padded = border_thickness(feature_cycle)
    products = jnp.einsum("kc,czxy->kzxy", conv_weight, padded, preferred_element_type=jnp.float32)
    depth_cells = feature_cycle.shape[1]
    out_rows = feature_cycle.shape[2] - 2
    out_cols = feature_cycle.shape[3] - 2
    logits = jnp.zeros((depth_cells, out_rows, out_cols), jnp.float32) + conv_bias[0]
    for position in range(27):
        depth_shift, row_shift, col_shift = (position // 9, position // 3 % 3, position % 3)
        logits = (
            logits
            + products[
                position,
                depth_shift : depth_shift + depth_cells,
                row_shift : row_shift + out_rows,
                col_shift : col_shift + out_cols,
            ]
        )
    return (padded, logits)


def shifted_stack(grad_logits):
    pieces = []
    for position in range(27):
        depth_shift, row_shift, col_shift = (position // 9, position // 3 % 3, position % 3)
        pieces.append(
            jnp.pad(
                grad_logits,
                (
                    (depth_shift, 2 - depth_shift),
                    (row_shift, 2 - row_shift),
                    (col_shift, 2 - col_shift),
                ),
            )
        )
    stacked = jnp.stack(pieces)
    upper_part = stacked.astype(jnp.bfloat16)
    lower_part = (stacked - upper_part.astype(jnp.float32)).astype(jnp.bfloat16)
    return (upper_part, lower_part)


def weight_terms(upper_part, lower_part, padded):
    first = jnp.einsum("kzxy,czxy->kc", upper_part, padded, preferred_element_type=jnp.float32)
    return first + jnp.einsum(
        "kzxy,czxy->kc", lower_part, padded, preferred_element_type=jnp.float32
    )


def feature_terms(upper_part, lower_part, conv_weight):
    first = jnp.einsum("kc,kzxy->czxy", conv_weight, upper_part, preferred_element_type=jnp.float32)
    collapsed_aggregate = first + jnp.einsum(
        "kc,kzxy->czxy", conv_weight, lower_part, preferred_element_type=jnp.float32
    )
    return collapsed_aggregate[:, 1:-1]


def fold_back(gradient, halo_width):
    middle = gradient[..., halo_width : gradient.shape[-1] - halo_width]
    for shift_by in (1, -1):
        if shift_by == 1:
            rim_cells = gradient[..., gradient.shape[-1] - halo_width :]
        else:
            rim_cells = gradient[..., :halo_width]
        arrived = passed_along(rim_cells.astype(jnp.bfloat16), "gy", shift_by).astype(
            rim_cells.dtype
        )
        if shift_by == 1:
            middle = middle.at[..., :halo_width].add(arrived)
        else:
            middle = middle.at[..., middle.shape[-1] - halo_width :].add(arrived)
    result = middle[..., halo_width : middle.shape[-2] - halo_width, :]
    for shift_by in (1, -1):
        if shift_by == 1:
            rim_cells = middle[..., middle.shape[-2] - halo_width :, :]
        else:
            rim_cells = middle[..., :halo_width, :]
        arrived = passed_along(rim_cells.astype(jnp.bfloat16), "gx", shift_by).astype(
            rim_cells.dtype
        )
        if shift_by == 1:
            result = result.at[..., :halo_width, :].add(arrived)
        else:
            result = result.at[..., result.shape[-2] - halo_width :, :].add(arrived)
    return result


def local(features, vessel_label, conv_weight, conv_bias):
    channels, depth_cells, tile_rows, tile_cols = features.shape
    voxels = float(depth_cells * tile_rows * lax.axis_size("gx") * tile_cols * lax.axis_size("gy"))
    skel_reach = ITERS + 2
    cell_neighbourhood = inside_mask(skel_reach, tile_rows, tile_cols)
    fold_width = skel_reach + 1
    joined = jnp.concatenate([features, vessel_label.astype(jnp.bfloat16)[None]], axis=0)
    widened = extend(joined, fold_width)
    padded, logits = convolve(widened[:channels], conv_weight, conv_bias)
    label_cycle = crop_cycle(widened[channels].astype(jnp.float32), 1)
    label_skeleton = skeleton(label_cycle, cell_neighbourhood, skel_reach)

    def local_sums(logit_field):
        prob_cycle = jax.nn.sigmoid(logit_field) * cell_neighbourhood
        return intersection_sums(
            prob_cycle, label_cycle, label_skeleton, cell_neighbourhood, skel_reach
        )

    partial_sums, pullback = jax.vjp(local_sums, logits)

    def backward(cotangents):
        return jnp.stack([pullback(entry)[0] for entry in cotangents])

    totals = lax.psum(jnp.stack(partial_sums), ("gx", "gy"))
    loss_value, slopes = jax.value_and_grad(topology_loss)(totals)
    grad_logits = backward([tuple((slopes[entry] for entry in range(4)))])[0]
    upper_part, lower_part = shifted_stack(grad_logits)
    local_weight = weight_terms(upper_part, lower_part, padded)
    weight_grad, bias_grad = lax.psum((local_weight, jnp.sum(grad_logits)[None]), ("gx", "gy"))
    grad_own = fold_back(feature_terms(upper_part, lower_part, conv_weight), fold_width) * voxels
    return (loss_value, weight_grad, bias_grad, grad_own.astype(jnp.bfloat16))


def solution(mesh):
    in_specs = (P(None, None, "gx", "gy"), P(None, "gx", "gy"), P(), P())
    out_specs = (P(), P(), P(), P(None, None, "gx", "gy"))
    return jax.shard_map(local, mesh=mesh, in_specs=in_specs, out_specs=out_specs, check_vma=False)
```

profile of v0, /device:TPU:1, one launch (start us, length us, event | category | flops | bytes accessed | tf_op | source)
XLA Modules:
  0.0 265.2 jit_solution(332422820204132034)
XLA Ops:
  0.6 0.7 convert_bitcast_fusion
  1.4 1.1 copy_dynamic-update-slice_fusion
  2.5 1.3 collective-permute-start.1
  3.8 5.0 %collective-permute-start = (bf16[33,4,8,128]{3,0,2,1:T(8,128)(2,1)S(1)}, bf16[33,4,8,128]{3,0,2,1:T(8,128)(2,1)S(1)}, u32[]{:S(2)}, u32[]{:S(2)}) collective-permute-start(bf16[33,4,8,128]{3,0,2,1:T(8,128)(2,1)S(1)} %constant_dynamic-update-slice_fusion), channel_id=1, source_target_pairs={{0,8},{8,16},{16,24},{24,32},{32,40},{40,48},{48,56},{56,64},{64,7... | collective-permute-start | bytes 811016 | tf_op jit(solution)/shard_map/ppermute | solution.py:20
  9.6 0.7 fusion.371
  10.9 0.7 fusion.373
  11.7 0.7 fusion.374
  12.4 0.9 collective-permute-done
  13.7 1.3 copy.71
  15.7 5.3 %collective-permute-start.3 = (bf16[33,4,24,8]{0,3,2,1:T(8,128)(2,1)S(1)}, bf16[33,4,24,8]{0,3,2,1:T(8,128)(2,1)}, u32[]{:S(2)}, u32[]{:S(2)}) collective-permute-start(bf16[33,4,24,8]{0,3,2,1:T(8,128)(2,1)S(1)} %copy.72), channel_id=1, source_target_pairs={{1,0},{2,1},{3,2},{4,3},{5,4},{6,5},{7,6},{9,8},{10,9},{11,10},{12... | collective-permute-start | bytes 152072 | tf_op jit(solution)/shard_map/ppermute | solution.py:21
  21.1 3.0 %collective-permute-start.2 = (bf16[33,4,24,8]{0,3,2,1:T(8,128)(2,1)}, bf16[33,4,24,8]{0,3,2,1:T(8,128)(2,1)S(1)}, u32[]{:S(2)}, u32[]{:S(2)}) collective-permute-start(bf16[33,4,24,8]{0,3,2,1:T(8,128)(2,1)} %copy.71), channel_id=1, source_target_pairs={{0,1},{1,2},{2,3},{3,4},{4,5},{5,6},{6,7},{8,9},{9,10},{10,11},{11... | collective-permute-start | bytes 152072 | tf_op jit(solution)/shard_map/ppermute | solution.py:20
  24.8 2.2 collective-permute-done.2
  27.0 0.7 copy.73
  27.7 1.6 copy.74
  29.8 1.2 pad_maximum_fusion
  31.0 1.3 copy-done.2
  33.0 2.3 copy.128
  39.4 0.9 log_multiply_fusion.3
  40.8 0.9 log_multiply_fusion.10
  41.8 0.9 log_multiply_fusion.4
  42.9 0.9 log_multiply_fusion.8
  44.0 1.5 multiply_reduce_fusion
  45.4 0.9 multiply_reduce_fusion.1
  46.3 2.6 pad_maximum_fusion.2
  48.9 83.7 %psum.21 = f32[4]{0:T(128)S(1)} all-reduce(f32[4]{0:T(128)S(1)} %pad_maximum_fusion.2), channel_id=1, replica_groups=mesh['gx'=32,'gy'=8] {'gx','gy'}, use_global_device_ids=true, to_apply=%region_4.6 | all-reduce | flops 4 | bytes 32 | tf_op jit(solution)/shard_map/psum | solution.py:242
  136.9 1.5 divide_multiply_fusion.5
  139.2 1.0 broadcast_multiply_fusion.15
  140.3 1.0 broadcast_multiply_fusion.16
  141.5 1.0 broadcast_multiply_fusion.5
  143.1 0.9 broadcast_multiply_fusion.7
  146.6 0.8 fusion.327
  149.8 1.8 fusion.5
  151.6 5.3 %fusion.379 = (bf16[32,6,24,144]{0,3,2,1:T(8,128)(2,1)S(1)}, f32[32,6,24,144]{0,3,2,1:T(8,128)}) fusion(f32[6,24,144,32]{3,2,1,0:T(8,128)S(1)} %fusion.5, bf16[27,32]{1,0:T(8,128)(2,1)S(1)} %copy-done, bf16[27,6,24,144]{3,2,1,0:T(8,128)(2,1)S(1)} %get-tuple-element.140), kind=kOutput, calls=%fused_computation.833 | convolution fusion | flops 37158912 | bytes 7756992 | tf_op jit(solution)/shard_map/kc,kzxy->czxy/dot_general | solution.py:183
  156.9 2.9 %collective-permute-start.4 = (bf16[32,4,24,8]{0,3,2,1:T(8,128)(2,1)S(1)}, bf16[32,4,24,8]{0,3,2,1:T(8,128)(2,1)S(1)}, u32[]{:S(2)}, u32[]{:S(2)}) collective-permute-start(bf16[32,4,24,8]{0,3,2,1:T(8,128)(2,1)S(1)} %get-tuple-element.213), channel_id=1, source_target_pairs={{0,1},{1,2},{2,3},{3,4},{4,5},{5,6},{6,7},{8,9},{9,10},{10,11},{11... | collective-permute-start | bytes 147464 | tf_op jit(solution)/shard_map/ppermute | solution.py:29
  159.8 1.3 fusion.17
  161.2 2.1 collective-permute-start.5
  163.3 3.2 %slice.1858 = f32[32,4,24,128]{0,3,2,1:T(8,128)S(1)} slice(f32[32,6,24,144]{0,3,2,1:T(8,128)} %get-tuple-element.273), slice={[0:32], [1:5], [0:24], [8:136]} | slice | bytes 3145728 | tf_op jit(solution)/shard_map/slice | solution.py:190
  166.6 1.0 fusion.28
  168.3 0.7 convert.10
  169.0 1.9 copy-done.1
  170.9 1.1 fusion.368
  172.0 2.4 copy.86
  175.0 1.3 collective-permute-start.7
  176.3 4.3 %collective-permute-start.6 = (bf16[32,4,8,128]{3,2,1,0:T(8,128)(2,1)}, bf16[32,4,8,128]{3,2,1,0:T(8,128)(2,1)S(1)}, u32[]{:S(2)}, u32[]{:S(2)}) collective-permute-start(bf16[32,4,8,128]{3,2,1,0:T(8,128)(2,1)} %copy.86), channel_id=1, source_target_pairs={{0,8},{8,16},{16,24},{24,32},{32,40},{40,48},{48,56},{56,64},{64,7... | collective-permute-start | bytes 786440 | tf_op jit(solution)/shard_map/ppermute | solution.py:29
  180.6 2.7 %fusion.22 = f32[27,32]{1,0:T(8,128)S(1)} fusion(f32[27,32]{1,0:T(8,128)S(1)} %fusion.17, bf16[27,6,24,144]{3,2,1,0:T(8,128)(2,1)S(1)} %get-tuple-element.141, bf16[33,4,24,144]{3,0,2,1:T(8,128)(2,1)} %copy-done.2), kind=kOutput, calls=%fused_computation.19 | convolution fusion | flops 35832672 | bytes 2699520 | tf_op jit(solution)/shard_map/kzxy,czxy->kc/dot_general | solution.py:175
  183.3 76.3 %all-reduce.209 = (f32[27,32]{1,0:T(8,128)}, f32[1]{0:T(128)}) all-reduce(f32[27,32]{1,0:T(8,128)S(1)} %fusion.22, f32[1]{0:T(128)} %bitcast.63), channel_id=1, replica_groups=mesh['gx'=32,'gy'=8] {'gx','gy'}, use_global_device_ids=true, to_apply=%region_5.7 | all-reduce | flops 865 | bytes 6920 | tf_op jit(solution)/shard_map/psum | solution.py:247
  260.6 2.2 fusion.11
  262.8 1.3 copy.90
  (196 shorter events, 18.3 us)
Async XLA Ops:
  0.6 31.7 %copy-start = (bf16[27,32]{1,0:T(8,128)(2,1)S(1)}, bf16[27,32]{1,0:T(8,128)(2,1)}, u32[]{:S(2)}) copy-start(bf16[27,32]{1,0:T(8,128)(2,1)} %param.19) | copy-start | bytes 5188
  2.5 9.9 %collective-permute-start.1 = (bf16[33,4,8,128]{3,0,2,1:T(8,128)(2,1)S(1)}, bf16[33,4,8,128]{3,0,2,1:T(8,128)(2,1)S(1)}, u32[]{:S(2)}, u32[]{:S(2)}) collective-permute-start(bf16[33,4,8,128]{3,0,2,1:T(8,128)(2,1)S(1)} %constant_dynamic-update-slice_fusion), channel_id=1, source_target_pairs={{8,0},{16,8},{24,16},{32,24},{40,32},{48,40},{56,48},{64,56},{72,6... | collective-permute-start | bytes 811016 | tf_op jit(solution)/shard_map/ppermute | solution.py:21
  3.8 9.5 %collective-permute-start = (bf16[33,4,8,128]{3,0,2,1:T(8,128)(2,1)S(1)}, bf16[33,4,8,128]{3,0,2,1:T(8,128)(2,1)S(1)}, u32[]{:S(2)}, u32[]{:S(2)}) collective-permute-start(bf16[33,4,8,128]{3,0,2,1:T(8,128)(2,1)S(1)} %constant_dynamic-update-slice_fusion), channel_id=1, source_target_pairs={{0,8},{8,16},{16,24},{24,32},{32,40},{40,48},{48,56},{56,64},{64,7... | collective-permute-start | bytes 811016 | tf_op jit(solution)/shard_map/ppermute | solution.py:20
  15.7 12.0 %collective-permute-start.3 = (bf16[33,4,24,8]{0,3,2,1:T(8,128)(2,1)S(1)}, bf16[33,4,24,8]{0,3,2,1:T(8,128)(2,1)}, u32[]{:S(2)}, u32[]{:S(2)}) collective-permute-start(bf16[33,4,24,8]{0,3,2,1:T(8,128)(2,1)S(1)} %copy.72), channel_id=1, source_target_pairs={{1,0},{2,1},{3,2},{4,3},{5,4},{6,5},{7,6},{9,8},{10,9},{11,10},{12... | collective-permute-start | bytes 152072 | tf_op jit(solution)/shard_map/ppermute | solution.py:21
  21.1 5.9 %collective-permute-start.2 = (bf16[33,4,24,8]{0,3,2,1:T(8,128)(2,1)}, bf16[33,4,24,8]{0,3,2,1:T(8,128)(2,1)S(1)}, u32[]{:S(2)}, u32[]{:S(2)}) collective-permute-start(bf16[33,4,24,8]{0,3,2,1:T(8,128)(2,1)} %copy.71), channel_id=1, source_target_pairs={{0,1},{1,2},{2,3},{3,4},{4,5},{5,6},{6,7},{8,9},{9,10},{10,11},{11... | collective-permute-start | bytes 152072 | tf_op jit(solution)/shard_map/ppermute | solution.py:20
  31.0 1.3 copy-start.2
  35.8 1.9 copy-start.8
  37.7 1.7 copy-start.7
  44.0 96.3 %copy-start.4 = (f32[4,10,130]{2,1,0:T(8,128)S(1)}, f32[4,10,130]{2,1,0:T(8,128)}, u32[]{:S(2)}) copy-start(f32[4,10,130]{2,1,0:T(8,128)} %get-tuple-element.198) | copy-start | bytes 62404
  45.4 98.8 %copy-start.9 = (f32[16,136]{1,0:T(8,128)S(1)}, f32[16,136]{1,0:T(8,128)}, u32[]{:S(2)}) copy-start(f32[16,136]{1,0:T(8,128)} %get-tuple-element.230) | copy-start | bytes 26116
  138.9 6.1 %copy-start.6 = (f32[18,138]{1,0:T(8,128)S(1)}, f32[18,138]{1,0:T(8,128)}, u32[]{:S(2)}) copy-start(f32[18,138]{1,0:T(8,128)} %get-tuple-element.232) | copy-start | bytes 29812
  140.2 5.2 %copy-start.5 = (f32[20,140]{1,0:T(8,128)S(1)}, f32[20,140]{1,0:T(8,128)}, u32[]{:S(2)}) copy-start(f32[20,140]{1,0:T(8,128)} %get-tuple-element.234) | copy-start | bytes 33604
  141.3 4.5 %copy-start.10 = (f32[4,8,128]{2,1,0:T(8,128)S(1)}, f32[4,8,128]{2,1,0:T(8,128)}, u32[]{:S(2)}) copy-start(f32[4,8,128]{2,1,0:T(8,128)} %get-tuple-element.209) | copy-start | bytes 49156
  151.6 8.2 %copy-start.3 = (bf16[33,4,24,144]{3,0,2,1:T(8,128)(2,1)S(1)}, bf16[33,4,24,144]{3,0,2,1:T(8,128)(2,1)}, u32[]{:S(2)}) copy-start(bf16[33,4,24,144]{3,0,2,1:T(8,128)(2,1)} %copy-done.2) | copy-start | bytes 2737156
  156.9 9.6 %collective-permute-start.4 = (bf16[32,4,24,8]{0,3,2,1:T(8,128)(2,1)S(1)}, bf16[32,4,24,8]{0,3,2,1:T(8,128)(2,1)S(1)}, u32[]{:S(2)}, u32[]{:S(2)}) collective-permute-start(bf16[32,4,24,8]{0,3,2,1:T(8,128)(2,1)S(1)} %get-tuple-element.213), channel_id=1, source_target_pairs={{0,1},{1,2},{2,3},{3,4},{4,5},{5,6},{6,7},{8,9},{9,10},{10,11},{11... | collective-permute-start | bytes 147464 | tf_op jit(solution)/shard_map/ppermute | solution.py:29
  161.2 7.0 %collective-permute-start.5 = (bf16[32,4,24,8]{0,3,2,1:T(8,128)(2,1)S(1)}, bf16[32,4,24,8]{0,3,2,1:T(8,128)(2,1)S(1)}, u32[]{:S(2)}, u32[]{:S(2)}) collective-permute-start(bf16[32,4,24,8]{0,3,2,1:T(8,128)(2,1)S(1)} %get-tuple-element.212), channel_id=1, source_target_pairs={{1,0},{2,1},{3,2},{4,3},{5,4},{6,5},{7,6},{9,8},{10,9},{11,10},{12... | collective-permute-start | bytes 147464 | tf_op jit(solution)/shard_map/ppermute | solution.py:29
  168.3 2.6 copy-start.1
  175.0 85.1 %collective-permute-start.7 = (bf16[32,4,8,128]{3,2,1,0:T(8,128)(2,1)S(1)}, bf16[32,4,8,128]{3,2,1,0:T(8,128)(2,1)S(1)}, u32[]{:S(2)}, u32[]{:S(2)}) collective-permute-start(bf16[32,4,8,128]{3,2,1,0:T(8,128)(2,1)S(1)} %copy.88), channel_id=1, source_target_pairs={{8,0},{16,8},{24,16},{32,24},{40,32},{48,40},{56,48},{64,56},{72,6... | collective-permute-start | bytes 786440 | tf_op jit(solution)/shard_map/ppermute | solution.py:29
  176.3 83.3 %collective-permute-start.6 = (bf16[32,4,8,128]{3,2,1,0:T(8,128)(2,1)}, bf16[32,4,8,128]{3,2,1,0:T(8,128)(2,1)S(1)}, u32[]{:S(2)}, u32[]{:S(2)}) collective-permute-start(bf16[32,4,8,128]{3,2,1,0:T(8,128)(2,1)} %copy.86), channel_id=1, source_target_pairs={{0,8},{8,16},{16,24},{24,32},{32,40},{40,48},{48,56},{56,64},{64,7... | collective-permute-start | bytes 786440 | tf_op jit(solution)/shard_map/ppermute | solution.py:29
where the time goes:
time: 266 us; the launch traced here: 265 us
  blocking collectives  160 us (60%)
  other arithmetic  33 us (12%)
  starting transfers between devices  25.3 us (10%)
  local copies, waits for them, and re-layouts  24.9 us (9%)
  matrix products  11.7 us (4%)
  between operations  6.76 us (3%)
  waiting for transfers between devices  3.59 us (1%)
    psum x1, blocking collectives, local(): totals = lax.psum(jnp.stack(partial_sums), ('gx', 'gy'))  83.7 us
    psum x1, blocking collectives, local(): lax.psum((local_weight, jnp.sum(grad_logits)[None]), ('gx', 'gy'))  76.3 us
    ppermute x4, starting transfers between devices, passed_along(): lax.ppermute(value, axis, [(source, source + steps) for source in range(i...  10.6 us
    ppermute x2, starting transfers between devices, padded_2(): before = lax.ppermute(last, axis, up)  8.04 us
    unnamed x51, local copies, waits for them, and re-layouts  7.28 us
    ppermute x2, starting transfers between devices, padded_2(): after = lax.ppermute(initial, axis, down)  6.62 us
    mul x11, other arithmetic, soft_erode(): -softmin_sharpness * jnp.log(middle_cell / 3.0 + neighbouring_cells / 9.0)  5.88 us
  transfers between devices with their start and end apart: 8, of which 3 were waited for; matrix products, arithmetic and copies ran while one was open for 5% of the time, Pallas kernels for 0%

commit v1 on v0

v1 whole, which is shorter than its diff:
```python
import jax
import jax.numpy as jnp
from jax import lax
from jax.experimental import pallas as pl
from jax.experimental.pallas import tpu as pltpu
from jax.sharding import PartitionSpec as P

ITERS = 5
F32 = jnp.float32
BF16 = jnp.bfloat16
SHARP = 10.0
SOFT = 0.05
EDGE = 16
VMEM_LIMIT = 48 * 1024 * 1024


def iota(shape, dim):
    return lax.broadcasted_iota(jnp.int32, shape, dim)


def dot(a, b, dims, precision=None):
    return lax.dot_general(a, b, (dims, ((), ())), precision=precision, preferred_element_type=F32)


def edge_row(q):
    return jnp.where(q < 8, q, jnp.where(q == 8, 8, jnp.where(q == 15, -1, -100)))


def weight_matrix(w):
    spread = jnp.where((iota((32, 256), 1) >> 3) == iota((32, 256), 0), 1.0, 0.0).astype(BF16)
    by_lane = dot(w, spread, ((1,), (0,))).astype(BF16)
    row = iota((144, 27), 0)
    ad = row >> 4
    base = ad + 6 * (jnp.where(ad >= 3, 1, 0) + jnp.where(ad >= 6, 1, 0))
    col = iota((144, 27), 1)
    offset = (iota((144, 256), 1) & 7) - edge_row(iota((144, 256), 0) & 15) + 1
    matrix = jnp.zeros((144, 256), F32)
    for b in range(3):
        pick = jnp.where(col == base + 3 * b, 1.0, 0.0).astype(BF16)
        matrix = matrix + jnp.where(offset == b, dot(pick, by_lane, ((1,), (0,))), 0.0)
    return matrix.astype(BF16)


def partial_logits_kernel(w_ref, f_ref, lab_ref, a_ref, near_ref, far_ref):
    matrix = weight_matrix(w_ref[...])
    a_ref[...] = matrix
    lane = iota((16, 128), 1)
    terms = [
        dot(matrix, f_ref[:, z].reshape(256, 128), ((1,), (0,))).reshape(3, 3, 16, 128)
        for z in range(4)
    ]
    corner = jnp.zeros((16, 128), F32)
    for z in range(4):
        byd = []
        for d in range(3):
            byd.append(sum(terms[z + a - 1][a, d] for a in range(3) if 0 <= z + a - 1 < 4))
        main = byd[1]
        main = main + jnp.where(lane >= 1, pltpu.roll(byd[0], 1, 1), 0.0)
        main = main + jnp.where(lane <= 126, pltpu.roll(byd[2], 127, 1), 0.0)
        near_ref[16 * z : 16 * z + 16] = main
        far_ref[16 * z : 16 * z + 16] = main
        shift = 32 * z + 17
        corner = jnp.where(lane == shift - 1, pltpu.roll(byd[0], shift, 1), corner)
        corner = jnp.where(lane == shift, pltpu.roll(byd[2], shift, 1), corner)
    near_ref[64:80] = corner
    far_ref[64:80] = corner
    near_ref[80:112] = lab_ref[...].reshape(32, 128).astype(F32)


def rows_kernel(own_ref, m1_ref, p1_ref, m2_ref, p2_ref, main_ref, lab_ref, right_ref, left_ref):
    blocks = [m2_ref, m1_ref, own_ref, p1_ref, p2_ref]
    sub = iota((8, 128), 0)

    def assemble(start):
        tiles = []
        for t in range(5):
            tile = blocks[t][start : start + 8]
            if t > 0:
                tile = tile + jnp.where(sub == 0, blocks[t - 1][start + 8 : start + 16], 0.0)
            if t < 4:
                tile = tile + jnp.where(sub == 7, blocks[t + 1][start + 8 : start + 16], 0.0)
            tiles.append(tile)
        return jnp.concatenate(tiles, axis=0)

    corner = assemble(64)
    group = iota((64, 128), 1) >> 5
    right = jnp.zeros((64, 128), F32)
    left = jnp.zeros((64, 128), F32)
    for z in range(4):
        main = assemble(16 * z)
        main_ref[z] = main
        lab = jnp.concatenate(
            [ref[80 + 8 * z : 88 + 8 * z] for ref in (m1_ref, own_ref, p1_ref)], axis=0
        )
        lab_ref[z] = lab
        both = jnp.concatenate([main, lab], axis=0)
        right = jnp.where(group == z, pltpu.roll(both, (32 * z + 16) % 128, 1), right)
        left = jnp.where(group == z, pltpu.roll(both, 32 * z, 1), left)
    main_ref[4] = corner
    spread = jnp.concatenate([corner, jnp.zeros((24, 128), F32)], axis=0)
    place = iota((64, 128), 1) & 31
    right_ref[...] = jnp.where(place < 16, right, spread)
    left_ref[...] = jnp.where(place < 16, left, spread)


def shift_rows(x, s):
    return pltpu.roll(x, s % x.shape[0], 0)


def shift_cols(x, s):
    return pltpu.roll(x, s % x.shape[1], 1)


def cross(fields, outside):
    result = []
    for z in range(4):
        x = fields[z]
        around = shift_rows(x, 1) + shift_rows(x, -1) + shift_cols(x, 1) + shift_cols(x, -1)
        before = fields[z - 1] if z > 0 else outside
        after = fields[z + 1] if z < 3 else outside
        result.append((around + (before + after)) * (1.0 / 9.0) + x * (1.0 / 3.0))
    return result


def box(fields, outside, crop):
    result = []
    for z in range(4):
        before = fields[z - 1] if z > 0 else outside
        after = fields[z + 1] if z < 3 else outside
        x = fields[z] + (before + after)
        x = x + shift_rows(x, 1) + shift_rows(x, -1)
        if crop:
            x = x[8:32]
        result.append(x + shift_cols(x, 1) + shift_cols(x, -1))
    return result


def inverse(x):
    return 1.0 / x


def forward(e0, q0, inside, crop, keep):
    def middle(x):
        return x[8:32] if crop else x

    e, q, s = e0, q0, None
    for i in range(ITERS + 1):
        e = [jnp.where(inside, x, 1.0) for x in cross(e, 1.0)]
        q_next = [inverse(x) for x in e]
        mean = box(q_next, 1.0, crop)
        s_next = []
        for z in range(4):
            d_inv = inverse(mean[z] * (1.0 / 27.0))
            qz = middle(q[z])
            ratio = qz * d_inv
            ratio = ratio * ratio
            log_term = jnp.log(1.0 + ratio)
            change = SOFT * log_term
            if i == 0:
                s_next.append(change)
                keep(i, z, qz, d_inv, ratio, None, None, None)
            else:
                rest = 1.0 - s[z]
                power = jnp.exp(log_term * rest)
                s_next.append(s[z] + SOFT * jnp.log(1.0 + power))
                keep(i, z, qz, d_inv, ratio, change, rest, power)
        s, q = s_next, q_next
    return s, q


def skeleton_kernel(
    bias_ref, f_ref, main_ref, lab_ref, from_left_ref, from_right_ref,
    grad_ref, sums_ref,
    qs_ref, ds_ref, rs_ref, gain_ref, direct_ref,
):
    row_ids = lax.axis_index("gx") * 8 - 16 + iota((40, 256), 0)
    lane = iota((40, 256), 1)
    col = jnp.where(lane < 144, lane, lane - 256)
    col_ids = lax.axis_index("gy") * 128 + col
    inside = (row_ids >= 0) & (row_ids < lax.axis_size("gx") * 8)
    inside = inside & (col_ids >= 0) & (col_ids < lax.axis_size("gy") * 128) & (col >= -16)
    inside_f = jnp.where(inside, 1.0, 0.0)
    inner = inside_f[8:32]
    inner_b = inner > 0.5
    bias = bias_ref[0]

    lane1 = iota((64, 128), 1)
    from_left = from_left_ref[...]
    from_right = from_right_ref[...]
    corner = main_ref[4]
    lane40 = lane1[:40]
    e0, q0, slope, probs, labels = [], [], [], [], []
    for z in range(4):
        start = 32 * z
        extra_left = pltpu.roll(from_left, (112 - start) % 128, 1)
        extra_right = pltpu.roll(from_right, (128 - start) % 128, 1)
        extra = jnp.where(lane1 >= 112, extra_left, jnp.where(lane1 < 16, extra_right, 0.0))
        at_zero = pltpu.roll(from_left[:40], (128 - start - 16) % 128, 1)
        at_last = pltpu.roll(from_right[:40], (110 - start) % 128, 1)
        main = main_ref[z]
        main = main + jnp.where(lane40 == 0, at_zero, jnp.where(lane40 == 127, at_last, 0.0))
        own_zero = pltpu.roll(corner, (128 - start - 16) % 128, 1)
        own_last = pltpu.roll(corner, (110 - start) % 128, 1)
        tail = extra[:40]
        tail = tail + jnp.where(lane40 == 0, own_zero, jnp.where(lane40 == 127, own_last, 0.0))
        logits = jnp.concatenate([main, tail], axis=1) + bias
        small = jnp.exp(-jnp.abs(logits))
        scale = inverse(1.0 + small)
        prob = jnp.where(logits >= 0.0, scale, small * scale)
        prob = jnp.where(inside, prob, 0.0)
        e = jnp.exp(-SHARP * prob)
        e0.append(e)
        q0.append(inverse(e))
        weight = (small * scale) * scale
        slope.append(((-SHARP) * e * weight)[8:32] * inner)
        probs.append((prob[8:32], weight[8:32]))
        labels.append(jnp.concatenate([lab_ref[z], extra[40:]], axis=1))

    low, high = jnp.exp(-SHARP * jnp.ones((24, 256), F32)), jnp.exp(SHARP * jnp.ones((24, 256), F32))
    true_skel, _ = forward(
        [jnp.where(x > 0.5, low, 1.0) for x in labels],
        [jnp.where(x > 0.5, high, 1.0) for x in labels],
        inner_b, False, lambda *factors: None,
    )

    def keep(i, z, qz, d_inv, ratio, change, rest, power):
        qs_ref[i, z] = qz
        ds_ref[i, z] = d_inv
        part = (-2.0 * SOFT) * (ratio * inverse(1.0 + ratio))
        if i > 0:
            share = power * inverse(1.0 + power)
            part = part * (share * rest)
            gain_ref[i, z] = 1.0 - share * change
        rs_ref[i, z] = part

    pred_skel, q_last = forward(e0, q0, inside, True, keep)

    def own(x):
        return x[8:16, :128]

    def total(values):
        acc = values[0] + values[1] + values[2] + values[3]
        return jnp.sum(jnp.sum(acc, axis=1, keepdims=True), axis=0, keepdims=True)

    t0 = total([own(pred_skel[z] * labels[z]) for z in range(4)])
    t1 = total([own(pred_skel[z]) for z in range(4)])
    t2 = total([own(true_skel[z] * probs[z][0]) for z in range(4)])
    t3 = total([own(true_skel[z]) for z in range(4)])

    weights = [labels, [inner] * 4]
    running = [jnp.ones((24, 256), F32)] * 4
    deep = [None, None]
    for i in range(ITERS, -1, -1):
        coefs = []
        for z in range(4):
            coefs.append(rs_ref[i, z] * running[z])
            if i > 0:
                running[z] = running[z] * gain_ref[i, z]
        for f in range(2):
            scaled = [coefs[z] * weights[f][z] for z in range(4)]
            spread = box([scaled[z] * ds_ref[i, z] for z in range(4)], 0.0, False)
            q_of = [q_last[z][8:32] if i == ITERS else qs_ref[i + 1, z] for z in range(4)]
            incoming = []
            for z in range(4):
                value = spread[z] * (q_of[z] * q_of[z]) * (-1.0 / 27.0)
                if deep[f] is not None:
                    value = value + deep[f][z]
                incoming.append(value * inner)
            moved = cross(incoming, 0.0)
            deep[f] = [moved[z] + scaled[z] * qs_ref[i, z] for z in range(4)]
    fields = [
        [deep[0][z] * slope[z] for z in range(4)],
        [deep[1][z] * slope[z] for z in range(4)],
        [true_skel[z] * probs[z][1] * inner for z in range(4)],
    ]
    bias_sums = [total([own(x) for x in field]) for field in fields]

    sub = iota((8, 256), 0)
    stacks = []
    for z in range(4):
        pieces = []
        for f in range(3):
            x = fields[f][z]
            edge = jnp.where(sub == 0, x[16:24], jnp.where(sub == 7, x[0:8], 0.0))
            block = jnp.concatenate([x[8:16], edge], axis=0)
            grad_ref[f, z] = block
            for d in range(3):
                moved = (shift_cols(block, d - 1) if d != 1 else block)[:, :128]
                upper = moved.astype(BF16)
                lower = (moved - upper.astype(F32)).astype(BF16)
                pieces += [upper, lower]
        stacks.append(jnp.concatenate(pieces, axis=0))
    offset = (iota((16, 256), 1) & 7) - edge_row(iota((16, 256), 0)) + 1
    rows = [[None] * 9 for _ in range(3)]
    picked = {}
    for a in range(3):
        moments = jnp.zeros((288, 256), F32)
        for z in range(4):
            if 0 <= z + a - 1 < 4:
                feats = f_ref[:, z + a - 1].reshape(256, 128)
                moments = moments + dot(stacks[z], feats, ((1,), (1,)))
        for f in range(3):
            for d in range(3):
                start = (f * 3 + d) * 32
                pair = moments[start : start + 16] + moments[start + 16 : start + 32]
                for b in range(3):
                    chosen = jnp.where(offset == b, pair, 0.0)
                    picked[b, f, a, d] = jnp.sum(chosen, axis=0, keepdims=True)
    result = jnp.zeros((32, 128), F32)
    for b in range(3):
        stacked = jnp.concatenate(
            [picked[b, f, a, d] for f in range(3) for a in range(3) for d in range(3)]
            + [jnp.zeros((5, 256), F32)],
            axis=0,
        )
        collect = jnp.where((iota((256, 128), 0) >> 3) + 32 * b == iota((256, 128), 1), 1.0, 0.0)
        result = result + dot(stacked, collect, ((1,), (0,)), precision=lax.Precision.HIGHEST)
    row32, lane32 = iota((32, 128), 0), iota((32, 128), 1)
    for k, value in enumerate([t0, t1, t2, t3] + bias_sums):
        result = jnp.where((row32 == 31) & (lane32 == k), value, result)
    for n in range(sums_ref.shape[0]):
        sums_ref[n] = result


def add_kernel(in_ref, out_ref):
    acc = in_ref[0]
    for n in range(1, in_ref.shape[0]):
        acc = acc + in_ref[n]
    for n in range(out_ref.shape[0]):
        out_ref[n] = acc


def final_kernel(in_ref, grad_ref, a_ref, loss_ref, weight_ref, bias_ref, out_ref, *, voxels):
    acc = in_ref[0]
    for n in range(1, in_ref.shape[0]):
        acc = acc + in_ref[n]
    sums = [acc[31:32, k : k + 1] for k in range(7)]
    precision = (sums[0] + 1.0) / (sums[1] + 1.0)
    sensitivity = (sums[2] + 1.0) / (sums[3] + 1.0)
    both = precision + sensitivity
    loss_ref[...] = 1.0 - 2.0 * precision * sensitivity / both
    by_precision = -2.0 * (sensitivity / both) * (sensitivity / both)
    by_sensitivity = -2.0 * (precision / both) * (precision / both)
    slopes = [
        by_precision / (sums[1] + 1.0),
        -by_precision * precision / (sums[1] + 1.0),
        by_sensitivity / (sums[3] + 1.0),
    ]
    bias_ref[...] = slopes[0] * sums[4] + slopes[1] * sums[5] + slopes[2] * sums[6]
    weight = slopes[0] * acc[0:9] + slopes[1] * acc[9:18] + slopes[2] * acc[18:27]
    for b in range(3):
        part = weight if b == 0 else pltpu.roll(weight, 128 - 32 * b, 1)
        for a in range(3):
            weight_ref[9 * a + 3 * b : 9 * a + 3 * b + 3] = part[3 * a : 3 * a + 3, :32]
    matrix = a_ref[...]
    parts = []
    for z in range(4):
        block = slopes[0] * grad_ref[0, z] + slopes[1] * grad_ref[1, z] + slopes[2] * grad_ref[2, z]
        block = block * voxels
        byd = []
        for d in range(3):
            moved = (shift_cols(block, d - 1) if d != 1 else block)[:, :128]
            upper = moved.astype(BF16)
            byd.append((upper, (moved - upper.astype(F32)).astype(BF16)))
        parts.append(byd)
    none = jnp.zeros((16, 128), BF16)
    for z in range(4):
        acc_z = None
        for level in range(2):
            stack = []
            for a in range(3):
                for d in range(3):
                    at = z - a + 1
                    stack.append(parts[at][d][level] if 0 <= at < 4 else none)
            term = dot(matrix, jnp.concatenate(stack, axis=0), ((0,), (0,)))
            acc_z = term if acc_z is None else acc_z + term
        out_ref[:, z] = acc_z.reshape(32, 8, 128).astype(BF16)


def call(kernel, out_shapes, *args, scratch=(), smem=()):
    spec = pl.BlockSpec(memory_space=pltpu.VMEM)
    in_specs = [pl.BlockSpec(memory_space=pltpu.SMEM) if n in smem else spec for n in range(len(args))]
    return pl.pallas_call(
        kernel,
        out_shape=[jax.ShapeDtypeStruct(shape, dtype) for shape, dtype in out_shapes],
        in_specs=in_specs,
        out_specs=[spec] * len(out_shapes),
        scratch_shapes=list(scratch),
        compiler_params=pltpu.CompilerParams(vmem_limit_bytes=VMEM_LIMIT),
    )(*args)


def passed(x, axis, steps):
    count = lax.axis_size(axis)
    pairs = [(n, n + steps) for n in range(count) if 0 <= n + steps < count]
    return lax.ppermute(x, axis, pairs)


def local(features, vessel_label, conv_weight, conv_bias):
    gx, gy = lax.axis_size("gx"), lax.axis_size("gy")
    voxels = float(4 * 8 * gx * 128 * gy)
    matrix, near, far = call(
        partial_logits_kernel,
        [((144, 256), BF16), ((112, 128), F32), ((80, 128), F32)],
        conv_weight, features, vessel_label,
    )
    m2, p2 = passed(far, "gx", 2), passed(far, "gx", -2)
    m1, p1 = passed(near, "gx", 1), passed(near, "gx", -1)
    main, labels, right, left = call(
        rows_kernel,
        [((5, 40, 128), F32), ((4, 24, 128), F32), ((64, 128), F32), ((64, 128), F32)],
        near, m1, p1, m2, p2,
    )
    from_left, from_right = passed(right, "gy", 1), passed(left, "gy", -1)
    field = pltpu.VMEM((ITERS + 1, 4, 24, 256), F32)
    grads, sums = call(
        skeleton_kernel,
        [((3, 4, 16, 256), F32), ((gy, 32, 128), F32)],
        conv_bias, features, main, labels, from_left, from_right,
        scratch=[field] * 5, smem=(0,),
    )
    sums = lax.all_to_all(sums, "gy", 0, 0, tiled=True)
    sums = call(add_kernel, [((gx, 32, 128), F32)], sums)[0]
    sums = lax.all_to_all(sums, "gx", 0, 0, tiled=True)

    def finish(*refs):
        final_kernel(*refs, voxels=voxels)

    loss, weight_grad, bias_grad, feature_grad = call(
        finish,
        [((1, 1), F32), ((27, 32), F32), ((1, 1), F32), ((32, 4, 8, 128), BF16)],
        sums, grads, matrix,
    )
    return (loss.reshape(()), weight_grad, bias_grad.reshape((1,)), feature_grad)


def solution(mesh):
    in_specs = (P(None, None, "gx", "gy"), P(None, "gx", "gy"), P(), P())
    out_specs = (P(), P(), P(), P(None, None, "gx", "gy"))
    return jax.shard_map(local, mesh=mesh, in_specs=in_specs, out_specs=out_specs, check_vma=False)
```

time: 266 us -> 77.4 us (0.29)
  the two profiles are of different devices: /device:TPU:1 before, /device:TPU:32 now
where the time goes in v1:
time: 77.4 us; the launch traced here: 76.9 us
  blocking collectives  43.9 us (57%)
  starting transfers between devices  16.7 us (22%)
  Pallas kernels  8.03 us (10%)
  waiting for transfers between devices  4.53 us (6%)
  local copies, waits for them, and re-layouts  2.36 us (3%)
  between operations  1.38 us (2%)
    all_to_all x1, blocking collectives, local(): sums = lax.all_to_all(sums, 'gx', 0, 0, tiled=True)  31.7 us
    ppermute x6, starting transfers between devices, passed(): return lax.ppermute(x, axis, pairs)  16.7 us
    all_to_all x1, blocking collectives, local(): sums = lax.all_to_all(sums, 'gy', 0, 0, tiled=True)  12.2 us
    pallas_call x5, Pallas kernels, call(): pl.pallas_call(kernel, out_shape=[jax.ShapeDtypeStruct(shape, dtype) for...  8.03 us
    ppermute x6, waiting for transfers between devices, passed(): return lax.ppermute(x, axis, pairs)  4.53 us
    unnamed x8, local copies, waits for them, and re-layouts  2.36 us
  transfers between devices with their start and end apart: 6, of which 3 were waited for; matrix products, arithmetic and copies ran while one was open for 0% of the time, Pallas kernels for 0%

profile of v1, /device:TPU:32, one launch (start us, length us, event | category | flops | bytes accessed | tf_op | source)
XLA Modules:
  0.0 76.9 jit_solution(9930976257414348980)
XLA Ops:
  0.6 0.0 copy-start
  0.6 0.9 %copy-done = bf16[32,4,8,128]{3,2,1,0:T(8,128)(2,1)S(1)} copy-done((bf16[32,4,8,128]{3,2,1,0:T(8,128)(2,1)S(1)}, bf16[32,4,8,128]{3,2,1,0:T(8,128)(2,1)}, u32[]{:S(2)}) %copy-start) | copy-done | bytes 262168
  1.6 0.0 copy-start.2
  1.6 0.7 copy-done.2
  2.3 0.0 copy-start.3
  2.3 0.7 copy-done.3
  3.0 0.0 copy-start.1
  3.0 0.6 shard_map.75
  3.6 3.8 %collective-permute-start.1 = (f32[112,128]{1,0:T(8,128)S(1)}, f32[112,128]{1,0:T(8,128)S(1)}, u32[]{:S(2)}, u32[]{:S(2)}) collective-permute-start(f32[112,128]{1,0:T(8,128)S(1)} %get-tuple-element.17.own_ref), channel_id=1, source_target_pairs={{8,0},{16,8},{24,16},{32,24},{40,32},{48,40},{56,48},{64,56},{72,6... | collective-permute-start | bytes 172040 | tf_op jit(solution)/shard_map/ppermute | solution.py:396
  7.4 2.1 %collective-permute-start = (f32[112,128]{1,0:T(8,128)S(1)}, f32[112,128]{1,0:T(8,128)S(1)}, u32[]{:S(2)}, u32[]{:S(2)}) collective-permute-start(f32[112,128]{1,0:T(8,128)S(1)} %get-tuple-element.17.own_ref), channel_id=1, source_target_pairs={{0,8},{8,16},{16,24},{24,32},{32,40},{40,48},{48,56},{56,64},{64,7... | collective-permute-start | bytes 172040 | tf_op jit(solution)/shard_map/ppermute | solution.py:396
  9.4 1.3 %collective-permute-start.3 = (f32[80,128]{1,0:T(8,128)S(1)}, f32[80,128]{1,0:T(8,128)S(1)}, u32[]{:S(2)}, u32[]{:S(2)}) collective-permute-start(f32[80,128]{1,0:T(8,128)S(1)} %get-tuple-element.18), channel_id=1, source_target_pairs={{16,0},{24,8},{32,16},{40,24},{48,32},{56,40},{64,48},{72,56},{80,... | collective-permute-start | bytes 122888 | tf_op jit(solution)/shard_map/ppermute | solution.py:396
  10.7 7.0 %collective-permute-start.2 = (f32[80,128]{1,0:T(8,128)S(1)}, f32[80,128]{1,0:T(8,128)S(1)}, u32[]{:S(2)}, u32[]{:S(2)}) collective-permute-start(f32[80,128]{1,0:T(8,128)S(1)} %get-tuple-element.18), channel_id=1, source_target_pairs={{0,16},{8,24},{16,32},{24,40},{32,48},{40,56},{48,64},{56,72},{64,... | collective-permute-start | bytes 122888 | tf_op jit(solution)/shard_map/ppermute | solution.py:396
  17.8 0.4 collective-permute-done.3.p2_ref
  18.2 1.3 %collective-permute-done.2.m2_ref = f32[80,128]{1,0:T(8,128)S(1)} collective-permute-done((f32[80,128]{1,0:T(8,128)S(1)}, f32[80,128]{1,0:T(8,128)S(1)}, u32[]{:S(2)}, u32[]{:S(2)}) %collective-permute-start.2) | collective-permute-done | bytes 40992 | tf_op jit(solution)/shard_map/ppermute | solution.py:396
  19.5 0.0 collective-permute-done.1.p1_ref
  19.5 0.0 collective-permute-done.m1_ref
  19.5 0.1 shard_map.76
  19.6 1.3 %collective-permute-start.4 = (f32[64,128]{1,0:T(8,128)S(1)}, f32[64,128]{1,0:T(8,128)S(1)}, u32[]{:S(2)}, u32[]{:S(2)}) collective-permute-start(f32[64,128]{1,0:T(8,128)S(1)} %get-tuple-element.21), channel_id=1, source_target_pairs={{0,1},{1,2},{2,3},{3,4},{4,5},{5,6},{6,7},{8,9},{9,10},{10,11},{11... | collective-permute-start | bytes 98312 | tf_op jit(solution)/shard_map/ppermute | solution.py:396
  20.9 1.3 %collective-permute-start.5 = (f32[64,128]{1,0:T(8,128)S(1)}, f32[64,128]{1,0:T(8,128)S(1)}, u32[]{:S(2)}, u32[]{:S(2)}) collective-permute-start(f32[64,128]{1,0:T(8,128)S(1)} %get-tuple-element.22), channel_id=1, source_target_pairs={{1,0},{2,1},{3,2},{4,3},{5,4},{6,5},{7,6},{9,8},{10,9},{11,10},{12... | collective-permute-start | bytes 98312 | tf_op jit(solution)/shard_map/ppermute | solution.py:396
  22.8 0.0 collective-permute-done.4.from_left_ref
  22.9 2.8 %collective-permute-done.5.from_right_ref = f32[64,128]{1,0:T(8,128)S(1)} collective-permute-done((f32[64,128]{1,0:T(8,128)S(1)}, f32[64,128]{1,0:T(8,128)S(1)}, u32[]{:S(2)}, u32[]{:S(2)}) %collective-permute-start.5) | collective-permute-done | bytes 32800 | tf_op jit(solution)/shard_map/ppermute | solution.py:396
  25.7 0.0 copy-done.1
  25.7 5.7 %shard_map.77 = (f32[3,4,16,256]{3,2,1,0:T(8,128)S(1)}, f32[8,32,128]{2,1,0:T(8,128)S(1)}) custom-call(f32[1]{0:T(128)S(6)} %copy.8.bias_ref, bf16[32,4,8,128]{3,2,1,0:T(8,128)(2,1)S(1)} %copy-done.1, f32[5,40,128]{2,1,0:T(8,128)S(1)} %get-tuple-element.19.main_ref, f32[4,24,128]{2,1,0:T(8,128)S(1)} %get-tuple-element.20.lab_ref, ...), custom_call_target="tpu_custom_call" | custom-call | tf_op jit(solution)/shard_map/pallas_call | solution.py:383
  31.4 12.2 %all_to_all.10.in_ref = f32[8,32,128]{2,1,0:T(8,128)S(1)} all-to-all(f32[8,32,128]{2,1,0:T(8,128)S(1)} %get-tuple-element.23), channel_id=1, replica_groups=mesh['gx'=32,'gy'=8] {'gy'}, dimensions={0} | all-to-all | bytes 262144 | tf_op jit(solution)/shard_map/all_to_all | solution.py:422
  43.6 0.1 shard_map.78
  43.6 31.7 %all_to_all.11.refs_0_ = f32[32,32,128]{2,1,0:T(8,128)S(1)} all-to-all(f32[32,32,128]{2,1,0:T(8,128)S(1)} %shard_map.78), channel_id=1, replica_groups=mesh['gx'=32,'gy'=8] {'gx'}, dimensions={0} | all-to-all | bytes 1048576 | tf_op jit(solution)/shard_map/all_to_all | solution.py:424
  75.3 1.6 %shard_map.79 = (f32[1,1]{1,0:T(1,128)}, f32[27,32]{1,0:T(8,128)}, f32[1,1]{1,0:T(1,128)}, bf16[32,4,8,128]{3,2,1,0:T(8,128)(2,1)}) custom-call(f32[32,32,128]{2,1,0:T(8,128)S(1)} %all_to_all.11.refs_0_, f32[3,4,16,256]{3,2,1,0:T(8,128)S(1)} %get-tuple-element.24.refs_1_, bf16[144,256]{1,0:T(8,128)(2,1)S(1)} %get-tuple-element.25.refs_2_), custom_call_target="tpu_custom_call" | custom-call | tf_op jit(solution)/shard_map/pallas_call | solution.py:383
Async XLA Ops:
  0.6 1.0 %copy-start = (bf16[32,4,8,128]{3,2,1,0:T(8,128)(2,1)S(1)}, bf16[32,4,8,128]{3,2,1,0:T(8,128)(2,1)}, u32[]{:S(2)}) copy-start(bf16[32,4,8,128]{3,2,1,0:T(8,128)(2,1)} %f_ref.3) | copy-start | bytes 786436
  1.6 0.7 copy-start.2
  2.3 0.7 copy-start.3
  3.0 22.7 %copy-start.1 = (bf16[32,4,8,128]{3,2,1,0:T(8,128)(2,1)S(1)}, bf16[32,4,8,128]{3,2,1,0:T(8,128)(2,1)}, u32[]{:S(2)}) copy-start(bf16[32,4,8,128]{3,2,1,0:T(8,128)(2,1)} %f_ref.3) | copy-start | bytes 786436
  3.6 15.9 %collective-permute-start.1 = (f32[112,128]{1,0:T(8,128)S(1)}, f32[112,128]{1,0:T(8,128)S(1)}, u32[]{:S(2)}, u32[]{:S(2)}) collective-permute-start(f32[112,128]{1,0:T(8,128)S(1)} %get-tuple-element.17.own_ref), channel_id=1, source_target_pairs={{8,0},{16,8},{24,16},{32,24},{40,32},{48,40},{56,48},{64,56},{72,6... | collective-permute-start | bytes 172040 | tf_op jit(solution)/shard_map/ppermute | solution.py:396
  7.4 12.1 %collective-permute-start = (f32[112,128]{1,0:T(8,128)S(1)}, f32[112,128]{1,0:T(8,128)S(1)}, u32[]{:S(2)}, u32[]{:S(2)}) collective-permute-start(f32[112,128]{1,0:T(8,128)S(1)} %get-tuple-element.17.own_ref), channel_id=1, source_target_pairs={{0,8},{8,16},{16,24},{24,32},{32,40},{40,48},{48,56},{56,64},{64,7... | collective-permute-start | bytes 172040 | tf_op jit(solution)/shard_map/ppermute | solution.py:396
  9.4 8.7 %collective-permute-start.3 = (f32[80,128]{1,0:T(8,128)S(1)}, f32[80,128]{1,0:T(8,128)S(1)}, u32[]{:S(2)}, u32[]{:S(2)}) collective-permute-start(f32[80,128]{1,0:T(8,128)S(1)} %get-tuple-element.18), channel_id=1, source_target_pairs={{16,0},{24,8},{32,16},{40,24},{48,32},{56,40},{64,48},{72,56},{80,... | collective-permute-start | bytes 122888 | tf_op jit(solution)/shard_map/ppermute | solution.py:396
  10.7 8.7 %collective-permute-start.2 = (f32[80,128]{1,0:T(8,128)S(1)}, f32[80,128]{1,0:T(8,128)S(1)}, u32[]{:S(2)}, u32[]{:S(2)}) collective-permute-start(f32[80,128]{1,0:T(8,128)S(1)} %get-tuple-element.18), channel_id=1, source_target_pairs={{0,16},{8,24},{16,32},{24,40},{32,48},{40,56},{48,64},{56,72},{64,... | collective-permute-start | bytes 122888 | tf_op jit(solution)/shard_map/ppermute | solution.py:396
  19.6 3.2 %collective-permute-start.4 = (f32[64,128]{1,0:T(8,128)S(1)}, f32[64,128]{1,0:T(8,128)S(1)}, u32[]{:S(2)}, u32[]{:S(2)}) collective-permute-start(f32[64,128]{1,0:T(8,128)S(1)} %get-tuple-element.21), channel_id=1, source_target_pairs={{0,1},{1,2},{2,3},{3,4},{4,5},{5,6},{6,7},{8,9},{9,10},{10,11},{11... | collective-permute-start | bytes 98312 | tf_op jit(solution)/shard_map/ppermute | solution.py:396
  20.9 4.8 %collective-permute-start.5 = (f32[64,128]{1,0:T(8,128)S(1)}, f32[64,128]{1,0:T(8,128)S(1)}, u32[]{:S(2)}, u32[]{:S(2)}) collective-permute-start(f32[64,128]{1,0:T(8,128)S(1)} %get-tuple-element.22), channel_id=1, source_target_pairs={{1,0},{2,1},{3,2},{4,3},{5,4},{6,5},{7,6},{9,8},{10,9},{11,10},{12... | collective-permute-start | bytes 98312 | tf_op jit(solution)/shard_map/ppermute | solution.py:396

commit v2 on v1

--- a/solution.py
+++ b/solution.py
@@ -41,9 +41,17 @@
     return matrix.astype(BF16)
 
 
-def partial_logits_kernel(w_ref, f_ref, lab_ref, a_ref, near_ref, far_ref):
+def partial_logits_kernel(
+    w_hbm, f_hbm, lab_hbm, a_ref, near_ref, far_ref, w_ref, f_ref, lab_ref, sems
+):
+    pairs = [(w_hbm, w_ref), (f_hbm, f_ref), (lab_hbm, lab_ref)]
+    copies = [pltpu.make_async_copy(x, y, sems.at[n]) for n, (x, y) in enumerate(pairs)]
+    for copy in copies:
+        copy.start()
+    copies[0].wait()
     matrix = weight_matrix(w_ref[...])
     a_ref[...] = matrix
+    copies[1].wait()
     lane = iota((16, 128), 1)
     terms = [
         dot(matrix, f_ref[:, z].reshape(256, 128), ((1,), (0,))).reshape(3, 3, 16, 128)
@@ -59,16 +67,26 @@
         main = main + jnp.where(lane <= 126, pltpu.roll(byd[2], 127, 1), 0.0)
         near_ref[16 * z : 16 * z + 16] = main
         far_ref[16 * z : 16 * z + 16] = main
-        shift = 32 * z + 17
-        corner = jnp.where(lane == shift - 1, pltpu.roll(byd[0], shift, 1), corner)
-        corner = jnp.where(lane == shift, pltpu.roll(byd[2], shift, 1), corner)
+        low, high = 16 * z, 16 * z + 15
+        corner = jnp.where(lane == low, pltpu.roll(byd[0], low + 1, 1), corner)
+        corner = jnp.where(lane == high, pltpu.roll(byd[2], high, 1), corner)
     near_ref[64:80] = corner
     far_ref[64:80] = corner
+    copies[2].wait()
     near_ref[80:112] = lab_ref[...].reshape(32, 128).astype(F32)
 
 
-def rows_kernel(own_ref, m1_ref, p1_ref, m2_ref, p2_ref, main_ref, lab_ref, right_ref, left_ref):
-    blocks = [m2_ref, m1_ref, own_ref, p1_ref, p2_ref]
+def rows_kernel(
+    own_ref, one_a_ref, one_b_ref, two_a_ref, two_b_ref, main_ref, lab_ref, send_a_ref, send_b_ref
+):
+    row_block, col_block = lax.axis_index("gx"), lax.axis_index("gy")
+    even1 = (row_block & 1) == 0
+    even2 = (row_block & 2) == 0
+    even_col = (col_block & 1) == 0
+    own = own_ref[...]
+    one_a, one_b, two_a, two_b = one_a_ref[...], one_b_ref[...], two_a_ref[...], two_b_ref[...]
+    before, after = jnp.where(even1, one_b, one_a), jnp.where(even1, one_a, one_b)
+    blocks = [jnp.where(even2, two_b, two_a), before, own, after, jnp.where(even2, two_a, two_b)]
     sub = iota((8, 128), 0)
 
     def assemble(start):
@@ -83,24 +101,24 @@
         return jnp.concatenate(tiles, axis=0)
 
     corner = assemble(64)
-    group = iota((64, 128), 1) >> 5
-    right = jnp.zeros((64, 128), F32)
-    left = jnp.zeros((64, 128), F32)
+    main_ref[4] = corner
+    lane = iota((40, 128), 1)
+    right = jnp.zeros((40, 128), F32)
+    left = jnp.zeros((40, 128), F32)
     for z in range(4):
         main = assemble(16 * z)
         main_ref[z] = main
-        lab = jnp.concatenate(
-            [ref[80 + 8 * z : 88 + 8 * z] for ref in (m1_ref, own_ref, p1_ref)], axis=0
-        )
+        lab = jnp.concatenate([x[80 + 8 * z : 88 + 8 * z] for x in (before, own, after)], axis=0)
         lab_ref[z] = lab
-        both = jnp.concatenate([main, lab], axis=0)
-        right = jnp.where(group == z, pltpu.roll(both, (32 * z + 16) % 128, 1), right)
-        left = jnp.where(group == z, pltpu.roll(both, 32 * z, 1), left)
-    main_ref[4] = corner
-    spread = jnp.concatenate([corner, jnp.zeros((24, 128), F32)], axis=0)
-    place = iota((64, 128), 1) & 31
-    right_ref[...] = jnp.where(place < 16, right, spread)
-    left_ref[...] = jnp.where(place < 16, left, spread)
+        lab = jnp.concatenate([lab, jnp.zeros((16, 128), F32)], axis=0)
+        right = jnp.where((lane >> 4) == z, pltpu.roll(main, 16 * z + 16, 1), right)
+        right = jnp.where((lane >> 4) == z + 4, pltpu.roll(lab, (16 * z + 80) % 128, 1), right)
+        left = jnp.where((lane >> 4) == z, pltpu.roll(main, 16 * z, 1), left)
+        left = jnp.where((lane >> 4) == z + 4, pltpu.roll(lab, 16 * z + 64, 1), left)
+    right = jnp.where((lane < 64) & ((lane & 15) == 0), corner, right)
+    left = jnp.where((lane < 64) & ((lane & 15) == 15), corner, left)
+    send_a_ref[...] = jnp.where(even_col, right, left)
+    send_b_ref[...] = jnp.where(even_col, left, right)
 
 
 def shift_rows(x, s):
@@ -169,9 +187,9 @@
 
 
 def skeleton_kernel(
-    bias_ref, f_ref, main_ref, lab_ref, from_left_ref, from_right_ref,
+    bias_ref, f_ref, main_ref, lab_ref, got_a_ref, got_b_ref,
     grad_ref, sums_ref,
-    qs_ref, ds_ref, rs_ref, gain_ref, direct_ref,
+    qs_ref, ds_ref, rs_ref, gain_ref,
 ):
     row_ids = lax.axis_index("gx") * 8 - 16 + iota((40, 256), 0)
     lane = iota((40, 256), 1)
@@ -184,25 +202,25 @@
     inner_b = inner > 0.5
     bias = bias_ref[0]
 
-    lane1 = iota((64, 128), 1)
-    from_left = from_left_ref[...]
-    from_right = from_right_ref[...]
+    even_col = (lax.axis_index("gy") & 1) == 0
+    from_left = jnp.where(even_col, got_b_ref[...], got_a_ref[...])
+    from_right = jnp.where(even_col, got_a_ref[...], got_b_ref[...])
     corner = main_ref[4]
-    lane40 = lane1[:40]
+    lane40 = iota((40, 128), 1)
+    lane24 = lane40[:24]
     e0, q0, slope, probs, labels = [], [], [], [], []
     for z in range(4):
-        start = 32 * z
-        extra_left = pltpu.roll(from_left, (112 - start) % 128, 1)
-        extra_right = pltpu.roll(from_right, (128 - start) % 128, 1)
-        extra = jnp.where(lane1 >= 112, extra_left, jnp.where(lane1 < 16, extra_right, 0.0))
-        at_zero = pltpu.roll(from_left[:40], (128 - start - 16) % 128, 1)
-        at_last = pltpu.roll(from_right[:40], (110 - start) % 128, 1)
+        to_zero, to_last = (128 - 16 * z) % 128, 112 - 16 * z
+        left_zero, left_last = pltpu.roll(from_left, to_zero, 1), pltpu.roll(from_left, to_last, 1)
+        right_zero, right_last = pltpu.roll(from_right, to_zero, 1), pltpu.roll(from_right, to_last, 1)
         main = main_ref[z]
-        main = main + jnp.where(lane40 == 0, at_zero, jnp.where(lane40 == 127, at_last, 0.0))
-        own_zero = pltpu.roll(corner, (128 - start - 16) % 128, 1)
-        own_last = pltpu.roll(corner, (110 - start) % 128, 1)
-        tail = extra[:40]
+        main = main + jnp.where(lane40 == 0, left_zero, jnp.where(lane40 == 127, right_last, 0.0))
+        tail = jnp.where(lane40 >= 112, left_last, jnp.where(lane40 < 16, right_zero, 0.0))
+        own_zero, own_last = pltpu.roll(corner, to_zero, 1), pltpu.roll(corner, to_last, 1)
         tail = tail + jnp.where(lane40 == 0, own_zero, jnp.where(lane40 == 127, own_last, 0.0))
+        lab_left = pltpu.roll(from_left[:24], 48 - 16 * z, 1)
+        lab_right = pltpu.roll(from_right[:24], 64 - 16 * z, 1)
+        lab_tail = jnp.where(lane24 >= 112, lab_left, jnp.where(lane24 < 16, lab_right, 0.0))
         logits = jnp.concatenate([main, tail], axis=1) + bias
         small = jnp.exp(-jnp.abs(logits))
         scale = inverse(1.0 + small)
@@ -214,7 +232,7 @@
         weight = (small * scale) * scale
         slope.append(((-SHARP) * e * weight)[8:32] * inner)
         probs.append((prob[8:32], weight[8:32]))
-        labels.append(jnp.concatenate([lab_ref[z], extra[40:]], axis=1))
+        labels.append(jnp.concatenate([lab_ref[z], lab_tail], axis=1))
 
     low, high = jnp.exp(-SHARP * jnp.ones((24, 256), F32)), jnp.exp(SHARP * jnp.ones((24, 256), F32))
     true_skel, _ = forward(
@@ -291,7 +309,6 @@
                 pieces += [upper, lower]
         stacks.append(jnp.concatenate(pieces, axis=0))
     offset = (iota((16, 256), 1) & 7) - edge_row(iota((16, 256), 0)) + 1
-    rows = [[None] * 9 for _ in range(3)]
     picked = {}
     for a in range(3):
         moments = jnp.zeros((288, 256), F32)
@@ -306,18 +323,18 @@
                 for b in range(3):
                     chosen = jnp.where(offset == b, pair, 0.0)
                     picked[b, f, a, d] = jnp.sum(chosen, axis=0, keepdims=True)
-    result = jnp.zeros((32, 128), F32)
-    for b in range(3):
-        stacked = jnp.concatenate(
-            [picked[b, f, a, d] for f in range(3) for a in range(3) for d in range(3)]
-            + [jnp.zeros((5, 256), F32)],
-            axis=0,
-        )
+    order = [(f, a, d) for f in range(3) for a in range(3) for d in range(3)]
+    groups = [[picked[(b,) + at] for at in order[:24]] for b in range(3)]
+    rest = [picked[(b,) + at] for b in range(3) for at in order[24:]]
+    groups.append(rest + [jnp.zeros((15, 256), F32)])
+    result = jnp.zeros((24, 128), F32)
+    for b in range(4):
+        stacked = jnp.concatenate(groups[b], axis=0)
         collect = jnp.where((iota((256, 128), 0) >> 3) + 32 * b == iota((256, 128), 1), 1.0, 0.0)
         result = result + dot(stacked, collect, ((1,), (0,)), precision=lax.Precision.HIGHEST)
-    row32, lane32 = iota((32, 128), 0), iota((32, 128), 1)
+    row24, lane_of = iota((24, 128), 0), iota((24, 128), 1)
     for k, value in enumerate([t0, t1, t2, t3] + bias_sums):
-        result = jnp.where((row32 == 31) & (lane32 == k), value, result)
+        result = jnp.where((row24 == 23) & (lane_of == 96 + k), value, result)
     for n in range(sums_ref.shape[0]):
         sums_ref[n] = result
 
@@ -334,7 +351,7 @@
     acc = in_ref[0]
     for n in range(1, in_ref.shape[0]):
         acc = acc + in_ref[n]
-    sums = [acc[31:32, k : k + 1] for k in range(7)]
+    sums = [acc[23:24, 96 + k : 97 + k] for k in range(7)]
     precision = (sums[0] + 1.0) / (sums[1] + 1.0)
     sensitivity = (sums[2] + 1.0) / (sums[3] + 1.0)
     both = precision + sensitivity
@@ -347,7 +364,12 @@
         by_sensitivity / (sums[3] + 1.0),
     ]
     bias_ref[...] = slopes[0] * sums[4] + slopes[1] * sums[5] + slopes[2] * sums[6]
-    weight = slopes[0] * acc[0:9] + slopes[1] * acc[9:18] + slopes[2] * acc[18:27]
+    group = iota((3, 128), 1) >> 5
+    last = acc[18:21]
+    for b in range(3):
+        last = jnp.where(group == b, pltpu.roll(acc[3 * b : 3 * b + 3], (32 * b + 32) % 128, 1), last)
+    third = jnp.concatenate([acc[18:24], last], axis=0)
+    weight = slopes[0] * acc[0:9] + slopes[1] * acc[9:18] + slopes[2] * third
     for b in range(3):
         part = weight if b == 0 else pltpu.roll(weight, 128 - 32 * b, 1)
         for a in range(3):
@@ -377,9 +399,9 @@
         out_ref[:, z] = acc_z.reshape(32, 8, 128).astype(BF16)
 
 
-def call(kernel, out_shapes, *args, scratch=(), smem=()):
+def call(kernel, out_shapes, *args, scratch=(), spaces={}):
     spec = pl.BlockSpec(memory_space=pltpu.VMEM)
-    in_specs = [pl.BlockSpec(memory_space=pltpu.SMEM) if n in smem else spec for n in range(len(args))]
+    in_specs = [pl.BlockSpec(memory_space=spaces.get(n, pltpu.VMEM)) for n in range(len(args))]
     return pl.pallas_call(
         kernel,
         out_shape=[jax.ShapeDtypeStruct(shape, dtype) for shape, dtype in out_shapes],
@@ -390,9 +412,12 @@
     )(*args)
 
 
-def passed(x, axis, steps):
+def swapped(x, axis, step, phase):
     count = lax.axis_size(axis)
-    pairs = [(n, n + steps) for n in range(count) if 0 <= n + steps < count]
+    pairs = []
+    for n in range(count - step):
+        if (n // step) % 2 == phase:
+            pairs += [(n, n + step), (n + step, n)]
     return lax.ppermute(x, axis, pairs)
 
 
@@ -402,25 +427,32 @@
     matrix, near, far = call(
         partial_logits_kernel,
         [((144, 256), BF16), ((112, 128), F32), ((80, 128), F32)],
-        conv_weight, features, vessel_label,
+        *[pltpu.with_memory_space_constraint(x, pltpu.HBM) for x in (conv_weight, features, vessel_label)],
+        scratch=[
+            pltpu.VMEM((27, 32), BF16),
+            pltpu.VMEM((32, 4, 8, 128), BF16),
+            pltpu.VMEM((4, 8, 128), jnp.int32),
+            pltpu.SemaphoreType.DMA((3,)),
+        ],
+        spaces={0: pltpu.HBM, 1: pltpu.HBM, 2: pltpu.HBM},
     )
-    m2, p2 = passed(far, "gx", 2), passed(far, "gx", -2)
-    m1, p1 = passed(near, "gx", 1), passed(near, "gx", -1)
-    main, labels, right, left = call(
+    two = [swapped(far, "gx", 2, phase) for phase in range(2)]
+    one = [swapped(near, "gx", 1, phase) for phase in range(2)]
+    main, labels, send_a, send_b = call(
         rows_kernel,
-        [((5, 40, 128), F32), ((4, 24, 128), F32), ((64, 128), F32), ((64, 128), F32)],
-        near, m1, p1, m2, p2,
+        [((5, 40, 128), F32), ((4, 24, 128), F32), ((40, 128), F32), ((40, 128), F32)],
+        near, *one, *two,
     )
-    from_left, from_right = passed(right, "gy", 1), passed(left, "gy", -1)
+    got = [swapped(send_a, "gy", 1, 0), swapped(send_b, "gy", 1, 1)]
     field = pltpu.VMEM((ITERS + 1, 4, 24, 256), F32)
     grads, sums = call(
         skeleton_kernel,
-        [((3, 4, 16, 256), F32), ((gy, 32, 128), F32)],
-        conv_bias, features, main, labels, from_left, from_right,
-        scratch=[field] * 5, smem=(0,),
+        [((3, 4, 16, 256), F32), ((gy, 24, 128), F32)],
+        conv_bias, features, main, labels, *got,
+        scratch=[field] * 4, spaces={0: pltpu.SMEM},
     )
     sums = lax.all_to_all(sums, "gy", 0, 0, tiled=True)
-    sums = call(add_kernel, [((gx, 32, 128), F32)], sums)[0]
+    sums = call(add_kernel, [((gx, 24, 128), F32)], sums)[0]
     sums = lax.all_to_all(sums, "gx", 0, 0, tiled=True)
 
     def finish(*refs):

time: 77.4 us -> 64.9 us (0.84)
  blocking collectives: 43.9 us -> 39.7 us
  starting transfers between devices: 16.7 us -> 12.7 us
  waiting for transfers between devices: 4.53 us -> 1.99 us
  local copies, waits for them, and re-layouts: 2.36 us -> 0.01 us
  Pallas kernels: 8.03 us -> 8.9 us
    all_to_all x1, blocking collectives: 31.7 us -> 26 us  [local(): sums = lax.all_to_all(sums, 'gx', 0, 0, tiled=True)]
    ppermute x6, starting transfers between devices: 16.7 us -> 12.7 us  [swapped(): return lax.ppermute(x, axis, pairs)]
    ppermute x6, waiting for transfers between devices: 4.53 us -> 1.99 us  [swapped(): return lax.ppermute(x, axis, pairs)]
    unnamed x8 -> x2, local copies, waits for them, and re-layouts: 2.36 us -> 0.01 us
    all_to_all x1, blocking collectives: 12.2 us -> 13.7 us  [local(): sums = lax.all_to_all(sums, 'gy', 0, 0, tiled=True)]
    pallas_call x5, Pallas kernels: 8.03 us -> 8.9 us  [call(): pl.pallas_call(kernel, out_shape=[jax.ShapeDtypeStruct(shape, dtype) for...]
  transfers between devices with their start and end apart: 6 -> 6, of which waited for: 3 -> 1; matrix products, arithmetic and copies ran while one was open for 0% -> 0% of each run, Pallas kernels for 0% -> 0%
where the time goes in v2:
time: 64.9 us; the launch traced here: 64.7 us
  blocking collectives  39.7 us (61%)
  starting transfers between devices  12.7 us (20%)
  Pallas kernels  8.9 us (14%)
  waiting for transfers between devices  1.99 us (3%)
  between operations  1.38 us (2%)
    all_to_all x1, blocking collectives, local(): sums = lax.all_to_all(sums, 'gx', 0, 0, tiled=True)  26 us
    all_to_all x1, blocking collectives, local(): sums = lax.all_to_all(sums, 'gy', 0, 0, tiled=True)  13.7 us
    ppermute x6, starting transfers between devices, swapped(): return lax.ppermute(x, axis, pairs)  12.7 us
    pallas_call x5, Pallas kernels, call(): pl.pallas_call(kernel, out_shape=[jax.ShapeDtypeStruct(shape, dtype) for...  8.9 us
    ppermute x6, waiting for transfers between devices, swapped(): return lax.ppermute(x, axis, pairs)  1.99 us
  transfers between devices with their start and end apart: 6, of which 1 were waited for; matrix products, arithmetic and copies ran while one was open for 0% of the time, Pallas kernels for 0%

profile of v2, /device:TPU:32, one launch (start us, length us, event | category | flops | bytes accessed | tf_op | source)
XLA Modules:
  0.0 64.7 jit_solution(15084179842664799880)
XLA Ops:
  0.6 0.0 copy-start
  0.6 1.4 %shard_map.75 = (bf16[144,256]{1,0:T(8,128)(2,1)S(1)}, f32[112,128]{1,0:T(8,128)S(1)}, f32[80,128]{1,0:T(8,128)S(1)}) custom-call(bf16[27,32]{1,0:T(8,128)(2,1)} %w_hbm.1, bf16[32,4,8,128]{3,2,1,0:T(8,128)(2,1)} %f_ref.1, s32[4,8,128]{2,1,0:T(8,128)} %lab_hbm.1), custom_call_target="tpu_custom_call" | custom-call | tf_op jit(solution)/shard_map/pallas_call | solution.py:405
  2.0 3.8 %collective-permute-start.1 = (f32[112,128]{1,0:T(8,128)S(1)}, f32[112,128]{1,0:T(8,128)S(1)}, u32[]{:S(2)}, u32[]{:S(2)}) collective-permute-start(f32[112,128]{1,0:T(8,128)S(1)} %get-tuple-element.17.own_ref), channel_id=1, source_target_pairs={{8,16},{16,8},{24,32},{32,24},{40,48},{48,40},{56,64},{64,56},{72,... | collective-permute-start | bytes 172040 | tf_op jit(solution)/shard_map/ppermute | solution.py:421
  5.9 0.1 collective-permute-start
  6.0 0.7 %collective-permute-start.3 = (f32[80,128]{1,0:T(8,128)S(1)}, f32[80,128]{1,0:T(8,128)S(1)}, u32[]{:S(2)}, u32[]{:S(2)}) collective-permute-start(f32[80,128]{1,0:T(8,128)S(1)} %get-tuple-element.18), channel_id=1, source_target_pairs={{16,32},{32,16},{24,40},{40,24},{48,64},{64,48},{56,72},{72,56},{8... | collective-permute-start | bytes 122888 | tf_op jit(solution)/shard_map/ppermute | solution.py:421
  6.6 7.4 %collective-permute-start.2 = (f32[80,128]{1,0:T(8,128)S(1)}, f32[80,128]{1,0:T(8,128)S(1)}, u32[]{:S(2)}, u32[]{:S(2)}) collective-permute-start(f32[80,128]{1,0:T(8,128)S(1)} %get-tuple-element.18), channel_id=1, source_target_pairs={{0,16},{16,0},{8,24},{24,8},{32,48},{48,32},{40,56},{56,40},{64,80... | collective-permute-start | bytes 122888 | tf_op jit(solution)/shard_map/ppermute | solution.py:421
  14.0 0.0 collective-permute-done.3.two_b_ref
  14.0 2.0 %collective-permute-done.2.two_a_ref = f32[80,128]{1,0:T(8,128)S(1)} collective-permute-done((f32[80,128]{1,0:T(8,128)S(1)}, f32[80,128]{1,0:T(8,128)S(1)}, u32[]{:S(2)}, u32[]{:S(2)}) %collective-permute-start.2) | collective-permute-done | bytes 40992 | tf_op jit(solution)/shard_map/ppermute | solution.py:421
  16.0 0.0 collective-permute-done.1.one_b_ref
  16.0 0.0 collective-permute-done.one_a_ref
  16.0 0.1 shard_map.76
  16.1 0.1 collective-permute-start.4
  16.2 0.7 %collective-permute-start.5 = (f32[40,128]{1,0:T(8,128)S(1)}, f32[40,128]{1,0:T(8,128)S(1)}, u32[]{:S(2)}, u32[]{:S(2)}) collective-permute-start(f32[40,128]{1,0:T(8,128)S(1)} %get-tuple-element.22), channel_id=1, source_target_pairs={{1,2},{2,1},{3,4},{4,3},{5,6},{6,5},{9,10},{10,9},{11,12},{12,11},... | collective-permute-start | bytes 61448 | tf_op jit(solution)/shard_map/ppermute | solution.py:421
  17.6 0.0 collective-permute-done.4.got_a_ref
  17.6 0.0 collective-permute-done.5.got_b_ref
  17.6 0.0 copy-done
  17.6 5.8 %shard_map.77 = (f32[3,4,16,256]{3,2,1,0:T(8,128)S(1)}, f32[8,24,128]{2,1,0:T(8,128)S(1)}) custom-call(f32[1]{0:T(128)S(6)} %copy.8.bias_ref, bf16[32,4,8,128]{3,2,1,0:T(8,128)(2,1)S(1)} %copy-done, f32[5,40,128]{2,1,0:T(8,128)S(1)} %get-tuple-element.19.main_ref, f32[4,24,128]{2,1,0:T(8,128)S(1)} %get-tuple-element.20.lab_ref, ...), custom_call_target="tpu_custom_call" | custom-call | tf_op jit(solution)/shard_map/pallas_call | solution.py:405
  23.4 13.7 %all_to_all.10.in_ref = f32[8,24,128]{2,1,0:T(8,128)S(1)} all-to-all(f32[8,24,128]{2,1,0:T(8,128)S(1)} %get-tuple-element.23), channel_id=1, replica_groups=mesh['gx'=32,'gy'=8] {'gy'}, dimensions={0} | all-to-all | bytes 196608 | tf_op jit(solution)/shard_map/all_to_all | solution.py:454
  37.1 26.0 %all_to_all.11.refs_0_ = f32[32,24,128]{2,1,0:T(8,128)S(1)} all-to-all(f32[32,24,128]{2,1,0:T(8,128)S(1)} %shard_map.78), channel_id=1, replica_groups=mesh['gx'=32,'gy'=8] {'gx'}, dimensions={0} | all-to-all | bytes 786432 | tf_op jit(solution)/shard_map/all_to_all | solution.py:456
  63.1 1.6 %shard_map.79 = (f32[1,1]{1,0:T(1,128)}, f32[27,32]{1,0:T(8,128)}, f32[1,1]{1,0:T(1,128)}, bf16[32,4,8,128]{3,2,1,0:T(8,128)(2,1)}) custom-call(f32[32,24,128]{2,1,0:T(8,128)S(1)} %all_to_all.11.refs_0_, f32[3,4,16,256]{3,2,1,0:T(8,128)S(1)} %get-tuple-element.24.refs_1_, bf16[144,256]{1,0:T(8,128)(2,1)S(1)} %get-tuple-element.25.refs_2_), custom_call_target="tpu_custom_call" | custom-call | tf_op jit(solution)/shard_map/pallas_call | solution.py:405
  (1 shorter events, 0.0 us)
Async XLA Ops:
  0.6 17.0 %copy-start = (bf16[32,4,8,128]{3,2,1,0:T(8,128)(2,1)S(1)}, bf16[32,4,8,128]{3,2,1,0:T(8,128)(2,1)}, u32[]{:S(2)}) copy-start(bf16[32,4,8,128]{3,2,1,0:T(8,128)(2,1)} %f_ref.1) | copy-start | bytes 786436
  2.0 13.9 %collective-permute-start.1 = (f32[112,128]{1,0:T(8,128)S(1)}, f32[112,128]{1,0:T(8,128)S(1)}, u32[]{:S(2)}, u32[]{:S(2)}) collective-permute-start(f32[112,128]{1,0:T(8,128)S(1)} %get-tuple-element.17.own_ref), channel_id=1, source_target_pairs={{8,16},{16,8},{24,32},{32,24},{40,48},{48,40},{56,64},{64,56},{72,... | collective-permute-start | bytes 172040 | tf_op jit(solution)/shard_map/ppermute | solution.py:421
  5.9 10.1 %collective-permute-start = (f32[112,128]{1,0:T(8,128)S(1)}, f32[112,128]{1,0:T(8,128)S(1)}, u32[]{:S(2)}, u32[]{:S(2)}) collective-permute-start(f32[112,128]{1,0:T(8,128)S(1)} %get-tuple-element.17.own_ref), channel_id=1, source_target_pairs={{0,8},{8,0},{16,24},{24,16},{32,40},{40,32},{48,56},{56,48},{64,72... | collective-permute-start | bytes 172040 | tf_op jit(solution)/shard_map/ppermute | solution.py:421
  6.0 8.0 %collective-permute-start.3 = (f32[80,128]{1,0:T(8,128)S(1)}, f32[80,128]{1,0:T(8,128)S(1)}, u32[]{:S(2)}, u32[]{:S(2)}) collective-permute-start(f32[80,128]{1,0:T(8,128)S(1)} %get-tuple-element.18), channel_id=1, source_target_pairs={{16,32},{32,16},{24,40},{40,24},{48,64},{64,48},{56,72},{72,56},{8... | collective-permute-start | bytes 122888 | tf_op jit(solution)/shard_map/ppermute | solution.py:421
  6.6 9.3 %collective-permute-start.2 = (f32[80,128]{1,0:T(8,128)S(1)}, f32[80,128]{1,0:T(8,128)S(1)}, u32[]{:S(2)}, u32[]{:S(2)}) collective-permute-start(f32[80,128]{1,0:T(8,128)S(1)} %get-tuple-element.18), channel_id=1, source_target_pairs={{0,16},{16,0},{8,24},{24,8},{32,48},{48,32},{40,56},{56,40},{64,80... | collective-permute-start | bytes 122888 | tf_op jit(solution)/shard_map/ppermute | solution.py:421
  16.1 1.4 %collective-permute-start.4 = (f32[40,128]{1,0:T(8,128)S(1)}, f32[40,128]{1,0:T(8,128)S(1)}, u32[]{:S(2)}, u32[]{:S(2)}) collective-permute-start(f32[40,128]{1,0:T(8,128)S(1)} %get-tuple-element.21), channel_id=1, source_target_pairs={{0,1},{1,0},{2,3},{3,2},{4,5},{5,4},{6,7},{7,6},{8,9},{9,8},{10,11... | collective-permute-start | bytes 61448 | tf_op jit(solution)/shard_map/ppermute | solution.py:421
  16.2 1.3 %collective-permute-start.5 = (f32[40,128]{1,0:T(8,128)S(1)}, f32[40,128]{1,0:T(8,128)S(1)}, u32[]{:S(2)}, u32[]{:S(2)}) collective-permute-start(f32[40,128]{1,0:T(8,128)S(1)} %get-tuple-element.22), channel_id=1, source_target_pairs={{1,2},{2,1},{3,4},{4,3},{5,6},{6,5},{9,10},{10,9},{11,12},{12,11},... | collective-permute-start | bytes 61448 | tf_op jit(solution)/shard_map/ppermute | solution.py:421

commit v3 on v2

--- a/solution.py
+++ b/solution.py
@@ -11,7 +11,7 @@
 SHARP = 10.0
 SOFT = 0.05
 EDGE = 16
-VMEM_LIMIT = 48 * 1024 * 1024
+VMEM_LIMIT = 24 * 1024 * 1024
 
 
 def iota(shape, dim):
@@ -41,8 +41,16 @@
     return matrix.astype(BF16)
 
 
+def turned(x, s):
+    return x if s == 0 else pltpu.roll(x, s % x.shape[0], 0)
+
+
+def at_end(lane):
+    return ((lane & 15) == 0) | ((lane & 15) == 15)
+
+
 def partial_logits_kernel(
-    w_hbm, f_hbm, lab_hbm, a_ref, near_ref, far_ref, w_ref, f_ref, lab_ref, sems
+    w_hbm, f_hbm, lab_hbm, a_ref, near_ref, far_ref, f_ref, w_ref, lab_ref, sems
 ):
     pairs = [(w_hbm, w_ref), (f_hbm, f_ref), (lab_hbm, lab_ref)]
     copies = [pltpu.make_async_copy(x, y, sems.at[n]) for n, (x, y) in enumerate(pairs)]
@@ -53,11 +61,13 @@
     a_ref[...] = matrix
     copies[1].wait()
     lane = iota((16, 128), 1)
+    sub = iota((8, 128), 0)
     terms = [
         dot(matrix, f_ref[:, z].reshape(256, 128), ((1,), (0,))).reshape(3, 3, 16, 128)
         for z in range(4)
     ]
     corner = jnp.zeros((16, 128), F32)
+    edges = jnp.zeros((8, 128), F32)
     for z in range(4):
         byd = []
         for d in range(3):
@@ -65,15 +75,20 @@
         main = byd[1]
         main = main + jnp.where(lane >= 1, pltpu.roll(byd[0], 1, 1), 0.0)
         main = main + jnp.where(lane <= 126, pltpu.roll(byd[2], 127, 1), 0.0)
-        near_ref[16 * z : 16 * z + 16] = main
-        far_ref[16 * z : 16 * z + 16] = main
+        near_ref[8 * z : 8 * z + 8] = main[:8]
+        far_ref[8 * z : 8 * z + 8] = main[:8]
+        edges = jnp.where(sub == z, turned(main[8:], z), edges)
+        edges = jnp.where(sub == 7 - z, turned(main[8:], -z), edges)
         low, high = 16 * z, 16 * z + 15
         corner = jnp.where(lane == low, pltpu.roll(byd[0], low + 1, 1), corner)
         corner = jnp.where(lane == high, pltpu.roll(byd[2], high, 1), corner)
-    near_ref[64:80] = corner
-    far_ref[64:80] = corner
+    corners = jnp.where(at_end(lane[:8]), corner[:8], pltpu.roll(corner[8:], 2, 1))
+    near_ref[32:40] = edges
+    far_ref[32:40] = edges
+    near_ref[40:48] = corners
+    far_ref[40:48] = corners
     copies[2].wait()
-    near_ref[80:112] = lab_ref[...].reshape(32, 128).astype(F32)
+    near_ref[48:80] = lab_ref[...].reshape(32, 128).astype(F32)
 
 
 def rows_kernel(
@@ -88,27 +103,34 @@
     before, after = jnp.where(even1, one_b, one_a), jnp.where(even1, one_a, one_b)
     blocks = [jnp.where(even2, two_b, two_a), before, own, after, jnp.where(even2, two_a, two_b)]
     sub = iota((8, 128), 0)
-
-    def assemble(start):
-        tiles = []
+    ends = at_end(iota((8, 128), 1))
+
+    def assemble(tiles, firsts, lasts):
+        result = []
         for t in range(5):
-            tile = blocks[t][start : start + 8]
+            tile = tiles[t]
             if t > 0:
-                tile = tile + jnp.where(sub == 0, blocks[t - 1][start + 8 : start + 16], 0.0)
+                tile = tile + jnp.where(sub == 0, firsts[t - 1], 0.0)
             if t < 4:
-                tile = tile + jnp.where(sub == 7, blocks[t + 1][start + 8 : start + 16], 0.0)
-            tiles.append(tile)
-        return jnp.concatenate(tiles, axis=0)
-
-    corner = assemble(64)
+                tile = tile + jnp.where(sub == 7, lasts[t + 1], 0.0)
+            result.append(tile)
+        return jnp.concatenate(result, axis=0)
+
+    corners = [jnp.where(ends, x[40:48], 0.0) for x in blocks]
+    beyond = [jnp.where(ends, pltpu.roll(x[40:48], 126, 1), 0.0) for x in blocks]
+    corner = assemble(corners, beyond, beyond)
     main_ref[4] = corner
     lane = iota((40, 128), 1)
     right = jnp.zeros((40, 128), F32)
     left = jnp.zeros((40, 128), F32)
     for z in range(4):
-        main = assemble(16 * z)
+        main = assemble(
+            [x[8 * z : 8 * z + 8] for x in blocks],
+            [turned(x[32:40], -z) for x in blocks],
+            [turned(x[32:40], z) for x in blocks],
+        )
         main_ref[z] = main
-        lab = jnp.concatenate([x[80 + 8 * z : 88 + 8 * z] for x in (before, own, after)], axis=0)
+        lab = jnp.concatenate([x[48 + 8 * z : 56 + 8 * z] for x in (before, own, after)], axis=0)
         lab_ref[z] = lab
         lab = jnp.concatenate([lab, jnp.zeros((16, 128), F32)], axis=0)
         right = jnp.where((lane >> 4) == z, pltpu.roll(main, 16 * z + 16, 1), right)
@@ -347,7 +369,7 @@
         out_ref[n] = acc
 
 
-def final_kernel(in_ref, grad_ref, a_ref, loss_ref, weight_ref, bias_ref, out_ref, *, voxels):
+def final_kernel(in_ref, part_ref, loss_ref, weight_ref, bias_ref, out_ref, *, voxels):
     acc = in_ref[0]
     for n in range(1, in_ref.shape[0]):
         acc = acc + in_ref[n]
@@ -374,32 +396,38 @@
         part = weight if b == 0 else pltpu.roll(weight, 128 - 32 * b, 1)
         for a in range(3):
             weight_ref[9 * a + 3 * b : 9 * a + 3 * b + 3] = part[3 * a : 3 * a + 3, :32]
+    for z in range(4):
+        value = slopes[0] * part_ref[0, z] + slopes[1] * part_ref[1, z] + slopes[2] * part_ref[2, z]
+        out_ref[:, z] = (value * voxels).reshape(32, 8, 128).astype(BF16)
+
+
+def feature_kernel(grad_ref, a_ref, part_ref):
     matrix = a_ref[...]
-    parts = []
-    for z in range(4):
-        block = slopes[0] * grad_ref[0, z] + slopes[1] * grad_ref[1, z] + slopes[2] * grad_ref[2, z]
-        block = block * voxels
-        byd = []
-        for d in range(3):
-            moved = (shift_cols(block, d - 1) if d != 1 else block)[:, :128]
-            upper = moved.astype(BF16)
-            byd.append((upper, (moved - upper.astype(F32)).astype(BF16)))
-        parts.append(byd)
     none = jnp.zeros((16, 128), BF16)
-    for z in range(4):
-        acc_z = None
-        for level in range(2):
-            stack = []
-            for a in range(3):
-                for d in range(3):
-                    at = z - a + 1
-                    stack.append(parts[at][d][level] if 0 <= at < 4 else none)
-            term = dot(matrix, jnp.concatenate(stack, axis=0), ((0,), (0,)))
-            acc_z = term if acc_z is None else acc_z + term
-        out_ref[:, z] = acc_z.reshape(32, 8, 128).astype(BF16)
-
-
-def call(kernel, out_shapes, *args, scratch=(), spaces={}):
+    for f in range(3):
+        parts = []
+        for z in range(4):
+            block = grad_ref[f, z]
+            byd = []
+            for d in range(3):
+                moved = (shift_cols(block, d - 1) if d != 1 else block)[:, :128]
+                upper = moved.astype(BF16)
+                byd.append((upper, (moved - upper.astype(F32)).astype(BF16)))
+            parts.append(byd)
+        for z in range(4):
+            acc = None
+            for level in range(2):
+                stack = []
+                for a in range(3):
+                    for d in range(3):
+                        at = z - a + 1
+                        stack.append(parts[at][d][level] if 0 <= at < 4 else none)
+                term = dot(matrix, jnp.concatenate(stack, axis=0), ((0,), (0,)))
+                acc = term if acc is None else acc + term
+            part_ref[f, z] = acc
+
+
+def call(kernel, out_shapes, *args, scratch=(), spaces={}, cost=None):
     spec = pl.BlockSpec(memory_space=pltpu.VMEM)
     in_specs = [pl.BlockSpec(memory_space=spaces.get(n, pltpu.VMEM)) for n in range(len(args))]
     return pl.pallas_call(
@@ -408,6 +436,7 @@
         in_specs=in_specs,
         out_specs=[spec] * len(out_shapes),
         scratch_shapes=list(scratch),
+        cost_estimate=cost and pl.CostEstimate(flops=1000 * cost, bytes_accessed=cost, transcendentals=0),
         compiler_params=pltpu.CompilerParams(vmem_limit_bytes=VMEM_LIMIT),
     )(*args)
 
@@ -424,13 +453,12 @@
 def local(features, vessel_label, conv_weight, conv_bias):
     gx, gy = lax.axis_size("gx"), lax.axis_size("gy")
     voxels = float(4 * 8 * gx * 128 * gy)
-    matrix, near, far = call(
+    matrix, near, far, features = call(
         partial_logits_kernel,
-        [((144, 256), BF16), ((112, 128), F32), ((80, 128), F32)],
+        [((144, 256), BF16), ((80, 128), F32), ((48, 128), F32), (features.shape, BF16)],
         *[pltpu.with_memory_space_constraint(x, pltpu.HBM) for x in (conv_weight, features, vessel_label)],
         scratch=[
             pltpu.VMEM((27, 32), BF16),
-            pltpu.VMEM((32, 4, 8, 128), BF16),
             pltpu.VMEM((4, 8, 128), jnp.int32),
             pltpu.SemaphoreType.DMA((3,)),
         ],
@@ -451,6 +479,7 @@
         conv_bias, features, main, labels, *got,
         scratch=[field] * 4, spaces={0: pltpu.SMEM},
     )
+    parts = call(feature_kernel, [((3, 4, 256, 128), F32)], grads, matrix, cost=2000000)[0]
     sums = lax.all_to_all(sums, "gy", 0, 0, tiled=True)
     sums = call(add_kernel, [((gx, 24, 128), F32)], sums)[0]
     sums = lax.all_to_all(sums, "gx", 0, 0, tiled=True)
@@ -461,7 +490,7 @@
     loss, weight_grad, bias_grad, feature_grad = call(
         finish,
         [((1, 1), F32), ((27, 32), F32), ((1, 1), F32), ((32, 4, 8, 128), BF16)],
-        sums, grads, matrix,
+        sums, parts,
     )
     return (loss.reshape(()), weight_grad, bias_grad.reshape((1,)), feature_grad)
 

time: 64.9 us -> 65.3 us (level)
  blocking collectives: 39.7 us -> 13.8 us
  waiting for transfers between devices: 1.99 us -> 15.6 us
  starting transfers between devices: 12.7 us -> 23.9 us
  Pallas kernels: 8.9 us -> 10.4 us
    all_to_all x1 -> x0, blocking collectives: 26 us -> none  [local(): sums = lax.all_to_all(sums, 'gx', 0, 0, tiled=True)]
    all_to_all x0 -> x1, waiting for transfers between devices: none -> 13.8 us  [local(): sums = lax.all_to_all(sums, 'gx', 0, 0, tiled=True)]
    all_to_all x0 -> x1, starting transfers between devices: none -> 11.2 us  [local(): sums = lax.all_to_all(sums, 'gx', 0, 0, tiled=True)]
    pallas_call x5 -> x6, Pallas kernels: 8.9 us -> 10.4 us  [call(): pl.pallas_call(kernel, out_shape=[jax.ShapeDtypeStruct(shape, dtype) for...]
  transfers between devices with their start and end apart: 6 -> 7, of which waited for: 1 -> 2; matrix products, arithmetic and copies ran while one was open for 0% -> 0% of each run, Pallas kernels for 0% -> 2%
where the time goes in v3:
time: 65.3 us; the launch traced here: 64.9 us
  starting transfers between devices  23.9 us (37%)
  waiting for transfers between devices  15.6 us (24%)
  blocking collectives  13.8 us (21%)
  Pallas kernels  10.4 us (16%)
  between operations  1.38 us (2%)
    all_to_all x1, blocking collectives, local(): sums = lax.all_to_all(sums, 'gy', 0, 0, tiled=True)  13.8 us
    all_to_all x1, waiting for transfers between devices, local(): sums = lax.all_to_all(sums, 'gx', 0, 0, tiled=True)  13.8 us
    ppermute x6, starting transfers between devices, swapped(): return lax.ppermute(x, axis, pairs)  12.7 us
    all_to_all x1, starting transfers between devices, local(): sums = lax.all_to_all(sums, 'gx', 0, 0, tiled=True)  11.2 us
    pallas_call x6, Pallas kernels, call(): pl.pallas_call(kernel, out_shape=[jax.ShapeDtypeStruct(shape, dtype) for...  10.4 us
    ppermute x6, waiting for transfers between devices, swapped(): return lax.ppermute(x, axis, pairs)  1.82 us
  transfers between devices with their start and end apart: 7, of which 2 were waited for; matrix products, arithmetic and copies ran while one was open for 0% of the time, Pallas kernels for 2%

profile of v3, /device:TPU:32, one launch (start us, length us, event | category | flops | bytes accessed | tf_op | source)
XLA Modules:
  0.0 64.9 jit_solution(12604570008117112566)
XLA Ops:
  0.6 1.4 %shard_map.75 = (bf16[144,256]{1,0:T(8,128)(2,1)S(1)}, f32[80,128]{1,0:T(8,128)S(1)}, f32[48,128]{1,0:T(8,128)S(1)}, bf16[32,4,8,128]{3,2,1,0:T(8,128)(2,1)S(1)}) custom-call(bf16[27,32]{1,0:T(8,128)(2,1)} %w_hbm.1, bf16[32,4,8,128]{3,2,1,0:T(8,128)(2,1)} %f_hbm.1, s32[4,8,128]{2,1,0:T(8,128)} %lab_hbm.1), custom_call_target="tpu_custom_call" | custom-call | tf_op jit(solution)/shard_map/pallas_call | solution.py:433
  2.1 3.8 %collective-permute-start.1 = (f32[80,128]{1,0:T(8,128)S(1)}, f32[80,128]{1,0:T(8,128)S(1)}, u32[]{:S(2)}, u32[]{:S(2)}) collective-permute-start(f32[80,128]{1,0:T(8,128)S(1)} %get-tuple-element.19.own_ref), channel_id=1, source_target_pairs={{8,16},{16,8},{24,32},{32,24},{40,48},{48,40},{56,64},{64,56},{72,... | collective-permute-start | bytes 122888 | tf_op jit(solution)/shard_map/ppermute | solution.py:450
  5.9 0.1 collective-permute-start
  6.0 0.7 %collective-permute-start.3 = (f32[48,128]{1,0:T(8,128)S(1)}, f32[48,128]{1,0:T(8,128)S(1)}, u32[]{:S(2)}, u32[]{:S(2)}) collective-permute-start(f32[48,128]{1,0:T(8,128)S(1)} %get-tuple-element.20), channel_id=1, source_target_pairs={{16,32},{32,16},{24,40},{40,24},{48,64},{64,48},{56,72},{72,56},{8... | collective-permute-start | bytes 73736 | tf_op jit(solution)/shard_map/ppermute | solution.py:450
  6.7 7.4 %collective-permute-start.2 = (f32[48,128]{1,0:T(8,128)S(1)}, f32[48,128]{1,0:T(8,128)S(1)}, u32[]{:S(2)}, u32[]{:S(2)}) collective-permute-start(f32[48,128]{1,0:T(8,128)S(1)} %get-tuple-element.20), channel_id=1, source_target_pairs={{0,16},{16,0},{8,24},{24,8},{32,48},{48,32},{40,56},{56,40},{64,80... | collective-permute-start | bytes 73736 | tf_op jit(solution)/shard_map/ppermute | solution.py:450
  14.0 0.0 collective-permute-done.3.two_b_ref
  14.0 1.8 %collective-permute-done.2.two_a_ref = f32[48,128]{1,0:T(8,128)S(1)} collective-permute-done((f32[48,128]{1,0:T(8,128)S(1)}, f32[48,128]{1,0:T(8,128)S(1)}, u32[]{:S(2)}, u32[]{:S(2)}) %collective-permute-start.2) | collective-permute-done | bytes 24608 | tf_op jit(solution)/shard_map/ppermute | solution.py:450
  15.8 0.0 collective-permute-done.1.one_b_ref
  15.8 0.0 collective-permute-done.one_a_ref
  15.8 0.2 shard_map.76
  16.0 0.1 collective-permute-start.4
  16.1 0.7 %collective-permute-start.5 = (f32[40,128]{1,0:T(8,128)S(1)}, f32[40,128]{1,0:T(8,128)S(1)}, u32[]{:S(2)}, u32[]{:S(2)}) collective-permute-start(f32[40,128]{1,0:T(8,128)S(1)} %get-tuple-element.24), channel_id=1, source_target_pairs={{1,2},{2,1},{3,4},{4,3},{5,6},{6,5},{9,10},{10,9},{11,12},{12,11},... | collective-permute-start | bytes 61448 | tf_op jit(solution)/shard_map/ppermute | solution.py:450
  17.4 0.0 collective-permute-done.4.got_a_ref
  17.4 0.0 collective-permute-done.5.got_b_ref
  17.4 5.8 %shard_map.77 = (f32[3,4,16,256]{3,2,1,0:T(8,128)S(1)}, f32[8,24,128]{2,1,0:T(8,128)S(1)}) custom-call(f32[1]{0:T(128)S(6)} %copy.8.bias_ref, bf16[32,4,8,128]{3,2,1,0:T(8,128)(2,1)S(1)} %get-tuple-element.18.f_ref, f32[5,40,128]{2,1,0:T(8,128)S(1)} %get-tuple-element.21.main_ref, f32[4,24,128]{2,1,0:T(8,128)S(1)} %get-tuple-element.22.lab_ref, ...), custom_call_target="tpu_custom_call" | custom-call | tf_op jit(solution)/shard_map/pallas_call | solution.py:433
  23.2 13.8 %all_to_all.10.in_ref = f32[8,24,128]{2,1,0:T(8,128)S(1)} all-to-all(f32[8,24,128]{2,1,0:T(8,128)S(1)} %get-tuple-element.25), channel_id=1, replica_groups=mesh['gx'=32,'gy'=8] {'gy'}, dimensions={0} | all-to-all | bytes 196608 | tf_op jit(solution)/shard_map/all_to_all | solution.py:483
  36.9 0.8 %shard_map.78 = f32[32,24,128]{2,1,0:T(8,128)} custom-call(f32[8,24,128]{2,1,0:T(8,128)S(1)} %all_to_all.10.in_ref), custom_call_target="tpu_custom_call" | custom-call | tf_op jit(solution)/shard_map/pallas_call | solution.py:433
  37.7 11.2 %all-to-all-start.1 = ((f32[32,24,128]{2,1,0:T(8,128)}), f32[32,24,128]{2,1,0:T(8,128)S(1)}, u32[]{:S(2)}, u32[]{:S(2)}) async-start(f32[32,24,128]{2,1,0:T(8,128)} %shard_map.78), calls=%async_computation.1 | async-start | bytes 786432 | tf_op jit(solution)/shard_map/all_to_all | solution.py:485
  48.9 1.0 %shard_map.79.refs_1_ = f32[3,4,256,128]{3,2,1,0:T(8,128)S(1)} custom-call(f32[3,4,16,256]{3,2,1,0:T(8,128)S(1)} %get-tuple-element.26.grad_ref, bf16[144,256]{1,0:T(8,128)(2,1)S(1)} %get-tuple-element.27.a_ref), custom_call_target="tpu_custom_call" | custom-call | flops 2000000000 | bytes 2000000 | tf_op jit(solution)/shard_map/pallas_call | solution.py:433
  50.0 13.8 %all-to-all-done.1.refs_0_ = f32[32,24,128]{2,1,0:T(8,128)S(1)} async-done(((f32[32,24,128]{2,1,0:T(8,128)}), f32[32,24,128]{2,1,0:T(8,128)S(1)}, u32[]{:S(2)}, u32[]{:S(2)}) %all-to-all-start.1) | async-done | bytes 393248 | tf_op jit(solution)/shard_map/all_to_all | solution.py:485
  63.7 1.2 %shard_map.80 = (f32[1,1]{1,0:T(1,128)}, f32[27,32]{1,0:T(8,128)}, f32[1,1]{1,0:T(1,128)}, bf16[32,4,8,128]{3,2,1,0:T(8,128)(2,1)}) custom-call(f32[32,24,128]{2,1,0:T(8,128)S(1)} %all-to-all-done.1.refs_0_, f32[3,4,256,128]{3,2,1,0:T(8,128)S(1)} %shard_map.79.refs_1_), custom_call_target="tpu_custom_call" | custom-call | tf_op jit(solution)/shard_map/pallas_call | solution.py:433
Async XLA Ops:
  2.1 13.8 %collective-permute-start.1 = (f32[80,128]{1,0:T(8,128)S(1)}, f32[80,128]{1,0:T(8,128)S(1)}, u32[]{:S(2)}, u32[]{:S(2)}) collective-permute-start(f32[80,128]{1,0:T(8,128)S(1)} %get-tuple-element.19.own_ref), channel_id=1, source_target_pairs={{8,16},{16,8},{24,32},{32,24},{40,48},{48,40},{56,64},{64,56},{72,... | collective-permute-start | bytes 122888 | tf_op jit(solution)/shard_map/ppermute | solution.py:450
  5.9 9.9 %collective-permute-start = (f32[80,128]{1,0:T(8,128)S(1)}, f32[80,128]{1,0:T(8,128)S(1)}, u32[]{:S(2)}, u32[]{:S(2)}) collective-permute-start(f32[80,128]{1,0:T(8,128)S(1)} %get-tuple-element.19.own_ref), channel_id=1, source_target_pairs={{0,8},{8,0},{16,24},{24,16},{32,40},{40,32},{48,56},{56,48},{64,72... | collective-permute-start | bytes 122888 | tf_op jit(solution)/shard_map/ppermute | solution.py:450
  6.0 8.0 %collective-permute-start.3 = (f32[48,128]{1,0:T(8,128)S(1)}, f32[48,128]{1,0:T(8,128)S(1)}, u32[]{:S(2)}, u32[]{:S(2)}) collective-permute-start(f32[48,128]{1,0:T(8,128)S(1)} %get-tuple-element.20), channel_id=1, source_target_pairs={{16,32},{32,16},{24,40},{40,24},{48,64},{64,48},{56,72},{72,56},{8... | collective-permute-start | bytes 73736 | tf_op jit(solution)/shard_map/ppermute | solution.py:450
  6.7 9.2 %collective-permute-start.2 = (f32[48,128]{1,0:T(8,128)S(1)}, f32[48,128]{1,0:T(8,128)S(1)}, u32[]{:S(2)}, u32[]{:S(2)}) collective-permute-start(f32[48,128]{1,0:T(8,128)S(1)} %get-tuple-element.20), channel_id=1, source_target_pairs={{0,16},{16,0},{8,24},{24,8},{32,48},{48,32},{40,56},{56,40},{64,80... | collective-permute-start | bytes 73736 | tf_op jit(solution)/shard_map/ppermute | solution.py:450
  16.0 1.4 %collective-permute-start.4 = (f32[40,128]{1,0:T(8,128)S(1)}, f32[40,128]{1,0:T(8,128)S(1)}, u32[]{:S(2)}, u32[]{:S(2)}) collective-permute-start(f32[40,128]{1,0:T(8,128)S(1)} %get-tuple-element.23), channel_id=1, source_target_pairs={{0,1},{1,0},{2,3},{3,2},{4,5},{5,4},{6,7},{7,6},{8,9},{9,8},{10,11... | collective-permute-start | bytes 61448 | tf_op jit(solution)/shard_map/ppermute | solution.py:450
  16.1 1.3 %collective-permute-start.5 = (f32[40,128]{1,0:T(8,128)S(1)}, f32[40,128]{1,0:T(8,128)S(1)}, u32[]{:S(2)}, u32[]{:S(2)}) collective-permute-start(f32[40,128]{1,0:T(8,128)S(1)} %get-tuple-element.24), channel_id=1, source_target_pairs={{1,2},{2,1},{3,4},{4,3},{5,6},{6,5},{9,10},{10,9},{11,12},{12,11},... | collective-permute-start | bytes 61448 | tf_op jit(solution)/shard_map/ppermute | solution.py:450
  37.7 26.0 %all-to-all-start.1 = ((f32[32,24,128]{2,1,0:T(8,128)}), f32[32,24,128]{2,1,0:T(8,128)S(1)}, u32[]{:S(2)}, u32[]{:S(2)}) async-start(f32[32,24,128]{2,1,0:T(8,128)} %shard_map.78), calls=%async_computation.1 | async-start | bytes 786432 | tf_op jit(solution)/shard_map/all_to_all | solution.py:485

commit v4 on v3

--- a/solution.py
+++ b/solution.py
@@ -356,28 +356,34 @@
         result = result + dot(stacked, collect, ((1,), (0,)), precision=lax.Precision.HIGHEST)
     row24, lane_of = iota((24, 128), 0), iota((24, 128), 1)
     for k, value in enumerate([t0, t1, t2, t3] + bias_sums):
-        result = jnp.where((row24 == 23) & (lane_of == 96 + k), value, result)
+        result = jnp.where(((row24 == 11) | (row24 == 23)) & (lane_of == 96 + k), value, result)
     for n in range(sums_ref.shape[0]):
         sums_ref[n] = result
 
 
-def add_kernel(in_ref, out_ref):
+def half_kernel(in_ref, out_ref):
     acc = in_ref[0]
     for n in range(1, in_ref.shape[0]):
         acc = acc + in_ref[n]
+    half = jnp.where((lax.axis_index("gy") & 1) == 0, acc[:12], acc[12:])
     for n in range(out_ref.shape[0]):
-        out_ref[n] = acc
-
-
-def final_kernel(in_ref, part_ref, loss_ref, weight_ref, bias_ref, out_ref, *, voxels):
-    acc = in_ref[0]
-    for n in range(1, in_ref.shape[0]):
-        acc = acc + in_ref[n]
-    sums = [acc[23:24, 96 + k : 97 + k] for k in range(7)]
+        out_ref[n] = half[4 * (n % 3) : 4 * (n % 3) + 4]
+
+
+def add_kernel(in_ref, out_ref):
+    for part in range(3):
+        acc = in_ref[part]
+        for n in range(part + 3, in_ref.shape[0], 3):
+            acc = acc + in_ref[n]
+        out_ref[part] = acc
+
+
+def loss_and_slopes(row):
+    sums = [row[:, 96 + k : 97 + k] for k in range(7)]
     precision = (sums[0] + 1.0) / (sums[1] + 1.0)
     sensitivity = (sums[2] + 1.0) / (sums[3] + 1.0)
     both = precision + sensitivity
-    loss_ref[...] = 1.0 - 2.0 * precision * sensitivity / both
+    loss = 1.0 - 2.0 * precision * sensitivity / both
     by_precision = -2.0 * (sensitivity / both) * (sensitivity / both)
     by_sensitivity = -2.0 * (precision / both) * (precision / both)
     slopes = [
@@ -385,7 +391,17 @@
         -by_precision * precision / (sums[1] + 1.0),
         by_sensitivity / (sums[3] + 1.0),
     ]
-    bias_ref[...] = slopes[0] * sums[4] + slopes[1] * sums[5] + slopes[2] * sums[6]
+    return loss, slopes, sums[4:]
+
+
+def weight_kernel(own_ref, got_ref, loss_ref, weight_ref, bias_ref):
+    even = (lax.axis_index("gy") & 1) == 0
+    own, got = own_ref[...], got_ref[...]
+    first, second = jnp.where(even, own, got), jnp.where(even, got, own)
+    acc = jnp.concatenate([x[part] for x in (first, second) for part in range(3)], axis=0)
+    loss, slopes, bias_sums = loss_and_slopes(acc[11:12])
+    loss_ref[...] = loss
+    bias_ref[...] = sum(slopes[f] * bias_sums[f] for f in range(3))
     group = iota((3, 128), 1) >> 5
     last = acc[18:21]
     for b in range(3):
@@ -396,38 +412,36 @@
         part = weight if b == 0 else pltpu.roll(weight, 128 - 32 * b, 1)
         for a in range(3):
             weight_ref[9 * a + 3 * b : 9 * a + 3 * b + 3] = part[3 * a : 3 * a + 3, :32]
-    for z in range(4):
-        value = slopes[0] * part_ref[0, z] + slopes[1] * part_ref[1, z] + slopes[2] * part_ref[2, z]
-        out_ref[:, z] = (value * voxels).reshape(32, 8, 128).astype(BF16)
-
-
-def feature_kernel(grad_ref, a_ref, part_ref):
+
+
+def feature_kernel(sums_ref, grad_ref, a_ref, out_ref, *, voxels):
+    _, slopes, _ = loss_and_slopes(sums_ref[2, 3:4])
     matrix = a_ref[...]
+    parts = []
+    for z in range(4):
+        block = slopes[0] * grad_ref[0, z] + slopes[1] * grad_ref[1, z] + slopes[2] * grad_ref[2, z]
+        block = block * voxels
+        byd = []
+        for d in range(3):
+            moved = (shift_cols(block, d - 1) if d != 1 else block)[:, :128]
+            upper = moved.astype(BF16)
+            byd.append((upper, (moved - upper.astype(F32)).astype(BF16)))
+        parts.append(byd)
     none = jnp.zeros((16, 128), BF16)
-    for f in range(3):
-        parts = []
-        for z in range(4):
-            block = grad_ref[f, z]
-            byd = []
-            for d in range(3):
-                moved = (shift_cols(block, d - 1) if d != 1 else block)[:, :128]
-                upper = moved.astype(BF16)
-                byd.append((upper, (moved - upper.astype(F32)).astype(BF16)))
-            parts.append(byd)
-        for z in range(4):
-            acc = None
-            for level in range(2):
-                stack = []
-                for a in range(3):
-                    for d in range(3):
-                        at = z - a + 1
-                        stack.append(parts[at][d][level] if 0 <= at < 4 else none)
-                term = dot(matrix, jnp.concatenate(stack, axis=0), ((0,), (0,)))
-                acc = term if acc is None else acc + term
-            part_ref[f, z] = acc
-
-
-def call(kernel, out_shapes, *args, scratch=(), spaces={}, cost=None):
+    for z in range(4):
+        acc_z = None
+        for level in range(2):
+            stack = []
+            for a in range(3):
+                for d in range(3):
+                    at = z - a + 1
+                    stack.append(parts[at][d][level] if 0 <= at < 4 else none)
+            term = dot(matrix, jnp.concatenate(stack, axis=0), ((0,), (0,)))
+            acc_z = term if acc_z is None else acc_z + term
+        out_ref[:, z] = acc_z.reshape(32, 8, 128).astype(BF16)
+
+
+def call(kernel, out_shapes, *args, scratch=(), spaces={}):
     spec = pl.BlockSpec(memory_space=pltpu.VMEM)
     in_specs = [pl.BlockSpec(memory_space=spaces.get(n, pltpu.VMEM)) for n in range(len(args))]
     return pl.pallas_call(
@@ -436,7 +450,6 @@
         in_specs=in_specs,
         out_specs=[spec] * len(out_shapes),
         scratch_shapes=list(scratch),
-        cost_estimate=cost and pl.CostEstimate(flops=1000 * cost, bytes_accessed=cost, transcendentals=0),
         compiler_params=pltpu.CompilerParams(vmem_limit_bytes=VMEM_LIMIT),
     )(*args)
 
@@ -479,18 +492,18 @@
         conv_bias, features, main, labels, *got,
         scratch=[field] * 4, spaces={0: pltpu.SMEM},
     )
-    parts = call(feature_kernel, [((3, 4, 256, 128), F32)], grads, matrix, cost=2000000)[0]
     sums = lax.all_to_all(sums, "gy", 0, 0, tiled=True)
-    sums = call(add_kernel, [((gx, 24, 128), F32)], sums)[0]
+    sums = call(half_kernel, [((3 * gx, 4, 128), F32)], sums)[0]
     sums = lax.all_to_all(sums, "gx", 0, 0, tiled=True)
-
-    def finish(*refs):
-        final_kernel(*refs, voxels=voxels)
-
-    loss, weight_grad, bias_grad, feature_grad = call(
-        finish,
-        [((1, 1), F32), ((27, 32), F32), ((1, 1), F32), ((32, 4, 8, 128), BF16)],
-        sums, parts,
+    sums = call(add_kernel, [((3, 4, 128), F32)], sums)[0]
+    other = swapped(sums, "gy", 1, 0)
+
+    def feature_part(*refs):
+        feature_kernel(*refs, voxels=voxels)
+
+    feature_grad = call(feature_part, [((32, 4, 8, 128), BF16)], sums, grads, matrix)[0]
+    loss, weight_grad, bias_grad = call(
+        weight_kernel, [((1, 1), F32), ((27, 32), F32), ((1, 1), F32)], sums, other
     )
     return (loss.reshape(()), weight_grad, bias_grad.reshape((1,)), feature_grad)
 

time: 65.3 us -> 63.7 us (0.975)
  the two profiles are of different devices: /device:TPU:32 before, /device:TPU:1 now
where the time goes in v4:
time: 63.7 us; the launch traced here: 63.4 us
  blocking collectives  27.7 us (43%)
  starting transfers between devices  21.8 us (34%)
  Pallas kernels  9.93 us (16%)
  waiting for transfers between devices  2.64 us (4%)
  between operations  1.35 us (2%)
    ppermute x7, starting transfers between devices, swapped(): return lax.ppermute(x, axis, pairs)  21.8 us
    all_to_all x1, blocking collectives, local(): sums = lax.all_to_all(sums, 'gx', 0, 0, tiled=True)  18.5 us
    pallas_call x7, Pallas kernels, call(): pl.pallas_call(kernel, out_shape=[jax.ShapeDtypeStruct(shape, dtype) for...  9.93 us
    all_to_all x1, blocking collectives, local(): sums = lax.all_to_all(sums, 'gy', 0, 0, tiled=True)  9.18 us
    ppermute x7, waiting for transfers between devices, swapped(): return lax.ppermute(x, axis, pairs)  2.64 us
  transfers between devices with their start and end apart: 7, of which 2 were waited for; matrix products, arithmetic and copies ran while one was open for 0% of the time, Pallas kernels for 2%

profile of v4, /device:TPU:1, one launch (start us, length us, event | category | flops | bytes accessed | tf_op | source)
XLA Modules:
  0.0 63.4 jit_solution(11004578357732294131)
XLA Ops:
  0.6 1.4 %shard_map.75 = (bf16[144,256]{1,0:T(8,128)(2,1)S(1)}, f32[80,128]{1,0:T(8,128)S(1)}, f32[48,128]{1,0:T(8,128)S(1)}, bf16[32,4,8,128]{3,2,1,0:T(8,128)(2,1)S(1)}) custom-call(bf16[27,32]{1,0:T(8,128)(2,1)} %w_hbm.1, bf16[32,4,8,128]{3,2,1,0:T(8,128)(2,1)} %f_hbm.1, s32[4,8,128]{2,1,0:T(8,128)} %lab_hbm.1), custom_call_target="tpu_custom_call" | custom-call | tf_op jit(solution)/shard_map/pallas_call | solution.py:447
  2.1 0.7 %collective-permute-start.1 = (f32[80,128]{1,0:T(8,128)S(1)}, f32[80,128]{1,0:T(8,128)S(1)}, u32[]{:S(2)}, u32[]{:S(2)}) collective-permute-start(f32[80,128]{1,0:T(8,128)S(1)} %get-tuple-element.18.own_ref), channel_id=1, source_target_pairs={{8,16},{16,8},{24,32},{32,24},{40,48},{48,40},{56,64},{64,56},{72,... | collective-permute-start | bytes 122888 | tf_op jit(solution)/shard_map/ppermute | solution.py:463
  2.7 5.4 %collective-permute-start = (f32[80,128]{1,0:T(8,128)S(1)}, f32[80,128]{1,0:T(8,128)S(1)}, u32[]{:S(2)}, u32[]{:S(2)}) collective-permute-start(f32[80,128]{1,0:T(8,128)S(1)} %get-tuple-element.18.own_ref), channel_id=1, source_target_pairs={{0,8},{8,0},{16,24},{24,16},{32,40},{40,32},{48,56},{56,48},{64,72... | collective-permute-start | bytes 122888 | tf_op jit(solution)/shard_map/ppermute | solution.py:463
  8.2 0.7 %collective-permute-start.3 = (f32[48,128]{1,0:T(8,128)S(1)}, f32[48,128]{1,0:T(8,128)S(1)}, u32[]{:S(2)}, u32[]{:S(2)}) collective-permute-start(f32[48,128]{1,0:T(8,128)S(1)} %get-tuple-element.19), channel_id=1, source_target_pairs={{16,32},{32,16},{24,40},{40,24},{48,64},{64,48},{56,72},{72,56},{8... | collective-permute-start | bytes 73736 | tf_op jit(solution)/shard_map/ppermute | solution.py:463
  8.8 6.7 %collective-permute-start.2 = (f32[48,128]{1,0:T(8,128)S(1)}, f32[48,128]{1,0:T(8,128)S(1)}, u32[]{:S(2)}, u32[]{:S(2)}) collective-permute-start(f32[48,128]{1,0:T(8,128)S(1)} %get-tuple-element.19), channel_id=1, source_target_pairs={{0,16},{16,0},{8,24},{24,8},{32,48},{48,32},{40,56},{56,40},{64,80... | collective-permute-start | bytes 73736 | tf_op jit(solution)/shard_map/ppermute | solution.py:463
  15.6 0.0 collective-permute-done.3.two_b_ref
  15.6 1.2 %collective-permute-done.2.two_a_ref = f32[48,128]{1,0:T(8,128)S(1)} collective-permute-done((f32[48,128]{1,0:T(8,128)S(1)}, f32[48,128]{1,0:T(8,128)S(1)}, u32[]{:S(2)}, u32[]{:S(2)}) %collective-permute-start.2) | collective-permute-done | bytes 24608 | tf_op jit(solution)/shard_map/ppermute | solution.py:463
  16.8 0.0 collective-permute-done.1.one_b_ref
  16.8 0.0 collective-permute-done.one_a_ref
  16.8 0.2 shard_map.76
  16.9 2.5 %collective-permute-start.4 = (f32[40,128]{1,0:T(8,128)S(1)}, f32[40,128]{1,0:T(8,128)S(1)}, u32[]{:S(2)}, u32[]{:S(2)}) collective-permute-start(f32[40,128]{1,0:T(8,128)S(1)} %get-tuple-element.22), channel_id=1, source_target_pairs={{0,1},{1,0},{2,3},{3,2},{4,5},{5,4},{6,7},{7,6},{8,9},{9,8},{10,11... | collective-permute-start | bytes 61448 | tf_op jit(solution)/shard_map/ppermute | solution.py:463
  19.4 3.0 %collective-permute-start.5 = (f32[40,128]{1,0:T(8,128)S(1)}, f32[40,128]{1,0:T(8,128)S(1)}, u32[]{:S(2)}, u32[]{:S(2)}) collective-permute-start(f32[40,128]{1,0:T(8,128)S(1)} %get-tuple-element.23), channel_id=1, source_target_pairs={{1,2},{2,1},{3,4},{4,3},{5,6},{6,5},{9,10},{10,9},{11,12},{12,11},... | collective-permute-start | bytes 61448 | tf_op jit(solution)/shard_map/ppermute | solution.py:463
  23.1 0.0 collective-permute-done.4.got_a_ref
  23.1 1.4 %collective-permute-done.5.got_b_ref = f32[40,128]{1,0:T(8,128)S(1)} collective-permute-done((f32[40,128]{1,0:T(8,128)S(1)}, f32[40,128]{1,0:T(8,128)S(1)}, u32[]{:S(2)}, u32[]{:S(2)}) %collective-permute-start.5) | collective-permute-done | bytes 20512 | tf_op jit(solution)/shard_map/ppermute | solution.py:463
  24.5 5.8 %shard_map.77 = (f32[3,4,16,256]{3,2,1,0:T(8,128)S(1)}, f32[8,24,128]{2,1,0:T(8,128)S(1)}) custom-call(f32[1]{0:T(128)S(6)} %copy.8.bias_ref, bf16[32,4,8,128]{3,2,1,0:T(8,128)(2,1)S(1)} %get-tuple-element.17.f_ref, f32[5,40,128]{2,1,0:T(8,128)S(1)} %get-tuple-element.20.main_ref, f32[4,24,128]{2,1,0:T(8,128)S(1)} %get-tuple-element.21.lab_ref, ...), custom_call_target="tpu_custom_call" | custom-call | tf_op jit(solution)/shard_map/pallas_call | solution.py:447
  30.3 9.2 %all_to_all.10.in_ref = f32[8,24,128]{2,1,0:T(8,128)S(1)} all-to-all(f32[8,24,128]{2,1,0:T(8,128)S(1)} %get-tuple-element.24), channel_id=1, replica_groups=mesh['gx'=32,'gy'=8] {'gy'}, dimensions={0} | all-to-all | bytes 196608 | tf_op jit(solution)/shard_map/all_to_all | solution.py:495
  39.5 18.5 %all_to_all.11.in_ref = f32[96,4,128]{2,1,0:T(4,128)S(1)} all-to-all(f32[96,4,128]{2,1,0:T(4,128)S(1)} %shard_map.78), channel_id=1, replica_groups=mesh['gx'=32,'gy'=8] {'gx'}, dimensions={0} | all-to-all | bytes 393216 | tf_op jit(solution)/shard_map/all_to_all | solution.py:497
  58.1 2.8 %collective-permute-start.6 = (f32[3,4,128]{2,1,0:T(4,128)S(1)}, f32[3,4,128]{2,1,0:T(4,128)S(1)}, u32[]{:S(2)}, u32[]{:S(2)}) collective-permute-start(f32[3,4,128]{2,1,0:T(4,128)S(1)} %shard_map.79.own_ref.refs_0_), channel_id=1, source_target_pairs={{0,1},{1,0},{2,3},{3,2},{4,5},{5,4},{6,7},{7,6},{8,9},{9,8},{10,11... | collective-permute-start | bytes 18440 | tf_op jit(solution)/shard_map/ppermute | solution.py:463
  60.9 1.5 %shard_map.81 = bf16[32,4,8,128]{3,2,1,0:T(8,128)(2,1)} custom-call(f32[3,4,128]{2,1,0:T(4,128)S(1)} %shard_map.79.own_ref.refs_0_, f32[3,4,16,256]{3,2,1,0:T(8,128)S(1)} %get-tuple-element.28.refs_1_, bf16[144,256]{1,0:T(8,128)(2,1)S(1)} %get-tuple-element.29.refs_2_), custom_call_target="tpu_custom_call" | custom-call | tf_op jit(solution)/shard_map/pallas_call | solution.py:447
  62.4 0.0 collective-permute-done.6.got_ref
  62.4 1.0 %shard_map.80 = (f32[1,1]{1,0:T(1,128)}, f32[27,32]{1,0:T(8,128)}, f32[1,1]{1,0:T(1,128)}) custom-call(f32[3,4,128]{2,1,0:T(4,128)S(1)} %shard_map.79.own_ref.refs_0_, f32[3,4,128]{2,1,0:T(4,128)S(1)} %collective-permute-done.6.got_ref), custom_call_target="tpu_custom_call" | custom-call | tf_op jit(solution)/shard_map/pallas_call | solution.py:447
  (2 shorter events, 0.1 us)
Async XLA Ops:
  2.1 14.7 %collective-permute-start.1 = (f32[80,128]{1,0:T(8,128)S(1)}, f32[80,128]{1,0:T(8,128)S(1)}, u32[]{:S(2)}, u32[]{:S(2)}) collective-permute-start(f32[80,128]{1,0:T(8,128)S(1)} %get-tuple-element.18.own_ref), channel_id=1, source_target_pairs={{8,16},{16,8},{24,32},{32,24},{40,48},{48,40},{56,64},{64,56},{72,... | collective-permute-start | bytes 122888 | tf_op jit(solution)/shard_map/ppermute | solution.py:463
  2.7 14.1 %collective-permute-start = (f32[80,128]{1,0:T(8,128)S(1)}, f32[80,128]{1,0:T(8,128)S(1)}, u32[]{:S(2)}, u32[]{:S(2)}) collective-permute-start(f32[80,128]{1,0:T(8,128)S(1)} %get-tuple-element.18.own_ref), channel_id=1, source_target_pairs={{0,8},{8,0},{16,24},{24,16},{32,40},{40,32},{48,56},{56,48},{64,72... | collective-permute-start | bytes 122888 | tf_op jit(solution)/shard_map/ppermute | solution.py:463
  8.2 7.4 %collective-permute-start.3 = (f32[48,128]{1,0:T(8,128)S(1)}, f32[48,128]{1,0:T(8,128)S(1)}, u32[]{:S(2)}, u32[]{:S(2)}) collective-permute-start(f32[48,128]{1,0:T(8,128)S(1)} %get-tuple-element.19), channel_id=1, source_target_pairs={{16,32},{32,16},{24,40},{40,24},{48,64},{64,48},{56,72},{72,56},{8... | collective-permute-start | bytes 73736 | tf_op jit(solution)/shard_map/ppermute | solution.py:463
  8.8 7.9 %collective-permute-start.2 = (f32[48,128]{1,0:T(8,128)S(1)}, f32[48,128]{1,0:T(8,128)S(1)}, u32[]{:S(2)}, u32[]{:S(2)}) collective-permute-start(f32[48,128]{1,0:T(8,128)S(1)} %get-tuple-element.19), channel_id=1, source_target_pairs={{0,16},{16,0},{8,24},{24,8},{32,48},{48,32},{40,56},{56,40},{64,80... | collective-permute-start | bytes 73736 | tf_op jit(solution)/shard_map/ppermute | solution.py:463
  16.9 6.1 %collective-permute-start.4 = (f32[40,128]{1,0:T(8,128)S(1)}, f32[40,128]{1,0:T(8,128)S(1)}, u32[]{:S(2)}, u32[]{:S(2)}) collective-permute-start(f32[40,128]{1,0:T(8,128)S(1)} %get-tuple-element.22), channel_id=1, source_target_pairs={{0,1},{1,0},{2,3},{3,2},{4,5},{5,4},{6,7},{7,6},{8,9},{9,8},{10,11... | collective-permute-start | bytes 61448 | tf_op jit(solution)/shard_map/ppermute | solution.py:463
  19.4 5.1 %collective-permute-start.5 = (f32[40,128]{1,0:T(8,128)S(1)}, f32[40,128]{1,0:T(8,128)S(1)}, u32[]{:S(2)}, u32[]{:S(2)}) collective-permute-start(f32[40,128]{1,0:T(8,128)S(1)} %get-tuple-element.23), channel_id=1, source_target_pairs={{1,2},{2,1},{3,4},{4,3},{5,6},{6,5},{9,10},{10,9},{11,12},{12,11},... | collective-permute-start | bytes 61448 | tf_op jit(solution)/shard_map/ppermute | solution.py:463
  58.1 4.3 %collective-permute-start.6 = (f32[3,4,128]{2,1,0:T(4,128)S(1)}, f32[3,4,128]{2,1,0:T(4,128)S(1)}, u32[]{:S(2)}, u32[]{:S(2)}) collective-permute-start(f32[3,4,128]{2,1,0:T(4,128)S(1)} %shard_map.79.own_ref.refs_0_), channel_id=1, source_target_pairs={{0,1},{1,0},{2,3},{3,2},{4,5},{5,4},{6,7},{7,6},{8,9},{9,8},{10,11... | collective-permute-start | bytes 18440 | tf_op jit(solution)/shard_map/ppermute | solution.py:463

commit v5 on v4

--- a/solution.py
+++ b/solution.py
@@ -209,7 +209,7 @@
 
 
 def skeleton_kernel(
-    bias_ref, f_ref, main_ref, lab_ref, got_a_ref, got_b_ref,
+    bias_ref, f_ref, main_ref, lab_ref, got_b_ref, got_a_ref,
     grad_ref, sums_ref,
     qs_ref, ds_ref, rs_ref, gain_ref,
 ):
@@ -394,7 +394,11 @@
     return loss, slopes, sums[4:]
 
 
-def weight_kernel(own_ref, got_ref, loss_ref, weight_ref, bias_ref):
+def weight_kernel(
+    own_ref, got_ref, feature_ref, loss_ref, weight_ref, bias_ref, feature_out_ref, sem
+):
+    copy = pltpu.make_async_copy(feature_ref, feature_out_ref, sem)
+    copy.start()
     even = (lax.axis_index("gy") & 1) == 0
     own, got = own_ref[...], got_ref[...]
     first, second = jnp.where(even, own, got), jnp.where(even, got, own)
@@ -412,6 +416,7 @@
         part = weight if b == 0 else pltpu.roll(weight, 128 - 32 * b, 1)
         for a in range(3):
             weight_ref[9 * a + 3 * b : 9 * a + 3 * b + 3] = part[3 * a : 3 * a + 3, :32]
+    copy.wait()
 
 
 def feature_kernel(sums_ref, grad_ref, a_ref, out_ref, *, voxels):
@@ -441,14 +446,15 @@
         out_ref[:, z] = acc_z.reshape(32, 8, 128).astype(BF16)
 
 
-def call(kernel, out_shapes, *args, scratch=(), spaces={}):
-    spec = pl.BlockSpec(memory_space=pltpu.VMEM)
+def call(kernel, out_shapes, *args, scratch=(), spaces={}, out_spaces={}):
     in_specs = [pl.BlockSpec(memory_space=spaces.get(n, pltpu.VMEM)) for n in range(len(args))]
     return pl.pallas_call(
         kernel,
         out_shape=[jax.ShapeDtypeStruct(shape, dtype) for shape, dtype in out_shapes],
         in_specs=in_specs,
-        out_specs=[spec] * len(out_shapes),
+        out_specs=[
+            pl.BlockSpec(memory_space=out_spaces.get(n, pltpu.VMEM)) for n in range(len(out_shapes))
+        ],
         scratch_shapes=list(scratch),
         compiler_params=pltpu.CompilerParams(vmem_limit_bytes=VMEM_LIMIT),
     )(*args)
@@ -484,12 +490,13 @@
         [((5, 40, 128), F32), ((4, 24, 128), F32), ((40, 128), F32), ((40, 128), F32)],
         near, *one, *two,
     )
-    got = [swapped(send_a, "gy", 1, 0), swapped(send_b, "gy", 1, 1)]
+    got_b = swapped(send_b, "gy", 1, 1)
+    got_a = swapped(send_a, "gy", 1, 0)
     field = pltpu.VMEM((ITERS + 1, 4, 24, 256), F32)
     grads, sums = call(
         skeleton_kernel,
         [((3, 4, 16, 256), F32), ((gy, 24, 128), F32)],
-        conv_bias, features, main, labels, *got,
+        conv_bias, features, main, labels, got_b, got_a,
         scratch=[field] * 4, spaces={0: pltpu.SMEM},
     )
     sums = lax.all_to_all(sums, "gy", 0, 0, tiled=True)
@@ -502,8 +509,12 @@
         feature_kernel(*refs, voxels=voxels)
 
     feature_grad = call(feature_part, [((32, 4, 8, 128), BF16)], sums, grads, matrix)[0]
-    loss, weight_grad, bias_grad = call(
-        weight_kernel, [((1, 1), F32), ((27, 32), F32), ((1, 1), F32)], sums, other
+    loss, weight_grad, bias_grad, feature_grad = call(
+        weight_kernel,
+        [((1, 1), F32), ((27, 32), F32), ((1, 1), F32), ((32, 4, 8, 128), BF16)],
+        sums, other, feature_grad,
+        scratch=[pltpu.SemaphoreType.DMA(())],
+        out_spaces={3: pltpu.HBM},
     )
     return (loss.reshape(()), weight_grad, bias_grad.reshape((1,)), feature_grad)
 

time: 63.7 us -> 63.2 us (level)
  waiting for transfers between devices: 2.64 us -> 1.94 us
    ppermute x7, waiting for transfers between devices: 2.64 us -> 1.94 us  [swapped(): return lax.ppermute(x, axis, pairs)]
  transfers between devices with their start and end apart: 7 -> 7, of which waited for: 2 -> 2; matrix products, arithmetic and copies ran while one was open for 0% -> 0% of each run, Pallas kernels for 2% -> 1%
where the time goes in v5:
time: 63.2 us; the launch traced here: 62.8 us
  blocking collectives  28.3 us (45%)
  starting transfers between devices  21.8 us (34%)
  Pallas kernels  9.53 us (15%)
  waiting for transfers between devices  1.94 us (3%)
  between operations  1.36 us (2%)
    ppermute x7, starting transfers between devices, swapped(): return lax.ppermute(x, axis, pairs)  21.8 us
    all_to_all x1, blocking collectives, local(): sums = lax.all_to_all(sums, 'gx', 0, 0, tiled=True)  18.5 us
    all_to_all x1, blocking collectives, local(): sums = lax.all_to_all(sums, 'gy', 0, 0, tiled=True)  9.71 us
    pallas_call x7, Pallas kernels, call(): pl.pallas_call(kernel, out_shape=[jax.ShapeDtypeStruct(shape, dtype) for...  9.53 us
    ppermute x7, waiting for transfers between devices, swapped(): return lax.ppermute(x, axis, pairs)  1.94 us
  transfers between devices with their start and end apart: 7, of which 2 were waited for; matrix products, arithmetic and copies ran while one was open for 0% of the time, Pallas kernels for 1%

profile of v5, /device:TPU:1, one launch (start us, length us, event | category | flops | bytes accessed | tf_op | source)
XLA Modules:
  0.0 62.8 jit_solution(15205290822831059246)
XLA Ops:
  0.6 1.4 %shard_map.75 = (bf16[144,256]{1,0:T(8,128)(2,1)S(1)}, f32[80,128]{1,0:T(8,128)S(1)}, f32[48,128]{1,0:T(8,128)S(1)}, bf16[32,4,8,128]{3,2,1,0:T(8,128)(2,1)S(1)}) custom-call(bf16[27,32]{1,0:T(8,128)(2,1)} %w_hbm.1, bf16[32,4,8,128]{3,2,1,0:T(8,128)(2,1)} %f_hbm.1, s32[4,8,128]{2,1,0:T(8,128)} %lab_hbm.1), custom_call_target="tpu_custom_call" | custom-call | tf_op jit(solution)/shard_map/pallas_call | solution.py:451
  2.1 0.7 %collective-permute-start.1 = (f32[80,128]{1,0:T(8,128)S(1)}, f32[80,128]{1,0:T(8,128)S(1)}, u32[]{:S(2)}, u32[]{:S(2)}) collective-permute-start(f32[80,128]{1,0:T(8,128)S(1)} %get-tuple-element.19.own_ref), channel_id=1, source_target_pairs={{8,16},{16,8},{24,32},{32,24},{40,48},{48,40},{56,64},{64,56},{72,... | collective-permute-start | bytes 122888 | tf_op jit(solution)/shard_map/ppermute | solution.py:469
  2.7 5.4 %collective-permute-start = (f32[80,128]{1,0:T(8,128)S(1)}, f32[80,128]{1,0:T(8,128)S(1)}, u32[]{:S(2)}, u32[]{:S(2)}) collective-permute-start(f32[80,128]{1,0:T(8,128)S(1)} %get-tuple-element.19.own_ref), channel_id=1, source_target_pairs={{0,8},{8,0},{16,24},{24,16},{32,40},{40,32},{48,56},{56,48},{64,72... | collective-permute-start | bytes 122888 | tf_op jit(solution)/shard_map/ppermute | solution.py:469
  8.2 0.7 %collective-permute-start.3 = (f32[48,128]{1,0:T(8,128)S(1)}, f32[48,128]{1,0:T(8,128)S(1)}, u32[]{:S(2)}, u32[]{:S(2)}) collective-permute-start(f32[48,128]{1,0:T(8,128)S(1)} %get-tuple-element.20), channel_id=1, source_target_pairs={{16,32},{32,16},{24,40},{40,24},{48,64},{64,48},{56,72},{72,56},{8... | collective-permute-start | bytes 73736 | tf_op jit(solution)/shard_map/ppermute | solution.py:469
  8.8 6.7 %collective-permute-start.2 = (f32[48,128]{1,0:T(8,128)S(1)}, f32[48,128]{1,0:T(8,128)S(1)}, u32[]{:S(2)}, u32[]{:S(2)}) collective-permute-start(f32[48,128]{1,0:T(8,128)S(1)} %get-tuple-element.20), channel_id=1, source_target_pairs={{0,16},{16,0},{8,24},{24,8},{32,48},{48,32},{40,56},{56,40},{64,80... | collective-permute-start | bytes 73736 | tf_op jit(solution)/shard_map/ppermute | solution.py:469
  15.6 0.0 collective-permute-done.3.two_b_ref
  15.6 1.2 %collective-permute-done.2.two_a_ref = f32[48,128]{1,0:T(8,128)S(1)} collective-permute-done((f32[48,128]{1,0:T(8,128)S(1)}, f32[48,128]{1,0:T(8,128)S(1)}, u32[]{:S(2)}, u32[]{:S(2)}) %collective-permute-start.2) | collective-permute-done | bytes 24608 | tf_op jit(solution)/shard_map/ppermute | solution.py:469
  16.8 0.0 collective-permute-done.1.one_b_ref
  16.8 0.0 collective-permute-done.one_a_ref
  16.8 0.2 shard_map.76
  16.9 5.4 %collective-permute-start.4 = (f32[40,128]{1,0:T(8,128)S(1)}, f32[40,128]{1,0:T(8,128)S(1)}, u32[]{:S(2)}, u32[]{:S(2)}) collective-permute-start(f32[40,128]{1,0:T(8,128)S(1)} %get-tuple-element.23), channel_id=1, source_target_pairs={{1,2},{2,1},{3,4},{4,3},{5,6},{6,5},{9,10},{10,9},{11,12},{12,11},... | collective-permute-start | bytes 61448 | tf_op jit(solution)/shard_map/ppermute | solution.py:469
  22.3 0.1 collective-permute-start.5
  23.1 0.7 %collective-permute-done.4.got_b_ref = f32[40,128]{1,0:T(8,128)S(1)} collective-permute-done((f32[40,128]{1,0:T(8,128)S(1)}, f32[40,128]{1,0:T(8,128)S(1)}, u32[]{:S(2)}, u32[]{:S(2)}) %collective-permute-start.4) | collective-permute-done | bytes 20512 | tf_op jit(solution)/shard_map/ppermute | solution.py:469
  23.8 0.0 collective-permute-done.5.got_a_ref
  23.8 5.8 %shard_map.77 = (f32[3,4,16,256]{3,2,1,0:T(8,128)S(1)}, f32[8,24,128]{2,1,0:T(8,128)S(1)}) custom-call(f32[1]{0:T(128)S(6)} %copy.8.bias_ref, bf16[32,4,8,128]{3,2,1,0:T(8,128)(2,1)S(1)} %get-tuple-element.18.f_ref, f32[5,40,128]{2,1,0:T(8,128)S(1)} %get-tuple-element.21.main_ref, f32[4,24,128]{2,1,0:T(8,128)S(1)} %get-tuple-element.22.lab_ref, ...), custom_call_target="tpu_custom_call" | custom-call | tf_op jit(solution)/shard_map/pallas_call | solution.py:451
  29.5 9.7 %all_to_all.10.in_ref = f32[8,24,128]{2,1,0:T(8,128)S(1)} all-to-all(f32[8,24,128]{2,1,0:T(8,128)S(1)} %get-tuple-element.25), channel_id=1, replica_groups=mesh['gx'=32,'gy'=8] {'gy'}, dimensions={0} | all-to-all | bytes 196608 | tf_op jit(solution)/shard_map/all_to_all | solution.py:502
  39.3 18.5 %all_to_all.11.in_ref = f32[96,4,128]{2,1,0:T(4,128)S(1)} all-to-all(f32[96,4,128]{2,1,0:T(4,128)S(1)} %shard_map.78), channel_id=1, replica_groups=mesh['gx'=32,'gy'=8] {'gx'}, dimensions={0} | all-to-all | bytes 393216 | tf_op jit(solution)/shard_map/all_to_all | solution.py:504
  57.9 2.8 %collective-permute-start.6 = (f32[3,4,128]{2,1,0:T(4,128)S(1)}, f32[3,4,128]{2,1,0:T(4,128)S(1)}, u32[]{:S(2)}, u32[]{:S(2)}) collective-permute-start(f32[3,4,128]{2,1,0:T(4,128)S(1)} %shard_map.79.refs_0_.own_ref), channel_id=1, source_target_pairs={{0,1},{1,0},{2,3},{3,2},{4,5},{5,4},{6,7},{7,6},{8,9},{9,8},{10,11... | collective-permute-start | bytes 18440 | tf_op jit(solution)/shard_map/ppermute | solution.py:469
  60.7 0.8 %shard_map.80.feature_ref = bf16[32,4,8,128]{3,2,1,0:T(8,128)(2,1)S(1)} custom-call(f32[3,4,128]{2,1,0:T(4,128)S(1)} %shard_map.79.refs_0_.own_ref, f32[3,4,16,256]{3,2,1,0:T(8,128)S(1)} %get-tuple-element.26.refs_1_, bf16[144,256]{1,0:T(8,128)(2,1)S(1)} %get-tuple-element.27.refs_2_), custom_call_target="tpu_custom_call" | custom-call | tf_op jit(solution)/shard_map/pallas_call | solution.py:451
  61.5 0.0 collective-permute-done.6.got_ref
  61.5 1.3 %shard_map.81 = (f32[1,1]{1,0:T(1,128)}, f32[27,32]{1,0:T(8,128)}, f32[1,1]{1,0:T(1,128)}, bf16[32,4,8,128]{3,2,1,0:T(8,128)(2,1)}) custom-call(f32[3,4,128]{2,1,0:T(4,128)S(1)} %shard_map.79.refs_0_.own_ref, f32[3,4,128]{2,1,0:T(4,128)S(1)} %collective-permute-done.6.got_ref, bf16[32,4,8,128]{3,2,1,0:T(8,128)(2,1)S(1)} %shard_map.80.feature_ref), custom_call_target="tpu_custom_call" | custom-call | tf_op jit(solution)/shard_map/pallas_call | solution.py:451
  (2 shorter events, 0.1 us)
Async XLA Ops:
  2.1 14.7 %collective-permute-start.1 = (f32[80,128]{1,0:T(8,128)S(1)}, f32[80,128]{1,0:T(8,128)S(1)}, u32[]{:S(2)}, u32[]{:S(2)}) collective-permute-start(f32[80,128]{1,0:T(8,128)S(1)} %get-tuple-element.19.own_ref), channel_id=1, source_target_pairs={{8,16},{16,8},{24,32},{32,24},{40,48},{48,40},{56,64},{64,56},{72,... | collective-permute-start | bytes 122888 | tf_op jit(solution)/shard_map/ppermute | solution.py:469
  2.7 14.1 %collective-permute-start = (f32[80,128]{1,0:T(8,128)S(1)}, f32[80,128]{1,0:T(8,128)S(1)}, u32[]{:S(2)}, u32[]{:S(2)}) collective-permute-start(f32[80,128]{1,0:T(8,128)S(1)} %get-tuple-element.19.own_ref), channel_id=1, source_target_pairs={{0,8},{8,0},{16,24},{24,16},{32,40},{40,32},{48,56},{56,48},{64,72... | collective-permute-start | bytes 122888 | tf_op jit(solution)/shard_map/ppermute | solution.py:469
  8.2 7.4 %collective-permute-start.3 = (f32[48,128]{1,0:T(8,128)S(1)}, f32[48,128]{1,0:T(8,128)S(1)}, u32[]{:S(2)}, u32[]{:S(2)}) collective-permute-start(f32[48,128]{1,0:T(8,128)S(1)} %get-tuple-element.20), channel_id=1, source_target_pairs={{16,32},{32,16},{24,40},{40,24},{48,64},{64,48},{56,72},{72,56},{8... | collective-permute-start | bytes 73736 | tf_op jit(solution)/shard_map/ppermute | solution.py:469
  8.8 7.9 %collective-permute-start.2 = (f32[48,128]{1,0:T(8,128)S(1)}, f32[48,128]{1,0:T(8,128)S(1)}, u32[]{:S(2)}, u32[]{:S(2)}) collective-permute-start(f32[48,128]{1,0:T(8,128)S(1)} %get-tuple-element.20), channel_id=1, source_target_pairs={{0,16},{16,0},{8,24},{24,8},{32,48},{48,32},{40,56},{56,40},{64,80... | collective-permute-start | bytes 73736 | tf_op jit(solution)/shard_map/ppermute | solution.py:469
  16.9 6.8 %collective-permute-start.4 = (f32[40,128]{1,0:T(8,128)S(1)}, f32[40,128]{1,0:T(8,128)S(1)}, u32[]{:S(2)}, u32[]{:S(2)}) collective-permute-start(f32[40,128]{1,0:T(8,128)S(1)} %get-tuple-element.23), channel_id=1, source_target_pairs={{1,2},{2,1},{3,4},{4,3},{5,6},{6,5},{9,10},{10,9},{11,12},{12,11},... | collective-permute-start | bytes 61448 | tf_op jit(solution)/shard_map/ppermute | solution.py:469
  22.3 1.5 %collective-permute-start.5 = (f32[40,128]{1,0:T(8,128)S(1)}, f32[40,128]{1,0:T(8,128)S(1)}, u32[]{:S(2)}, u32[]{:S(2)}) collective-permute-start(f32[40,128]{1,0:T(8,128)S(1)} %get-tuple-element.24), channel_id=1, source_target_pairs={{0,1},{1,0},{2,3},{3,2},{4,5},{5,4},{6,7},{7,6},{8,9},{9,8},{10,11... | collective-permute-start | bytes 61448 | tf_op jit(solution)/shard_map/ppermute | solution.py:469
  57.9 3.6 %collective-permute-start.6 = (f32[3,4,128]{2,1,0:T(4,128)S(1)}, f32[3,4,128]{2,1,0:T(4,128)S(1)}, u32[]{:S(2)}, u32[]{:S(2)}) collective-permute-start(f32[3,4,128]{2,1,0:T(4,128)S(1)} %shard_map.79.refs_0_.own_ref), channel_id=1, source_target_pairs={{0,1},{1,0},{2,3},{3,2},{4,5},{5,4},{6,7},{7,6},{8,9},{9,8},{10,11... | collective-permute-start | bytes 18440 | tf_op jit(solution)/shard_map/ppermute | solution.py:469

commit v6 on v5

--- a/solution.py
+++ b/solution.py
@@ -92,7 +92,7 @@
 
 
 def rows_kernel(
-    own_ref, one_a_ref, one_b_ref, two_a_ref, two_b_ref, main_ref, lab_ref, send_a_ref, send_b_ref
+    own_ref, two_b_ref, two_a_ref, one_b_ref, one_a_ref, main_ref, lab_ref, send_a_ref, send_b_ref
 ):
     row_block, col_block = lax.axis_index("gx"), lax.axis_index("gy")
     even1 = (row_block & 1) == 0
@@ -395,10 +395,16 @@
 
 
 def weight_kernel(
-    own_ref, got_ref, feature_ref, loss_ref, weight_ref, bias_ref, feature_out_ref, sem
+    own_ref, got_ref, feature_ref,
+    loss_out_ref, weight_out_ref, bias_out_ref, feature_out_ref,
+    loss_ref, weight_ref, bias_ref, sems,
 ):
-    copy = pltpu.make_async_copy(feature_ref, feature_out_ref, sem)
-    copy.start()
+    pairs = [
+        (feature_ref, feature_out_ref), (loss_ref, loss_out_ref),
+        (bias_ref, bias_out_ref), (weight_ref, weight_out_ref),
+    ]
+    copies = [pltpu.make_async_copy(x, y, sems.at[n]) for n, (x, y) in enumerate(pairs)]
+    copies[0].start()
     even = (lax.axis_index("gy") & 1) == 0
     own, got = own_ref[...], got_ref[...]
     first, second = jnp.where(even, own, got), jnp.where(even, got, own)
@@ -406,6 +412,8 @@
     loss, slopes, bias_sums = loss_and_slopes(acc[11:12])
     loss_ref[...] = loss
     bias_ref[...] = sum(slopes[f] * bias_sums[f] for f in range(3))
+    copies[1].start()
+    copies[2].start()
     group = iota((3, 128), 1) >> 5
     last = acc[18:21]
     for b in range(3):
@@ -416,7 +424,9 @@
         part = weight if b == 0 else pltpu.roll(weight, 128 - 32 * b, 1)
         for a in range(3):
             weight_ref[9 * a + 3 * b : 9 * a + 3 * b + 3] = part[3 * a : 3 * a + 3, :32]
-    copy.wait()
+    copies[3].start()
+    for copy in copies:
+        copy.wait()
 
 
 def feature_kernel(sums_ref, grad_ref, a_ref, out_ref, *, voxels):
@@ -488,7 +498,7 @@
     main, labels, send_a, send_b = call(
         rows_kernel,
         [((5, 40, 128), F32), ((4, 24, 128), F32), ((40, 128), F32), ((40, 128), F32)],
-        near, *one, *two,
+        near, *two[::-1], *one[::-1],
     )
     got_b = swapped(send_b, "gy", 1, 1)
     got_a = swapped(send_a, "gy", 1, 0)
@@ -513,8 +523,13 @@
         weight_kernel,
         [((1, 1), F32), ((27, 32), F32), ((1, 1), F32), ((32, 4, 8, 128), BF16)],
         sums, other, feature_grad,
-        scratch=[pltpu.SemaphoreType.DMA(())],
-        out_spaces={3: pltpu.HBM},
+        scratch=[
+            pltpu.VMEM((1, 1), F32),
+            pltpu.VMEM((27, 32), F32),
+            pltpu.VMEM((1, 1), F32),
+            pltpu.SemaphoreType.DMA((4,)),
+        ],
+        out_spaces={n: pltpu.HBM for n in range(4)},
     )
     return (loss.reshape(()), weight_grad, bias_grad.reshape((1,)), feature_grad)
 

time: 63.2 us -> 62.7 us (level)
  blocking collectives: 28.3 us -> 34.2 us
  starting transfers between devices: 21.8 us -> 15.9 us
    all_to_all x1, blocking collectives: 18.5 us -> 24.5 us  [local(): sums = lax.all_to_all(sums, 'gx', 0, 0, tiled=True)]
    ppermute x7, starting transfers between devices: 21.8 us -> 15.9 us  [swapped(): return lax.ppermute(x, axis, pairs)]
where the time goes in v6:
time: 62.7 us; the launch traced here: 62.4 us
  blocking collectives  34.2 us (55%)
  starting transfers between devices  15.9 us (25%)
  Pallas kernels  9.26 us (15%)
  waiting for transfers between devices  1.6 us (3%)
  between operations  1.36 us (2%)
    all_to_all x1, blocking collectives, local(): sums = lax.all_to_all(sums, 'gx', 0, 0, tiled=True)  24.5 us
    ppermute x7, starting transfers between devices, swapped(): return lax.ppermute(x, axis, pairs)  15.9 us
    all_to_all x1, blocking collectives, local(): sums = lax.all_to_all(sums, 'gy', 0, 0, tiled=True)  9.71 us
    pallas_call x7, Pallas kernels, call(): pl.pallas_call(kernel, out_shape=[jax.ShapeDtypeStruct(shape, dtype) for...  9.26 us
    ppermute x7, waiting for transfers between devices, swapped(): return lax.ppermute(x, axis, pairs)  1.6 us
  transfers between devices with their start and end apart: 7, of which 2 were waited for; matrix products, arithmetic and copies ran while one was open for 0% of the time, Pallas kernels for 1%

profile of v6, /device:TPU:1, one launch (start us, length us, event | category | flops | bytes accessed | tf_op | source)
XLA Modules:
  0.0 62.4 jit_solution(5593128474174214568)
XLA Ops:
  0.6 1.4 %shard_map.75 = (bf16[144,256]{1,0:T(8,128)(2,1)S(1)}, f32[80,128]{1,0:T(8,128)S(1)}, f32[48,128]{1,0:T(8,128)S(1)}, bf16[32,4,8,128]{3,2,1,0:T(8,128)(2,1)S(1)}) custom-call(bf16[27,32]{1,0:T(8,128)(2,1)} %w_hbm.1, bf16[32,4,8,128]{3,2,1,0:T(8,128)(2,1)} %f_hbm.1, s32[4,8,128]{2,1,0:T(8,128)} %lab_hbm.1), custom_call_target="tpu_custom_call" | custom-call | tf_op jit(solution)/shard_map/pallas_call | solution.py:461
  2.1 2.6 %collective-permute-start.3 = (f32[80,128]{1,0:T(8,128)S(1)}, f32[80,128]{1,0:T(8,128)S(1)}, u32[]{:S(2)}, u32[]{:S(2)}) collective-permute-start(f32[80,128]{1,0:T(8,128)S(1)} %get-tuple-element.19.own_ref), channel_id=1, source_target_pairs={{0,8},{8,0},{16,24},{24,16},{32,40},{40,32},{48,56},{56,48},{64,72... | collective-permute-start | bytes 122888 | tf_op jit(solution)/shard_map/ppermute | solution.py:479
  4.6 0.7 %collective-permute-start.2 = (f32[80,128]{1,0:T(8,128)S(1)}, f32[80,128]{1,0:T(8,128)S(1)}, u32[]{:S(2)}, u32[]{:S(2)}) collective-permute-start(f32[80,128]{1,0:T(8,128)S(1)} %get-tuple-element.19.own_ref), channel_id=1, source_target_pairs={{8,16},{16,8},{24,32},{32,24},{40,48},{48,40},{56,64},{64,56},{72,... | collective-permute-start | bytes 122888 | tf_op jit(solution)/shard_map/ppermute | solution.py:479
  5.3 4.3 %collective-permute-start.1 = (f32[48,128]{1,0:T(8,128)S(1)}, f32[48,128]{1,0:T(8,128)S(1)}, u32[]{:S(2)}, u32[]{:S(2)}) collective-permute-start(f32[48,128]{1,0:T(8,128)S(1)} %get-tuple-element.20), channel_id=1, source_target_pairs={{0,16},{16,0},{8,24},{24,8},{32,48},{48,32},{40,56},{56,40},{64,80... | collective-permute-start | bytes 73736 | tf_op jit(solution)/shard_map/ppermute | solution.py:479
  9.6 0.7 %collective-permute-start = (f32[48,128]{1,0:T(8,128)S(1)}, f32[48,128]{1,0:T(8,128)S(1)}, u32[]{:S(2)}, u32[]{:S(2)}) collective-permute-start(f32[48,128]{1,0:T(8,128)S(1)} %get-tuple-element.20), channel_id=1, source_target_pairs={{16,32},{32,16},{24,40},{40,24},{48,64},{64,48},{56,72},{72,56},{8... | collective-permute-start | bytes 73736 | tf_op jit(solution)/shard_map/ppermute | solution.py:479
  10.3 0.9 %collective-permute-done.1.two_a_ref = f32[48,128]{1,0:T(8,128)S(1)} collective-permute-done((f32[48,128]{1,0:T(8,128)S(1)}, f32[48,128]{1,0:T(8,128)S(1)}, u32[]{:S(2)}, u32[]{:S(2)}) %collective-permute-start.1) | collective-permute-done | bytes 24608 | tf_op jit(solution)/shard_map/ppermute | solution.py:479
  11.1 0.0 collective-permute-done.two_b_ref
  11.1 0.0 collective-permute-done.3.one_a_ref
  11.1 0.0 collective-permute-done.2.one_b_ref
  11.2 0.2 shard_map.76
  11.3 4.8 %collective-permute-start.4 = (f32[40,128]{1,0:T(8,128)S(1)}, f32[40,128]{1,0:T(8,128)S(1)}, u32[]{:S(2)}, u32[]{:S(2)}) collective-permute-start(f32[40,128]{1,0:T(8,128)S(1)} %get-tuple-element.23), channel_id=1, source_target_pairs={{1,2},{2,1},{3,4},{4,3},{5,6},{6,5},{9,10},{10,9},{11,12},{12,11},... | collective-permute-start | bytes 61448 | tf_op jit(solution)/shard_map/ppermute | solution.py:479
  16.2 0.1 collective-permute-start.5
  16.9 0.7 %collective-permute-done.4.got_b_ref = f32[40,128]{1,0:T(8,128)S(1)} collective-permute-done((f32[40,128]{1,0:T(8,128)S(1)}, f32[40,128]{1,0:T(8,128)S(1)}, u32[]{:S(2)}, u32[]{:S(2)}) %collective-permute-start.4) | collective-permute-done | bytes 20512 | tf_op jit(solution)/shard_map/ppermute | solution.py:479
  17.6 0.0 collective-permute-done.5.got_a_ref
  17.6 5.8 %shard_map.77 = (f32[3,4,16,256]{3,2,1,0:T(8,128)S(1)}, f32[8,24,128]{2,1,0:T(8,128)S(1)}) custom-call(f32[1]{0:T(128)S(6)} %copy.8.bias_ref, bf16[32,4,8,128]{3,2,1,0:T(8,128)(2,1)S(1)} %get-tuple-element.18.f_ref, f32[5,40,128]{2,1,0:T(8,128)S(1)} %get-tuple-element.21.main_ref, f32[4,24,128]{2,1,0:T(8,128)S(1)} %get-tuple-element.22.lab_ref, ...), custom_call_target="tpu_custom_call" | custom-call | tf_op jit(solution)/shard_map/pallas_call | solution.py:461
  23.4 9.7 %all_to_all.10.in_ref = f32[8,24,128]{2,1,0:T(8,128)S(1)} all-to-all(f32[8,24,128]{2,1,0:T(8,128)S(1)} %get-tuple-element.25), channel_id=1, replica_groups=mesh['gx'=32,'gy'=8] {'gy'}, dimensions={0} | all-to-all | bytes 196608 | tf_op jit(solution)/shard_map/all_to_all | solution.py:512
  33.1 24.5 %all_to_all.11.in_ref = f32[96,4,128]{2,1,0:T(4,128)S(1)} all-to-all(f32[96,4,128]{2,1,0:T(4,128)S(1)} %shard_map.78), channel_id=1, replica_groups=mesh['gx'=32,'gy'=8] {'gx'}, dimensions={0} | all-to-all | bytes 393216 | tf_op jit(solution)/shard_map/all_to_all | solution.py:514
  57.7 2.8 %collective-permute-start.6 = (f32[3,4,128]{2,1,0:T(4,128)S(1)}, f32[3,4,128]{2,1,0:T(4,128)S(1)}, u32[]{:S(2)}, u32[]{:S(2)}) collective-permute-start(f32[3,4,128]{2,1,0:T(4,128)S(1)} %shard_map.79.refs_0_.own_ref), channel_id=1, source_target_pairs={{0,1},{1,0},{2,3},{3,2},{4,5},{5,4},{6,7},{7,6},{8,9},{9,8},{10,11... | collective-permute-start | bytes 18440 | tf_op jit(solution)/shard_map/ppermute | solution.py:479
  60.5 0.8 %shard_map.80.feature_ref = bf16[32,4,8,128]{3,2,1,0:T(8,128)(2,1)S(1)} custom-call(f32[3,4,128]{2,1,0:T(4,128)S(1)} %shard_map.79.refs_0_.own_ref, f32[3,4,16,256]{3,2,1,0:T(8,128)S(1)} %get-tuple-element.26.refs_1_, bf16[144,256]{1,0:T(8,128)(2,1)S(1)} %get-tuple-element.27.refs_2_), custom_call_target="tpu_custom_call" | custom-call | tf_op jit(solution)/shard_map/pallas_call | solution.py:461
  61.3 0.0 collective-permute-done.6.got_ref
  61.3 1.0 %shard_map.81 = (f32[1,1]{1,0:T(1,128)}, f32[27,32]{1,0:T(8,128)}, f32[1,1]{1,0:T(1,128)}, bf16[32,4,8,128]{3,2,1,0:T(8,128)(2,1)}) custom-call(f32[3,4,128]{2,1,0:T(4,128)S(1)} %shard_map.79.refs_0_.own_ref, f32[3,4,128]{2,1,0:T(4,128)S(1)} %collective-permute-done.6.got_ref, bf16[32,4,8,128]{3,2,1,0:T(8,128)(2,1)S(1)} %shard_map.80.feature_ref), custom_call_target="tpu_custom_call" | custom-call | tf_op jit(solution)/shard_map/pallas_call | solution.py:461
  (2 shorter events, 0.1 us)
Async XLA Ops:
  2.1 9.1 %collective-permute-start.3 = (f32[80,128]{1,0:T(8,128)S(1)}, f32[80,128]{1,0:T(8,128)S(1)}, u32[]{:S(2)}, u32[]{:S(2)}) collective-permute-start(f32[80,128]{1,0:T(8,128)S(1)} %get-tuple-element.19.own_ref), channel_id=1, source_target_pairs={{0,8},{8,0},{16,24},{24,16},{32,40},{40,32},{48,56},{56,48},{64,72... | collective-permute-start | bytes 122888 | tf_op jit(solution)/shard_map/ppermute | solution.py:479
  4.6 6.5 %collective-permute-start.2 = (f32[80,128]{1,0:T(8,128)S(1)}, f32[80,128]{1,0:T(8,128)S(1)}, u32[]{:S(2)}, u32[]{:S(2)}) collective-permute-start(f32[80,128]{1,0:T(8,128)S(1)} %get-tuple-element.19.own_ref), channel_id=1, source_target_pairs={{8,16},{16,8},{24,32},{32,24},{40,48},{48,40},{56,64},{64,56},{72,... | collective-permute-start | bytes 122888 | tf_op jit(solution)/shard_map/ppermute | solution.py:479
  5.3 5.9 %collective-permute-start.1 = (f32[48,128]{1,0:T(8,128)S(1)}, f32[48,128]{1,0:T(8,128)S(1)}, u32[]{:S(2)}, u32[]{:S(2)}) collective-permute-start(f32[48,128]{1,0:T(8,128)S(1)} %get-tuple-element.20), channel_id=1, source_target_pairs={{0,16},{16,0},{8,24},{24,8},{32,48},{48,32},{40,56},{56,40},{64,80... | collective-permute-start | bytes 73736 | tf_op jit(solution)/shard_map/ppermute | solution.py:479
  9.6 1.5 %collective-permute-start = (f32[48,128]{1,0:T(8,128)S(1)}, f32[48,128]{1,0:T(8,128)S(1)}, u32[]{:S(2)}, u32[]{:S(2)}) collective-permute-start(f32[48,128]{1,0:T(8,128)S(1)} %get-tuple-element.20), channel_id=1, source_target_pairs={{16,32},{32,16},{24,40},{40,24},{48,64},{64,48},{56,72},{72,56},{8... | collective-permute-start | bytes 73736 | tf_op jit(solution)/shard_map/ppermute | solution.py:479
  11.3 6.3 %collective-permute-start.4 = (f32[40,128]{1,0:T(8,128)S(1)}, f32[40,128]{1,0:T(8,128)S(1)}, u32[]{:S(2)}, u32[]{:S(2)}) collective-permute-start(f32[40,128]{1,0:T(8,128)S(1)} %get-tuple-element.23), channel_id=1, source_target_pairs={{1,2},{2,1},{3,4},{4,3},{5,6},{6,5},{9,10},{10,9},{11,12},{12,11},... | collective-permute-start | bytes 61448 | tf_op jit(solution)/shard_map/ppermute | solution.py:479
  16.2 1.5 %collective-permute-start.5 = (f32[40,128]{1,0:T(8,128)S(1)}, f32[40,128]{1,0:T(8,128)S(1)}, u32[]{:S(2)}, u32[]{:S(2)}) collective-permute-start(f32[40,128]{1,0:T(8,128)S(1)} %get-tuple-element.24), channel_id=1, source_target_pairs={{0,1},{1,0},{2,3},{3,2},{4,5},{5,4},{6,7},{7,6},{8,9},{9,8},{10,11... | collective-permute-start | bytes 61448 | tf_op jit(solution)/shard_map/ppermute | solution.py:479
  57.7 3.6 %collective-permute-start.6 = (f32[3,4,128]{2,1,0:T(4,128)S(1)}, f32[3,4,128]{2,1,0:T(4,128)S(1)}, u32[]{:S(2)}, u32[]{:S(2)}) collective-permute-start(f32[3,4,128]{2,1,0:T(4,128)S(1)} %shard_map.79.refs_0_.own_ref), channel_id=1, source_target_pairs={{0,1},{1,0},{2,3},{3,2},{4,5},{5,4},{6,7},{7,6},{8,9},{9,8},{10,11... | collective-permute-start | bytes 18440 | tf_op jit(solution)/shard_map/ppermute | solution.py:479

commit v7 on v6

--- a/solution.py
+++ b/solution.py
@@ -87,6 +87,7 @@
     far_ref[32:40] = edges
     near_ref[40:48] = corners
     far_ref[40:48] = corners
+    far_ref[48:88] = jnp.zeros((40, 128), F32)
     copies[2].wait()
     near_ref[48:80] = lab_ref[...].reshape(32, 128).astype(F32)
 
@@ -101,6 +102,7 @@
     own = own_ref[...]
     one_a, one_b, two_a, two_b = one_a_ref[...], one_b_ref[...], two_a_ref[...], two_b_ref[...]
     before, after = jnp.where(even1, one_b, one_a), jnp.where(even1, one_a, one_b)
+    two_a, two_b = two_a[:48], two_b[:48]
     blocks = [jnp.where(even2, two_b, two_a), before, own, after, jnp.where(even2, two_a, two_b)]
     sub = iota((8, 128), 0)
     ends = at_end(iota((8, 128), 1))
@@ -210,7 +212,7 @@
 
 def skeleton_kernel(
     bias_ref, f_ref, main_ref, lab_ref, got_b_ref, got_a_ref,
-    grad_ref, sums_ref,
+    grad_ref, keep_ref, send_ref,
     qs_ref, ds_ref, rs_ref, gain_ref,
 ):
     row_ids = lax.axis_index("gx") * 8 - 16 + iota((40, 256), 0)
@@ -357,15 +359,16 @@
     row24, lane_of = iota((24, 128), 0), iota((24, 128), 1)
     for k, value in enumerate([t0, t1, t2, t3] + bias_sums):
         result = jnp.where(((row24 == 11) | (row24 == 23)) & (lane_of == 96 + k), value, result)
-    for n in range(sums_ref.shape[0]):
-        sums_ref[n] = result
-
-
-def half_kernel(in_ref, out_ref):
-    acc = in_ref[0]
-    for n in range(1, in_ref.shape[0]):
-        acc = acc + in_ref[n]
-    half = jnp.where((lax.axis_index("gy") & 1) == 0, acc[:12], acc[12:])
+    keep_ref[...] = jnp.where(even_col, result[:12], result[12:])
+    send_ref[...] = jnp.where(even_col, result[12:], result[:12])
+
+
+def pair_kernel(own_ref, got_ref, out_ref):
+    out_ref[...] = own_ref[...] + got_ref[...]
+
+
+def four_kernel(own_ref, one_ref, two_ref, three_ref, out_ref):
+    half = (own_ref[...] + one_ref[...]) + (two_ref[...] + three_ref[...])
     for n in range(out_ref.shape[0]):
         out_ref[n] = half[4 * (n % 3) : 4 * (n % 3) + 4]
 
@@ -484,7 +487,7 @@
     voxels = float(4 * 8 * gx * 128 * gy)
     matrix, near, far, features = call(
         partial_logits_kernel,
-        [((144, 256), BF16), ((80, 128), F32), ((48, 128), F32), (features.shape, BF16)],
+        [((144, 256), BF16), ((80, 128), F32), ((88, 128), F32), (features.shape, BF16)],
         *[pltpu.with_memory_space_constraint(x, pltpu.HBM) for x in (conv_weight, features, vessel_label)],
         scratch=[
             pltpu.VMEM((27, 32), BF16),
@@ -503,14 +506,15 @@
     got_b = swapped(send_b, "gy", 1, 1)
     got_a = swapped(send_a, "gy", 1, 0)
     field = pltpu.VMEM((ITERS + 1, 4, 24, 256), F32)
-    grads, sums = call(
+    grads, keep, send = call(
         skeleton_kernel,
-        [((3, 4, 16, 256), F32), ((gy, 24, 128), F32)],
+        [((3, 4, 16, 256), F32), ((12, 128), F32), ((12, 128), F32)],
         conv_bias, features, main, labels, got_b, got_a,
         scratch=[field] * 4, spaces={0: pltpu.SMEM},
     )
-    sums = lax.all_to_all(sums, "gy", 0, 0, tiled=True)
-    sums = call(half_kernel, [((3 * gx, 4, 128), F32)], sums)[0]
+    half = call(pair_kernel, [((12, 128), F32)], keep, swapped(send, "gy", 1, 0))[0]
+    others = [lax.ppermute(half, "gy", [(n, n ^ mask) for n in range(gy)]) for mask in (2, 4, 6)]
+    sums = call(four_kernel, [((3 * gx, 4, 128), F32)], half, *others)[0]
     sums = lax.all_to_all(sums, "gx", 0, 0, tiled=True)
     sums = call(add_kernel, [((3, 4, 128), F32)], sums)[0]
     other = swapped(sums, "gy", 1, 0)

time: 62.7 us -> 60.9 us (0.971)
  blocking collectives: 34.2 us -> 25 us
  waiting for transfers between devices: 1.6 us -> 6.68 us
  starting transfers between devices: 15.9 us -> 18.3 us
    all_to_all x1 -> x0, blocking collectives: 9.71 us -> none  [local(): sums = lax.all_to_all(sums, 'gy', 0, 0, tiled=True)]
    ppermute x0 -> x3, waiting for transfers between devices: none -> 3.43 us  [local(): lax.ppermute(half, 'gy', [(n, n ^ mask) for n in range(gy)])]
    ppermute x0 -> x3, starting transfers between devices: none -> 3.36 us  [local(): lax.ppermute(half, 'gy', [(n, n ^ mask) for n in range(gy)])]
    ppermute x7 -> x8, waiting for transfers between devices: 1.6 us -> 3.25 us  [swapped(): return lax.ppermute(x, axis, pairs)]
    ppermute x7 -> x8, starting transfers between devices: 15.9 us -> 14.9 us  [swapped(): return lax.ppermute(x, axis, pairs)]
    pallas_call x7 -> x8, Pallas kernels: 9.26 us -> 9.26 us  [call(): pl.pallas_call(kernel, out_shape=[jax.ShapeDtypeStruct(shape, dtype) for...]
  transfers between devices with their start and end apart: 7 -> 11, of which waited for: 2 -> 5; matrix products, arithmetic and copies ran while one was open for 0% -> 0% of each run, Pallas kernels for 1% -> 1%
where the time goes in v7:
time: 60.9 us; the launch traced here: 60.6 us
  blocking collectives  25 us (41%)
  starting transfers between devices  18.3 us (30%)
  Pallas kernels  9.26 us (15%)
  waiting for transfers between devices  6.68 us (11%)
  between operations  1.38 us (2%)
    all_to_all x1, blocking collectives, local(): sums = lax.all_to_all(sums, 'gx', 0, 0, tiled=True)  25 us
    ppermute x8, starting transfers between devices, swapped(): return lax.ppermute(x, axis, pairs)  14.9 us
    pallas_call x8, Pallas kernels, call(): pl.pallas_call(kernel, out_shape=[jax.ShapeDtypeStruct(shape, dtype) for...  9.26 us
    ppermute x3, waiting for transfers between devices, local(): lax.ppermute(half, 'gy', [(n, n ^ mask) for n in range(gy)])  3.43 us
    ppermute x3, starting transfers between devices, local(): lax.ppermute(half, 'gy', [(n, n ^ mask) for n in range(gy)])  3.36 us
    ppermute x8, waiting for transfers between devices, swapped(): return lax.ppermute(x, axis, pairs)  3.25 us
  transfers between devices with their start and end apart: 11, of which 5 were waited for; matrix products, arithmetic and copies ran while one was open for 0% of the time, Pallas kernels for 1%

profile of v7, /device:TPU:1, one launch (start us, length us, event | category | flops | bytes accessed | tf_op | source)
XLA Modules:
  0.0 60.6 jit_solution(1065419030441907396)
XLA Ops:
  0.6 1.4 %shard_map.75 = (bf16[144,256]{1,0:T(8,128)(2,1)S(1)}, f32[80,128]{1,0:T(8,128)S(1)}, f32[88,128]{1,0:T(8,128)S(1)}, bf16[32,4,8,128]{3,2,1,0:T(8,128)(2,1)S(1)}) custom-call(bf16[27,32]{1,0:T(8,128)(2,1)} %w_hbm.1, bf16[32,4,8,128]{3,2,1,0:T(8,128)(2,1)} %f_hbm.1, s32[4,8,128]{2,1,0:T(8,128)} %lab_hbm.1), custom_call_target="tpu_custom_call" | custom-call | tf_op jit(solution)/shard_map/pallas_call | solution.py:464
  2.1 3.9 %collective-permute-start.1 = (f32[88,128]{1,0:T(8,128)S(1)}, f32[88,128]{1,0:T(8,128)S(1)}, u32[]{:S(2)}, u32[]{:S(2)}) collective-permute-start(f32[88,128]{1,0:T(8,128)S(1)} %get-tuple-element.21), channel_id=1, source_target_pairs={{0,16},{16,0},{8,24},{24,8},{32,48},{48,32},{40,56},{56,40},{64,80... | collective-permute-start | bytes 135176 | tf_op jit(solution)/shard_map/ppermute | solution.py:482
  6.0 0.7 %collective-permute-start = (f32[88,128]{1,0:T(8,128)S(1)}, f32[88,128]{1,0:T(8,128)S(1)}, u32[]{:S(2)}, u32[]{:S(2)}) collective-permute-start(f32[88,128]{1,0:T(8,128)S(1)} %get-tuple-element.21), channel_id=1, source_target_pairs={{16,32},{32,16},{24,40},{40,24},{48,64},{64,48},{56,72},{72,56},{8... | collective-permute-start | bytes 135176 | tf_op jit(solution)/shard_map/ppermute | solution.py:482
  6.6 1.7 %collective-permute-start.3 = (f32[80,128]{1,0:T(8,128)S(1)}, f32[80,128]{1,0:T(8,128)S(1)}, u32[]{:S(2)}, u32[]{:S(2)}) collective-permute-start(f32[80,128]{1,0:T(8,128)S(1)} %get-tuple-element.20.own_ref), channel_id=1, source_target_pairs={{0,8},{8,0},{16,24},{24,16},{32,40},{40,32},{48,56},{56,48},{64,72... | collective-permute-start | bytes 122888 | tf_op jit(solution)/shard_map/ppermute | solution.py:482
  8.3 0.7 %collective-permute-start.2 = (f32[80,128]{1,0:T(8,128)S(1)}, f32[80,128]{1,0:T(8,128)S(1)}, u32[]{:S(2)}, u32[]{:S(2)}) collective-permute-start(f32[80,128]{1,0:T(8,128)S(1)} %get-tuple-element.20.own_ref), channel_id=1, source_target_pairs={{8,16},{16,8},{24,32},{32,24},{40,48},{48,40},{56,64},{64,56},{72,... | collective-permute-start | bytes 122888 | tf_op jit(solution)/shard_map/ppermute | solution.py:482
  9.0 1.4 %collective-permute-done.3.one_a_ref = f32[80,128]{1,0:T(8,128)S(1)} collective-permute-done((f32[80,128]{1,0:T(8,128)S(1)}, f32[80,128]{1,0:T(8,128)S(1)}, u32[]{:S(2)}, u32[]{:S(2)}) %collective-permute-start.3) | collective-permute-done | bytes 40992 | tf_op jit(solution)/shard_map/ppermute | solution.py:482
  10.4 0.0 collective-permute-done.2.one_b_ref
  10.4 0.0 collective-permute-done.1.two_a_ref
  10.4 0.0 collective-permute-done.two_b_ref
  10.4 0.2 shard_map.76
  10.6 4.3 %collective-permute-start.4 = (f32[40,128]{1,0:T(8,128)S(1)}, f32[40,128]{1,0:T(8,128)S(1)}, u32[]{:S(2)}, u32[]{:S(2)}) collective-permute-start(f32[40,128]{1,0:T(8,128)S(1)} %get-tuple-element.24), channel_id=1, source_target_pairs={{1,2},{2,1},{3,4},{4,3},{5,6},{6,5},{9,10},{10,9},{11,12},{12,11},... | collective-permute-start | bytes 61448 | tf_op jit(solution)/shard_map/ppermute | solution.py:482
  14.9 0.1 collective-permute-start.5
  15.6 0.7 %collective-permute-done.4.got_b_ref = f32[40,128]{1,0:T(8,128)S(1)} collective-permute-done((f32[40,128]{1,0:T(8,128)S(1)}, f32[40,128]{1,0:T(8,128)S(1)}, u32[]{:S(2)}, u32[]{:S(2)}) %collective-permute-start.4) | collective-permute-done | bytes 20512 | tf_op jit(solution)/shard_map/ppermute | solution.py:482
  16.3 0.0 collective-permute-done.5.got_a_ref
  16.3 5.7 %shard_map.77 = (f32[3,4,16,256]{3,2,1,0:T(8,128)S(1)}, f32[12,128]{1,0:T(8,128)S(1)}, f32[12,128]{1,0:T(8,128)S(1)}) custom-call(f32[1]{0:T(128)S(6)} %copy.8.bias_ref, bf16[32,4,8,128]{3,2,1,0:T(8,128)(2,1)S(1)} %get-tuple-element.19.f_ref, f32[5,40,128]{2,1,0:T(8,128)S(1)} %get-tuple-element.22.main_ref, f32[4,24,128]{2,1,0:T(8,128)S(1)} %get-tuple-element.23.lab_ref, ...), custom_call_target="tpu_custom_call" | custom-call | tf_op jit(solution)/shard_map/pallas_call | solution.py:464
  22.1 0.1 collective-permute-start.6
  22.2 1.2 %collective-permute-done.6.got_ref = f32[12,128]{1,0:T(8,128)S(1)} collective-permute-done((f32[12,128]{1,0:T(8,128)S(1)}, f32[12,128]{1,0:T(8,128)S(1)}, u32[]{:S(2)}, u32[]{:S(2)}) %collective-permute-start.6) | collective-permute-done | bytes 6176 | tf_op jit(solution)/shard_map/ppermute | solution.py:482
  23.3 2.8 %collective-permute-start.9 = (f32[12,128]{1,0:T(8,128)S(1)}, f32[12,128]{1,0:T(8,128)S(1)}, u32[]{:S(2)}, u32[]{:S(2)}) collective-permute-start(f32[12,128]{1,0:T(8,128)S(1)} %shard_map.78.own_ref), channel_id=1, source_target_pairs={{0,6},{1,7},{2,4},{3,5},{4,2},{5,3},{6,0},{7,1},{8,14},{9,15},{10,... | collective-permute-start | bytes 18440 | tf_op jit(solution)/shard_map/ppermute | solution.py:516
  26.1 0.5 collective-permute-start.8
  26.6 0.1 collective-permute-start.7
  26.7 0.5 collective-permute-done.9.three_ref
  27.1 3.0 %collective-permute-done.8.two_ref = f32[12,128]{1,0:T(8,128)S(1)} collective-permute-done((f32[12,128]{1,0:T(8,128)S(1)}, f32[12,128]{1,0:T(8,128)S(1)}, u32[]{:S(2)}, u32[]{:S(2)}) %collective-permute-start.8) | collective-permute-done | bytes 6176 | tf_op jit(solution)/shard_map/ppermute | solution.py:516
  30.1 0.0 collective-permute-done.7.one_ref
  30.1 25.0 %all_to_all.5.in_ref = f32[96,4,128]{2,1,0:T(4,128)S(1)} all-to-all(f32[96,4,128]{2,1,0:T(4,128)S(1)} %shard_map.79), channel_id=1, replica_groups=mesh['gx'=32,'gy'=8] {'gx'}, dimensions={0} | all-to-all | bytes 393216 | tf_op jit(solution)/shard_map/all_to_all | solution.py:518
  55.1 3.5 %collective-permute-start.10 = (f32[3,4,128]{2,1,0:T(4,128)S(1)}, f32[3,4,128]{2,1,0:T(4,128)S(1)}, u32[]{:S(2)}, u32[]{:S(2)}) collective-permute-start(f32[3,4,128]{2,1,0:T(4,128)S(1)} %shard_map.80.refs_0_.own_ref), channel_id=1, source_target_pairs={{0,1},{1,0},{2,3},{3,2},{4,5},{5,4},{6,7},{7,6},{8,9},{9,8},{10,11... | collective-permute-start | bytes 18440 | tf_op jit(solution)/shard_map/ppermute | solution.py:482
  58.7 0.8 %shard_map.81.feature_ref = bf16[32,4,8,128]{3,2,1,0:T(8,128)(2,1)S(1)} custom-call(f32[3,4,128]{2,1,0:T(4,128)S(1)} %shard_map.80.refs_0_.own_ref, f32[3,4,16,256]{3,2,1,0:T(8,128)S(1)} %get-tuple-element.28.refs_1_, bf16[144,256]{1,0:T(8,128)(2,1)S(1)} %get-tuple-element.29.refs_2_), custom_call_target="tpu_custom_call" | custom-call | tf_op jit(solution)/shard_map/pallas_call | solution.py:464
  59.5 0.0 collective-permute-done.10.got_ref
  59.5 1.0 %shard_map.82 = (f32[1,1]{1,0:T(1,128)}, f32[27,32]{1,0:T(8,128)}, f32[1,1]{1,0:T(1,128)}, bf16[32,4,8,128]{3,2,1,0:T(8,128)(2,1)}) custom-call(f32[3,4,128]{2,1,0:T(4,128)S(1)} %shard_map.80.refs_0_.own_ref, f32[3,4,128]{2,1,0:T(4,128)S(1)} %collective-permute-done.10.got_ref, bf16[32,4,8,128]{3,2,1,0:T(8,128)(2,1)S(1)} %shard_map.81.feature_ref), custom_call_target="tpu_custom_call" | custom-call | tf_op jit(solution)/shard_map/pallas_call | solution.py:464
  (3 shorter events, 0.1 us)
Async XLA Ops:
  2.1 8.3 %collective-permute-start.1 = (f32[88,128]{1,0:T(8,128)S(1)}, f32[88,128]{1,0:T(8,128)S(1)}, u32[]{:S(2)}, u32[]{:S(2)}) collective-permute-start(f32[88,128]{1,0:T(8,128)S(1)} %get-tuple-element.21), channel_id=1, source_target_pairs={{0,16},{16,0},{8,24},{24,8},{32,48},{48,32},{40,56},{56,40},{64,80... | collective-permute-start | bytes 135176 | tf_op jit(solution)/shard_map/ppermute | solution.py:482
  6.0 4.4 %collective-permute-start = (f32[88,128]{1,0:T(8,128)S(1)}, f32[88,128]{1,0:T(8,128)S(1)}, u32[]{:S(2)}, u32[]{:S(2)}) collective-permute-start(f32[88,128]{1,0:T(8,128)S(1)} %get-tuple-element.21), channel_id=1, source_target_pairs={{16,32},{32,16},{24,40},{40,24},{48,64},{64,48},{56,72},{72,56},{8... | collective-permute-start | bytes 135176 | tf_op jit(solution)/shard_map/ppermute | solution.py:482
  6.6 3.8 %collective-permute-start.3 = (f32[80,128]{1,0:T(8,128)S(1)}, f32[80,128]{1,0:T(8,128)S(1)}, u32[]{:S(2)}, u32[]{:S(2)}) collective-permute-start(f32[80,128]{1,0:T(8,128)S(1)} %get-tuple-element.20.own_ref), channel_id=1, source_target_pairs={{0,8},{8,0},{16,24},{24,16},{32,40},{40,32},{48,56},{56,48},{64,72... | collective-permute-start | bytes 122888 | tf_op jit(solution)/shard_map/ppermute | solution.py:482
  8.3 2.0 %collective-permute-start.2 = (f32[80,128]{1,0:T(8,128)S(1)}, f32[80,128]{1,0:T(8,128)S(1)}, u32[]{:S(2)}, u32[]{:S(2)}) collective-permute-start(f32[80,128]{1,0:T(8,128)S(1)} %get-tuple-element.20.own_ref), channel_id=1, source_target_pairs={{8,16},{16,8},{24,32},{32,24},{40,48},{48,40},{56,64},{64,56},{72,... | collective-permute-start | bytes 122888 | tf_op jit(solution)/shard_map/ppermute | solution.py:482
  10.6 5.7 %collective-permute-start.4 = (f32[40,128]{1,0:T(8,128)S(1)}, f32[40,128]{1,0:T(8,128)S(1)}, u32[]{:S(2)}, u32[]{:S(2)}) collective-permute-start(f32[40,128]{1,0:T(8,128)S(1)} %get-tuple-element.24), channel_id=1, source_target_pairs={{1,2},{2,1},{3,4},{4,3},{5,6},{6,5},{9,10},{10,9},{11,12},{12,11},... | collective-permute-start | bytes 61448 | tf_op jit(solution)/shard_map/ppermute | solution.py:482
  14.9 1.5 %collective-permute-start.5 = (f32[40,128]{1,0:T(8,128)S(1)}, f32[40,128]{1,0:T(8,128)S(1)}, u32[]{:S(2)}, u32[]{:S(2)}) collective-permute-start(f32[40,128]{1,0:T(8,128)S(1)} %get-tuple-element.25), channel_id=1, source_target_pairs={{0,1},{1,0},{2,3},{3,2},{4,5},{5,4},{6,7},{7,6},{8,9},{9,8},{10,11... | collective-permute-start | bytes 61448 | tf_op jit(solution)/shard_map/ppermute | solution.py:482
  22.1 1.3 %collective-permute-start.6 = (f32[12,128]{1,0:T(8,128)S(1)}, f32[12,128]{1,0:T(8,128)S(1)}, u32[]{:S(2)}, u32[]{:S(2)}) collective-permute-start(f32[12,128]{1,0:T(8,128)S(1)} %get-tuple-element.27), channel_id=1, source_target_pairs={{0,1},{1,0},{2,3},{3,2},{4,5},{5,4},{6,7},{7,6},{8,9},{9,8},{10,11... | collective-permute-start | bytes 18440 | tf_op jit(solution)/shard_map/ppermute | solution.py:482
  23.3 3.8 %collective-permute-start.9 = (f32[12,128]{1,0:T(8,128)S(1)}, f32[12,128]{1,0:T(8,128)S(1)}, u32[]{:S(2)}, u32[]{:S(2)}) collective-permute-start(f32[12,128]{1,0:T(8,128)S(1)} %shard_map.78.own_ref), channel_id=1, source_target_pairs={{0,6},{1,7},{2,4},{3,5},{4,2},{5,3},{6,0},{7,1},{8,14},{9,15},{10,... | collective-permute-start | bytes 18440 | tf_op jit(solution)/shard_map/ppermute | solution.py:516
  26.1 4.0 %collective-permute-start.8 = (f32[12,128]{1,0:T(8,128)S(1)}, f32[12,128]{1,0:T(8,128)S(1)}, u32[]{:S(2)}, u32[]{:S(2)}) collective-permute-start(f32[12,128]{1,0:T(8,128)S(1)} %shard_map.78.own_ref), channel_id=1, source_target_pairs={{0,4},{1,5},{2,6},{3,7},{4,0},{5,1},{6,2},{7,3},{8,12},{9,13},{10,... | collective-permute-start | bytes 18440 | tf_op jit(solution)/shard_map/ppermute | solution.py:516
  26.6 3.5 %collective-permute-start.7 = (f32[12,128]{1,0:T(8,128)S(1)}, f32[12,128]{1,0:T(8,128)S(1)}, u32[]{:S(2)}, u32[]{:S(2)}) collective-permute-start(f32[12,128]{1,0:T(8,128)S(1)} %shard_map.78.own_ref), channel_id=1, source_target_pairs={{0,2},{1,3},{2,0},{3,1},{4,6},{5,7},{6,4},{7,5},{8,10},{9,11},{10,... | collective-permute-start | bytes 18440 | tf_op jit(solution)/shard_map/ppermute | solution.py:516
  55.1 4.4 %collective-permute-start.10 = (f32[3,4,128]{2,1,0:T(4,128)S(1)}, f32[3,4,128]{2,1,0:T(4,128)S(1)}, u32[]{:S(2)}, u32[]{:S(2)}) collective-permute-start(f32[3,4,128]{2,1,0:T(4,128)S(1)} %shard_map.80.refs_0_.own_ref), channel_id=1, source_target_pairs={{0,1},{1,0},{2,3},{3,2},{4,5},{5,4},{6,7},{7,6},{8,9},{9,8},{10,11... | collective-permute-start | bytes 18440 | tf_op jit(solution)/shard_map/ppermute | solution.py:482

commit v8 on v7

--- a/solution.py
+++ b/solution.py
@@ -181,33 +181,31 @@
     return 1.0 / x
 
 
-def forward(e0, q0, inside, crop, keep):
+def forward_step(i, state, inside, crop, keep):
     def middle(x):
         return x[8:32] if crop else x
 
-    e, q, s = e0, q0, None
-    for i in range(ITERS + 1):
-        e = [jnp.where(inside, x, 1.0) for x in cross(e, 1.0)]
-        q_next = [inverse(x) for x in e]
-        mean = box(q_next, 1.0, crop)
-        s_next = []
-        for z in range(4):
-            d_inv = inverse(mean[z] * (1.0 / 27.0))
-            qz = middle(q[z])
-            ratio = qz * d_inv
-            ratio = ratio * ratio
-            log_term = jnp.log(1.0 + ratio)
-            change = SOFT * log_term
-            if i == 0:
-                s_next.append(change)
-                keep(i, z, qz, d_inv, ratio, None, None, None)
-            else:
-                rest = 1.0 - s[z]
-                power = jnp.exp(log_term * rest)
-                s_next.append(s[z] + SOFT * jnp.log(1.0 + power))
-                keep(i, z, qz, d_inv, ratio, change, rest, power)
-        s, q = s_next, q_next
-    return s, q
+    e, q, s = state
+    e = [jnp.where(inside, x, 1.0) for x in cross(e, 1.0)]
+    q_next = [inverse(x) for x in e]
+    mean = box(q_next, 1.0, crop)
+    s_next = []
+    for z in range(4):
+        d_inv = inverse(mean[z] * (1.0 / 27.0))
+        qz = middle(q[z])
+        ratio = qz * d_inv
+        ratio = ratio * ratio
+        log_term = jnp.log(1.0 + ratio)
+        change = SOFT * log_term
+        if i == 0:
+            s_next.append(change)
+            keep(i, z, qz, d_inv, ratio, None, None, None)
+        else:
+            rest = 1.0 - s[z]
+            power = jnp.exp(log_term * rest)
+            s_next.append(s[z] + SOFT * jnp.log(1.0 + power))
+            keep(i, z, qz, d_inv, ratio, change, rest, power)
+    return e, q_next, s_next
 
 
 def skeleton_kernel(
@@ -259,10 +257,10 @@
         labels.append(jnp.concatenate([lab_ref[z], lab_tail], axis=1))
 
     low, high = jnp.exp(-SHARP * jnp.ones((24, 256), F32)), jnp.exp(SHARP * jnp.ones((24, 256), F32))
-    true_skel, _ = forward(
+    true_state = (
         [jnp.where(x > 0.5, low, 1.0) for x in labels],
         [jnp.where(x > 0.5, high, 1.0) for x in labels],
-        inner_b, False, lambda *factors: None,
+        None,
     )
 
     def keep(i, z, qz, d_inv, ratio, change, rest, power):
@@ -275,7 +273,12 @@
             gain_ref[i, z] = 1.0 - share * change
         rs_ref[i, z] = part
 
-    pred_skel, q_last = forward(e0, q0, inside, True, keep)
+    pred_state = (e0, q0, None)
+    for i in range(ITERS + 1):
+        true_state = forward_step(i, true_state, inner_b, False, lambda *factors: None)
+        pred_state = forward_step(i, pred_state, inside, True, keep)
+    true_skel = true_state[2]
+    q_last, pred_skel = pred_state[1], pred_state[2]
 
     def own(x):
         return x[8:16, :128]
@@ -351,11 +354,17 @@
     groups = [[picked[(b,) + at] for at in order[:24]] for b in range(3)]
     rest = [picked[(b,) + at] for b in range(3) for at in order[24:]]
     groups.append(rest + [jnp.zeros((15, 256), F32)])
-    result = jnp.zeros((24, 128), F32)
-    for b in range(4):
-        stacked = jnp.concatenate(groups[b], axis=0)
-        collect = jnp.where((iota((256, 128), 0) >> 3) + 32 * b == iota((256, 128), 1), 1.0, 0.0)
-        result = result + dot(stacked, collect, ((1,), (0,)), precision=lax.Precision.HIGHEST)
+    stacked = jnp.concatenate([row for rows in groups for row in rows], axis=0)
+    high = stacked.astype(BF16)
+    left_over = stacked - high.astype(F32)
+    middle = left_over.astype(BF16)
+    low = (left_over - middle.astype(F32)).astype(BF16)
+    collect = jnp.where((iota((256, 128), 0) >> 3) == iota((256, 128), 1), 1.0, 0.0).astype(BF16)
+    summed = dot(jnp.concatenate([high, middle, low], axis=0), collect, ((1,), (0,)))
+    summed = summed[:96] + summed[96:192] + summed[192:]
+    result = summed[:24]
+    for b in range(1, 4):
+        result = result + pltpu.roll(summed[24 * b : 24 * b + 24], 32 * b, 1)
     row24, lane_of = iota((24, 128), 0), iota((24, 128), 1)
     for k, value in enumerate([t0, t1, t2, t3] + bias_sums):
         result = jnp.where(((row24 == 11) | (row24 == 23)) & (lane_of == 96 + k), value, result)

time: 60.9 us -> 60.6 us (level)
  no operation moved by 1% of the time
where the time goes in v8:
time: 60.6 us; the launch traced here: 60.3 us
  blocking collectives  25 us (41%)
  starting transfers between devices  18.3 us (30%)
  Pallas kernels  9.02 us (15%)
  waiting for transfers between devices  6.68 us (11%)
  between operations  1.38 us (2%)
    all_to_all x1, blocking collectives, local(): sums = lax.all_to_all(sums, 'gx', 0, 0, tiled=True)  25 us
    ppermute x8, starting transfers between devices, swapped(): return lax.ppermute(x, axis, pairs)  14.9 us
    pallas_call x8, Pallas kernels, call(): pl.pallas_call(kernel, out_shape=[jax.ShapeDtypeStruct(shape, dtype) for...  9.02 us
    ppermute x3, waiting for transfers between devices, local(): lax.ppermute(half, 'gy', [(n, n ^ mask) for n in range(gy)])  3.43 us
    ppermute x3, starting transfers between devices, local(): lax.ppermute(half, 'gy', [(n, n ^ mask) for n in range(gy)])  3.36 us
    ppermute x8, waiting for transfers between devices, swapped(): return lax.ppermute(x, axis, pairs)  3.25 us
  transfers between devices with their start and end apart: 11, of which 5 were waited for; matrix products, arithmetic and copies ran while one was open for 0% of the time, Pallas kernels for 1%

profile of v8, /device:TPU:1, one launch (start us, length us, event | category | flops | bytes accessed | tf_op | source)
XLA Modules:
  0.0 60.3 jit_solution(17951113386577267899)
XLA Ops:
  0.6 1.4 %shard_map.75 = (bf16[144,256]{1,0:T(8,128)(2,1)S(1)}, f32[80,128]{1,0:T(8,128)S(1)}, f32[88,128]{1,0:T(8,128)S(1)}, bf16[32,4,8,128]{3,2,1,0:T(8,128)(2,1)S(1)}) custom-call(bf16[27,32]{1,0:T(8,128)(2,1)} %w_hbm.1, bf16[32,4,8,128]{3,2,1,0:T(8,128)(2,1)} %f_hbm.1, s32[4,8,128]{2,1,0:T(8,128)} %lab_hbm.1), custom_call_target="tpu_custom_call" | custom-call | tf_op jit(solution)/shard_map/pallas_call | solution.py:473
  2.1 3.9 %collective-permute-start.1 = (f32[88,128]{1,0:T(8,128)S(1)}, f32[88,128]{1,0:T(8,128)S(1)}, u32[]{:S(2)}, u32[]{:S(2)}) collective-permute-start(f32[88,128]{1,0:T(8,128)S(1)} %get-tuple-element.21), channel_id=1, source_target_pairs={{0,16},{16,0},{8,24},{24,8},{32,48},{48,32},{40,56},{56,40},{64,80... | collective-permute-start | bytes 135176 | tf_op jit(solution)/shard_map/ppermute | solution.py:491
  6.0 0.7 %collective-permute-start = (f32[88,128]{1,0:T(8,128)S(1)}, f32[88,128]{1,0:T(8,128)S(1)}, u32[]{:S(2)}, u32[]{:S(2)}) collective-permute-start(f32[88,128]{1,0:T(8,128)S(1)} %get-tuple-element.21), channel_id=1, source_target_pairs={{16,32},{32,16},{24,40},{40,24},{48,64},{64,48},{56,72},{72,56},{8... | collective-permute-start | bytes 135176 | tf_op jit(solution)/shard_map/ppermute | solution.py:491
  6.6 1.7 %collective-permute-start.3 = (f32[80,128]{1,0:T(8,128)S(1)}, f32[80,128]{1,0:T(8,128)S(1)}, u32[]{:S(2)}, u32[]{:S(2)}) collective-permute-start(f32[80,128]{1,0:T(8,128)S(1)} %get-tuple-element.20.own_ref), channel_id=1, source_target_pairs={{0,8},{8,0},{16,24},{24,16},{32,40},{40,32},{48,56},{56,48},{64,72... | collective-permute-start | bytes 122888 | tf_op jit(solution)/shard_map/ppermute | solution.py:491
  8.3 0.7 %collective-permute-start.2 = (f32[80,128]{1,0:T(8,128)S(1)}, f32[80,128]{1,0:T(8,128)S(1)}, u32[]{:S(2)}, u32[]{:S(2)}) collective-permute-start(f32[80,128]{1,0:T(8,128)S(1)} %get-tuple-element.20.own_ref), channel_id=1, source_target_pairs={{8,16},{16,8},{24,32},{32,24},{40,48},{48,40},{56,64},{64,56},{72,... | collective-permute-start | bytes 122888 | tf_op jit(solution)/shard_map/ppermute | solution.py:491
  9.0 1.4 %collective-permute-done.3.one_a_ref = f32[80,128]{1,0:T(8,128)S(1)} collective-permute-done((f32[80,128]{1,0:T(8,128)S(1)}, f32[80,128]{1,0:T(8,128)S(1)}, u32[]{:S(2)}, u32[]{:S(2)}) %collective-permute-start.3) | collective-permute-done | bytes 40992 | tf_op jit(solution)/shard_map/ppermute | solution.py:491
  10.4 0.0 collective-permute-done.2.one_b_ref
  10.4 0.0 collective-permute-done.1.two_a_ref
  10.4 0.0 collective-permute-done.two_b_ref
  10.4 0.2 shard_map.76
  10.6 4.3 %collective-permute-start.4 = (f32[40,128]{1,0:T(8,128)S(1)}, f32[40,128]{1,0:T(8,128)S(1)}, u32[]{:S(2)}, u32[]{:S(2)}) collective-permute-start(f32[40,128]{1,0:T(8,128)S(1)} %get-tuple-element.24), channel_id=1, source_target_pairs={{1,2},{2,1},{3,4},{4,3},{5,6},{6,5},{9,10},{10,9},{11,12},{12,11},... | collective-permute-start | bytes 61448 | tf_op jit(solution)/shard_map/ppermute | solution.py:491
  14.9 0.1 collective-permute-start.5
  15.6 0.7 %collective-permute-done.4.got_b_ref = f32[40,128]{1,0:T(8,128)S(1)} collective-permute-done((f32[40,128]{1,0:T(8,128)S(1)}, f32[40,128]{1,0:T(8,128)S(1)}, u32[]{:S(2)}, u32[]{:S(2)}) %collective-permute-start.4) | collective-permute-done | bytes 20512 | tf_op jit(solution)/shard_map/ppermute | solution.py:491
  16.3 0.0 collective-permute-done.5.got_a_ref
  16.3 5.5 %shard_map.77 = (f32[3,4,16,256]{3,2,1,0:T(8,128)S(1)}, f32[12,128]{1,0:T(8,128)S(1)}, f32[12,128]{1,0:T(8,128)S(1)}) custom-call(f32[1]{0:T(128)S(6)} %copy.8.bias_ref, bf16[32,4,8,128]{3,2,1,0:T(8,128)(2,1)S(1)} %get-tuple-element.19.f_ref, f32[5,40,128]{2,1,0:T(8,128)S(1)} %get-tuple-element.22.main_ref, f32[4,24,128]{2,1,0:T(8,128)S(1)} %get-tuple-element.23.lab_ref, ...), custom_call_target="tpu_custom_call" | custom-call | tf_op jit(solution)/shard_map/pallas_call | solution.py:473
  21.8 0.1 collective-permute-start.6
  21.9 1.2 %collective-permute-done.6.got_ref = f32[12,128]{1,0:T(8,128)S(1)} collective-permute-done((f32[12,128]{1,0:T(8,128)S(1)}, f32[12,128]{1,0:T(8,128)S(1)}, u32[]{:S(2)}, u32[]{:S(2)}) %collective-permute-start.6) | collective-permute-done | bytes 6176 | tf_op jit(solution)/shard_map/ppermute | solution.py:491
  23.1 2.8 %collective-permute-start.9 = (f32[12,128]{1,0:T(8,128)S(1)}, f32[12,128]{1,0:T(8,128)S(1)}, u32[]{:S(2)}, u32[]{:S(2)}) collective-permute-start(f32[12,128]{1,0:T(8,128)S(1)} %shard_map.78.own_ref), channel_id=1, source_target_pairs={{0,6},{1,7},{2,4},{3,5},{4,2},{5,3},{6,0},{7,1},{8,14},{9,15},{10,... | collective-permute-start | bytes 18440 | tf_op jit(solution)/shard_map/ppermute | solution.py:525
  25.9 0.5 collective-permute-start.8
  26.4 0.1 collective-permute-start.7
  26.5 0.5 collective-permute-done.9.three_ref
  26.9 3.0 %collective-permute-done.8.two_ref = f32[12,128]{1,0:T(8,128)S(1)} collective-permute-done((f32[12,128]{1,0:T(8,128)S(1)}, f32[12,128]{1,0:T(8,128)S(1)}, u32[]{:S(2)}, u32[]{:S(2)}) %collective-permute-start.8) | collective-permute-done | bytes 6176 | tf_op jit(solution)/shard_map/ppermute | solution.py:525
  29.9 0.0 collective-permute-done.7.one_ref
  29.9 25.0 %all_to_all.5.in_ref = f32[96,4,128]{2,1,0:T(4,128)S(1)} all-to-all(f32[96,4,128]{2,1,0:T(4,128)S(1)} %shard_map.79), channel_id=1, replica_groups=mesh['gx'=32,'gy'=8] {'gx'}, dimensions={0} | all-to-all | bytes 393216 | tf_op jit(solution)/shard_map/all_to_all | solution.py:527
  54.9 3.5 %collective-permute-start.10 = (f32[3,4,128]{2,1,0:T(4,128)S(1)}, f32[3,4,128]{2,1,0:T(4,128)S(1)}, u32[]{:S(2)}, u32[]{:S(2)}) collective-permute-start(f32[3,4,128]{2,1,0:T(4,128)S(1)} %shard_map.80.refs_0_.own_ref), channel_id=1, source_target_pairs={{0,1},{1,0},{2,3},{3,2},{4,5},{5,4},{6,7},{7,6},{8,9},{9,8},{10,11... | collective-permute-start | bytes 18440 | tf_op jit(solution)/shard_map/ppermute | solution.py:491
  58.4 0.8 %shard_map.81.feature_ref = bf16[32,4,8,128]{3,2,1,0:T(8,128)(2,1)S(1)} custom-call(f32[3,4,128]{2,1,0:T(4,128)S(1)} %shard_map.80.refs_0_.own_ref, f32[3,4,16,256]{3,2,1,0:T(8,128)S(1)} %get-tuple-element.28.refs_1_, bf16[144,256]{1,0:T(8,128)(2,1)S(1)} %get-tuple-element.29.refs_2_), custom_call_target="tpu_custom_call" | custom-call | tf_op jit(solution)/shard_map/pallas_call | solution.py:473
  59.3 0.0 collective-permute-done.10.got_ref
  59.3 1.0 %shard_map.82 = (f32[1,1]{1,0:T(1,128)}, f32[27,32]{1,0:T(8,128)}, f32[1,1]{1,0:T(1,128)}, bf16[32,4,8,128]{3,2,1,0:T(8,128)(2,1)}) custom-call(f32[3,4,128]{2,1,0:T(4,128)S(1)} %shard_map.80.refs_0_.own_ref, f32[3,4,128]{2,1,0:T(4,128)S(1)} %collective-permute-done.10.got_ref, bf16[32,4,8,128]{3,2,1,0:T(8,128)(2,1)S(1)} %shard_map.81.feature_ref), custom_call_target="tpu_custom_call" | custom-call | tf_op jit(solution)/shard_map/pallas_call | solution.py:473
  (3 shorter events, 0.1 us)
Async XLA Ops:
  2.1 8.3 %collective-permute-start.1 = (f32[88,128]{1,0:T(8,128)S(1)}, f32[88,128]{1,0:T(8,128)S(1)}, u32[]{:S(2)}, u32[]{:S(2)}) collective-permute-start(f32[88,128]{1,0:T(8,128)S(1)} %get-tuple-element.21), channel_id=1, source_target_pairs={{0,16},{16,0},{8,24},{24,8},{32,48},{48,32},{40,56},{56,40},{64,80... | collective-permute-start | bytes 135176 | tf_op jit(solution)/shard_map/ppermute | solution.py:491
  6.0 4.4 %collective-permute-start = (f32[88,128]{1,0:T(8,128)S(1)}, f32[88,128]{1,0:T(8,128)S(1)}, u32[]{:S(2)}, u32[]{:S(2)}) collective-permute-start(f32[88,128]{1,0:T(8,128)S(1)} %get-tuple-element.21), channel_id=1, source_target_pairs={{16,32},{32,16},{24,40},{40,24},{48,64},{64,48},{56,72},{72,56},{8... | collective-permute-start | bytes 135176 | tf_op jit(solution)/shard_map/ppermute | solution.py:491
  6.6 3.8 %collective-permute-start.3 = (f32[80,128]{1,0:T(8,128)S(1)}, f32[80,128]{1,0:T(8,128)S(1)}, u32[]{:S(2)}, u32[]{:S(2)}) collective-permute-start(f32[80,128]{1,0:T(8,128)S(1)} %get-tuple-element.20.own_ref), channel_id=1, source_target_pairs={{0,8},{8,0},{16,24},{24,16},{32,40},{40,32},{48,56},{56,48},{64,72... | collective-permute-start | bytes 122888 | tf_op jit(solution)/shard_map/ppermute | solution.py:491
  8.3 2.0 %collective-permute-start.2 = (f32[80,128]{1,0:T(8,128)S(1)}, f32[80,128]{1,0:T(8,128)S(1)}, u32[]{:S(2)}, u32[]{:S(2)}) collective-permute-start(f32[80,128]{1,0:T(8,128)S(1)} %get-tuple-element.20.own_ref), channel_id=1, source_target_pairs={{8,16},{16,8},{24,32},{32,24},{40,48},{48,40},{56,64},{64,56},{72,... | collective-permute-start | bytes 122888 | tf_op jit(solution)/shard_map/ppermute | solution.py:491
  10.6 5.7 %collective-permute-start.4 = (f32[40,128]{1,0:T(8,128)S(1)}, f32[40,128]{1,0:T(8,128)S(1)}, u32[]{:S(2)}, u32[]{:S(2)}) collective-permute-start(f32[40,128]{1,0:T(8,128)S(1)} %get-tuple-element.24), channel_id=1, source_target_pairs={{1,2},{2,1},{3,4},{4,3},{5,6},{6,5},{9,10},{10,9},{11,12},{12,11},... | collective-permute-start | bytes 61448 | tf_op jit(solution)/shard_map/ppermute | solution.py:491
  14.9 1.5 %collective-permute-start.5 = (f32[40,128]{1,0:T(8,128)S(1)}, f32[40,128]{1,0:T(8,128)S(1)}, u32[]{:S(2)}, u32[]{:S(2)}) collective-permute-start(f32[40,128]{1,0:T(8,128)S(1)} %get-tuple-element.25), channel_id=1, source_target_pairs={{0,1},{1,0},{2,3},{3,2},{4,5},{5,4},{6,7},{7,6},{8,9},{9,8},{10,11... | collective-permute-start | bytes 61448 | tf_op jit(solution)/shard_map/ppermute | solution.py:491
  21.8 1.3 %collective-permute-start.6 = (f32[12,128]{1,0:T(8,128)S(1)}, f32[12,128]{1,0:T(8,128)S(1)}, u32[]{:S(2)}, u32[]{:S(2)}) collective-permute-start(f32[12,128]{1,0:T(8,128)S(1)} %get-tuple-element.27), channel_id=1, source_target_pairs={{0,1},{1,0},{2,3},{3,2},{4,5},{5,4},{6,7},{7,6},{8,9},{9,8},{10,11... | collective-permute-start | bytes 18440 | tf_op jit(solution)/shard_map/ppermute | solution.py:491
  23.1 3.8 %collective-permute-start.9 = (f32[12,128]{1,0:T(8,128)S(1)}, f32[12,128]{1,0:T(8,128)S(1)}, u32[]{:S(2)}, u32[]{:S(2)}) collective-permute-start(f32[12,128]{1,0:T(8,128)S(1)} %shard_map.78.own_ref), channel_id=1, source_target_pairs={{0,6},{1,7},{2,4},{3,5},{4,2},{5,3},{6,0},{7,1},{8,14},{9,15},{10,... | collective-permute-start | bytes 18440 | tf_op jit(solution)/shard_map/ppermute | solution.py:525
  25.9 4.0 %collective-permute-start.8 = (f32[12,128]{1,0:T(8,128)S(1)}, f32[12,128]{1,0:T(8,128)S(1)}, u32[]{:S(2)}, u32[]{:S(2)}) collective-permute-start(f32[12,128]{1,0:T(8,128)S(1)} %shard_map.78.own_ref), channel_id=1, source_target_pairs={{0,4},{1,5},{2,6},{3,7},{4,0},{5,1},{6,2},{7,3},{8,12},{9,13},{10,... | collective-permute-start | bytes 18440 | tf_op jit(solution)/shard_map/ppermute | solution.py:525
  26.4 3.5 %collective-permute-start.7 = (f32[12,128]{1,0:T(8,128)S(1)}, f32[12,128]{1,0:T(8,128)S(1)}, u32[]{:S(2)}, u32[]{:S(2)}) collective-permute-start(f32[12,128]{1,0:T(8,128)S(1)} %shard_map.78.own_ref), channel_id=1, source_target_pairs={{0,2},{1,3},{2,0},{3,1},{4,6},{5,7},{6,4},{7,5},{8,10},{9,11},{10,... | collective-permute-start | bytes 18440 | tf_op jit(solution)/shard_map/ppermute | solution.py:525
  54.9 4.4 %collective-permute-start.10 = (f32[3,4,128]{2,1,0:T(4,128)S(1)}, f32[3,4,128]{2,1,0:T(4,128)S(1)}, u32[]{:S(2)}, u32[]{:S(2)}) collective-permute-start(f32[3,4,128]{2,1,0:T(4,128)S(1)} %shard_map.80.refs_0_.own_ref), channel_id=1, source_target_pairs={{0,1},{1,0},{2,3},{3,2},{4,5},{5,4},{6,7},{7,6},{8,9},{9,8},{10,11... | collective-permute-start | bytes 18440 | tf_op jit(solution)/shard_map/ppermute | solution.py:491

commit v9 on v8

--- a/solution.py
+++ b/solution.py
@@ -191,9 +191,9 @@
     mean = box(q_next, 1.0, crop)
     s_next = []
     for z in range(4):
-        d_inv = inverse(mean[z] * (1.0 / 27.0))
+        d_inv = inverse(mean[z])
         qz = middle(q[z])
-        ratio = qz * d_inv
+        ratio = (27.0 * qz) * d_inv
         ratio = ratio * ratio
         log_term = jnp.log(1.0 + ratio)
         change = SOFT * log_term
@@ -301,16 +301,17 @@
             coefs.append(rs_ref[i, z] * running[z])
             if i > 0:
                 running[z] = running[z] * gain_ref[i, z]
+        q_of = [q_last[z][8:32] if i == ITERS else qs_ref[i + 1, z] for z in range(4)]
+        q_of = [(x * x) * inner for x in q_of]
         for f in range(2):
             scaled = [coefs[z] * weights[f][z] for z in range(4)]
             spread = box([scaled[z] * ds_ref[i, z] for z in range(4)], 0.0, False)
-            q_of = [q_last[z][8:32] if i == ITERS else qs_ref[i + 1, z] for z in range(4)]
             incoming = []
             for z in range(4):
-                value = spread[z] * (q_of[z] * q_of[z]) * (-1.0 / 27.0)
-                if deep[f] is not None:
-                    value = value + deep[f][z]
-                incoming.append(value * inner)
+                if deep[f] is None:
+                    incoming.append(-(spread[z] * q_of[z]))
+                else:
+                    incoming.append(deep[f][z] * inner - spread[z] * q_of[z])
             moved = cross(incoming, 0.0)
             deep[f] = [moved[z] + scaled[z] * qs_ref[i, z] for z in range(4)]
     fields = [

time: 60.6 us -> 60.7 us (level)
  no operation moved by 1% of the time
where the time goes in v9:
time: 60.7 us; the launch traced here: 60.4 us
  blocking collectives  25 us (41%)
  starting transfers between devices  18.3 us (30%)
  Pallas kernels  9.07 us (15%)
  waiting for transfers between devices  6.68 us (11%)
  between operations  1.38 us (2%)
    all_to_all x1, blocking collectives, local(): sums = lax.all_to_all(sums, 'gx', 0, 0, tiled=True)  25 us
    ppermute x8, starting transfers between devices, swapped(): return lax.ppermute(x, axis, pairs)  14.9 us
    pallas_call x8, Pallas kernels, call(): pl.pallas_call(kernel, out_shape=[jax.ShapeDtypeStruct(shape, dtype) for...  9.07 us
    ppermute x3, waiting for transfers between devices, local(): lax.ppermute(half, 'gy', [(n, n ^ mask) for n in range(gy)])  3.43 us
    ppermute x3, starting transfers between devices, local(): lax.ppermute(half, 'gy', [(n, n ^ mask) for n in range(gy)])  3.36 us
    ppermute x8, waiting for transfers between devices, swapped(): return lax.ppermute(x, axis, pairs)  3.25 us
  transfers between devices with their start and end apart: 11, of which 5 were waited for; matrix products, arithmetic and copies ran while one was open for 0% of the time, Pallas kernels for 1%

profile of v9, /device:TPU:1, one launch (start us, length us, event | category | flops | bytes accessed | tf_op | source)
XLA Modules:
  0.0 60.4 jit_solution(12599841934201241746)
XLA Ops:
  0.6 1.4 %shard_map.75 = (bf16[144,256]{1,0:T(8,128)(2,1)S(1)}, f32[80,128]{1,0:T(8,128)S(1)}, f32[88,128]{1,0:T(8,128)S(1)}, bf16[32,4,8,128]{3,2,1,0:T(8,128)(2,1)S(1)}) custom-call(bf16[27,32]{1,0:T(8,128)(2,1)} %w_hbm.1, bf16[32,4,8,128]{3,2,1,0:T(8,128)(2,1)} %f_hbm.1, s32[4,8,128]{2,1,0:T(8,128)} %lab_hbm.1), custom_call_target="tpu_custom_call" | custom-call | tf_op jit(solution)/shard_map/pallas_call | solution.py:474
  2.1 3.9 %collective-permute-start.1 = (f32[88,128]{1,0:T(8,128)S(1)}, f32[88,128]{1,0:T(8,128)S(1)}, u32[]{:S(2)}, u32[]{:S(2)}) collective-permute-start(f32[88,128]{1,0:T(8,128)S(1)} %get-tuple-element.21), channel_id=1, source_target_pairs={{0,16},{16,0},{8,24},{24,8},{32,48},{48,32},{40,56},{56,40},{64,80... | collective-permute-start | bytes 135176 | tf_op jit(solution)/shard_map/ppermute | solution.py:492
  6.0 0.7 %collective-permute-start = (f32[88,128]{1,0:T(8,128)S(1)}, f32[88,128]{1,0:T(8,128)S(1)}, u32[]{:S(2)}, u32[]{:S(2)}) collective-permute-start(f32[88,128]{1,0:T(8,128)S(1)} %get-tuple-element.21), channel_id=1, source_target_pairs={{16,32},{32,16},{24,40},{40,24},{48,64},{64,48},{56,72},{72,56},{8... | collective-permute-start | bytes 135176 | tf_op jit(solution)/shard_map/ppermute | solution.py:492
  6.6 1.7 %collective-permute-start.3 = (f32[80,128]{1,0:T(8,128)S(1)}, f32[80,128]{1,0:T(8,128)S(1)}, u32[]{:S(2)}, u32[]{:S(2)}) collective-permute-start(f32[80,128]{1,0:T(8,128)S(1)} %get-tuple-element.20.own_ref), channel_id=1, source_target_pairs={{0,8},{8,0},{16,24},{24,16},{32,40},{40,32},{48,56},{56,48},{64,72... | collective-permute-start | bytes 122888 | tf_op jit(solution)/shard_map/ppermute | solution.py:492
  8.3 0.7 %collective-permute-start.2 = (f32[80,128]{1,0:T(8,128)S(1)}, f32[80,128]{1,0:T(8,128)S(1)}, u32[]{:S(2)}, u32[]{:S(2)}) collective-permute-start(f32[80,128]{1,0:T(8,128)S(1)} %get-tuple-element.20.own_ref), channel_id=1, source_target_pairs={{8,16},{16,8},{24,32},{32,24},{40,48},{48,40},{56,64},{64,56},{72,... | collective-permute-start | bytes 122888 | tf_op jit(solution)/shard_map/ppermute | solution.py:492
  9.0 1.4 %collective-permute-done.3.one_a_ref = f32[80,128]{1,0:T(8,128)S(1)} collective-permute-done((f32[80,128]{1,0:T(8,128)S(1)}, f32[80,128]{1,0:T(8,128)S(1)}, u32[]{:S(2)}, u32[]{:S(2)}) %collective-permute-start.3) | collective-permute-done | bytes 40992 | tf_op jit(solution)/shard_map/ppermute | solution.py:492
  10.4 0.0 collective-permute-done.2.one_b_ref
  10.4 0.0 collective-permute-done.1.two_a_ref
  10.4 0.0 collective-permute-done.two_b_ref
  10.4 0.2 shard_map.76
  10.6 4.3 %collective-permute-start.4 = (f32[40,128]{1,0:T(8,128)S(1)}, f32[40,128]{1,0:T(8,128)S(1)}, u32[]{:S(2)}, u32[]{:S(2)}) collective-permute-start(f32[40,128]{1,0:T(8,128)S(1)} %get-tuple-element.24), channel_id=1, source_target_pairs={{1,2},{2,1},{3,4},{4,3},{5,6},{6,5},{9,10},{10,9},{11,12},{12,11},... | collective-permute-start | bytes 61448 | tf_op jit(solution)/shard_map/ppermute | solution.py:492
  14.9 0.1 collective-permute-start.5
  15.6 0.7 %collective-permute-done.4.got_b_ref = f32[40,128]{1,0:T(8,128)S(1)} collective-permute-done((f32[40,128]{1,0:T(8,128)S(1)}, f32[40,128]{1,0:T(8,128)S(1)}, u32[]{:S(2)}, u32[]{:S(2)}) %collective-permute-start.4) | collective-permute-done | bytes 20512 | tf_op jit(solution)/shard_map/ppermute | solution.py:492
  16.3 0.0 collective-permute-done.5.got_a_ref
  16.3 5.6 %shard_map.77 = (f32[3,4,16,256]{3,2,1,0:T(8,128)S(1)}, f32[12,128]{1,0:T(8,128)S(1)}, f32[12,128]{1,0:T(8,128)S(1)}) custom-call(f32[1]{0:T(128)S(6)} %copy.8.bias_ref, bf16[32,4,8,128]{3,2,1,0:T(8,128)(2,1)S(1)} %get-tuple-element.19.f_ref, f32[5,40,128]{2,1,0:T(8,128)S(1)} %get-tuple-element.22.main_ref, f32[4,24,128]{2,1,0:T(8,128)S(1)} %get-tuple-element.23.lab_ref, ...), custom_call_target="tpu_custom_call" | custom-call | tf_op jit(solution)/shard_map/pallas_call | solution.py:474
  21.9 0.1 collective-permute-start.6
  22.0 1.2 %collective-permute-done.6.got_ref = f32[12,128]{1,0:T(8,128)S(1)} collective-permute-done((f32[12,128]{1,0:T(8,128)S(1)}, f32[12,128]{1,0:T(8,128)S(1)}, u32[]{:S(2)}, u32[]{:S(2)}) %collective-permute-start.6) | collective-permute-done | bytes 6176 | tf_op jit(solution)/shard_map/ppermute | solution.py:492
  23.1 2.8 %collective-permute-start.9 = (f32[12,128]{1,0:T(8,128)S(1)}, f32[12,128]{1,0:T(8,128)S(1)}, u32[]{:S(2)}, u32[]{:S(2)}) collective-permute-start(f32[12,128]{1,0:T(8,128)S(1)} %shard_map.78.own_ref), channel_id=1, source_target_pairs={{0,6},{1,7},{2,4},{3,5},{4,2},{5,3},{6,0},{7,1},{8,14},{9,15},{10,... | collective-permute-start | bytes 18440 | tf_op jit(solution)/shard_map/ppermute | solution.py:526
  25.9 0.5 collective-permute-start.8
  26.4 0.1 collective-permute-start.7
  26.5 0.5 collective-permute-done.9.three_ref
  27.0 3.0 %collective-permute-done.8.two_ref = f32[12,128]{1,0:T(8,128)S(1)} collective-permute-done((f32[12,128]{1,0:T(8,128)S(1)}, f32[12,128]{1,0:T(8,128)S(1)}, u32[]{:S(2)}, u32[]{:S(2)}) %collective-permute-start.8) | collective-permute-done | bytes 6176 | tf_op jit(solution)/shard_map/ppermute | solution.py:526
  29.9 0.0 collective-permute-done.7.one_ref
  30.0 25.0 %all_to_all.5.in_ref = f32[96,4,128]{2,1,0:T(4,128)S(1)} all-to-all(f32[96,4,128]{2,1,0:T(4,128)S(1)} %shard_map.79), channel_id=1, replica_groups=mesh['gx'=32,'gy'=8] {'gx'}, dimensions={0} | all-to-all | bytes 393216 | tf_op jit(solution)/shard_map/all_to_all | solution.py:528
  55.0 3.5 %collective-permute-start.10 = (f32[3,4,128]{2,1,0:T(4,128)S(1)}, f32[3,4,128]{2,1,0:T(4,128)S(1)}, u32[]{:S(2)}, u32[]{:S(2)}) collective-permute-start(f32[3,4,128]{2,1,0:T(4,128)S(1)} %shard_map.80.refs_0_.own_ref), channel_id=1, source_target_pairs={{0,1},{1,0},{2,3},{3,2},{4,5},{5,4},{6,7},{7,6},{8,9},{9,8},{10,11... | collective-permute-start | bytes 18440 | tf_op jit(solution)/shard_map/ppermute | solution.py:492
  58.5 0.8 %shard_map.81.feature_ref = bf16[32,4,8,128]{3,2,1,0:T(8,128)(2,1)S(1)} custom-call(f32[3,4,128]{2,1,0:T(4,128)S(1)} %shard_map.80.refs_0_.own_ref, f32[3,4,16,256]{3,2,1,0:T(8,128)S(1)} %get-tuple-element.28.refs_1_, bf16[144,256]{1,0:T(8,128)(2,1)S(1)} %get-tuple-element.29.refs_2_), custom_call_target="tpu_custom_call" | custom-call | tf_op jit(solution)/shard_map/pallas_call | solution.py:474
  59.3 0.0 collective-permute-done.10.got_ref
  59.3 1.0 %shard_map.82 = (f32[1,1]{1,0:T(1,128)}, f32[27,32]{1,0:T(8,128)}, f32[1,1]{1,0:T(1,128)}, bf16[32,4,8,128]{3,2,1,0:T(8,128)(2,1)}) custom-call(f32[3,4,128]{2,1,0:T(4,128)S(1)} %shard_map.80.refs_0_.own_ref, f32[3,4,128]{2,1,0:T(4,128)S(1)} %collective-permute-done.10.got_ref, bf16[32,4,8,128]{3,2,1,0:T(8,128)(2,1)S(1)} %shard_map.81.feature_ref), custom_call_target="tpu_custom_call" | custom-call | tf_op jit(solution)/shard_map/pallas_call | solution.py:474
  (3 shorter events, 0.1 us)
Async XLA Ops:
  2.1 8.3 %collective-permute-start.1 = (f32[88,128]{1,0:T(8,128)S(1)}, f32[88,128]{1,0:T(8,128)S(1)}, u32[]{:S(2)}, u32[]{:S(2)}) collective-permute-start(f32[88,128]{1,0:T(8,128)S(1)} %get-tuple-element.21), channel_id=1, source_target_pairs={{0,16},{16,0},{8,24},{24,8},{32,48},{48,32},{40,56},{56,40},{64,80... | collective-permute-start | bytes 135176 | tf_op jit(solution)/shard_map/ppermute | solution.py:492
  6.0 4.4 %collective-permute-start = (f32[88,128]{1,0:T(8,128)S(1)}, f32[88,128]{1,0:T(8,128)S(1)}, u32[]{:S(2)}, u32[]{:S(2)}) collective-permute-start(f32[88,128]{1,0:T(8,128)S(1)} %get-tuple-element.21), channel_id=1, source_target_pairs={{16,32},{32,16},{24,40},{40,24},{48,64},{64,48},{56,72},{72,56},{8... | collective-permute-start | bytes 135176 | tf_op jit(solution)/shard_map/ppermute | solution.py:492
  6.6 3.8 %collective-permute-start.3 = (f32[80,128]{1,0:T(8,128)S(1)}, f32[80,128]{1,0:T(8,128)S(1)}, u32[]{:S(2)}, u32[]{:S(2)}) collective-permute-start(f32[80,128]{1,0:T(8,128)S(1)} %get-tuple-element.20.own_ref), channel_id=1, source_target_pairs={{0,8},{8,0},{16,24},{24,16},{32,40},{40,32},{48,56},{56,48},{64,72... | collective-permute-start | bytes 122888 | tf_op jit(solution)/shard_map/ppermute | solution.py:492
  8.3 2.0 %collective-permute-start.2 = (f32[80,128]{1,0:T(8,128)S(1)}, f32[80,128]{1,0:T(8,128)S(1)}, u32[]{:S(2)}, u32[]{:S(2)}) collective-permute-start(f32[80,128]{1,0:T(8,128)S(1)} %get-tuple-element.20.own_ref), channel_id=1, source_target_pairs={{8,16},{16,8},{24,32},{32,24},{40,48},{48,40},{56,64},{64,56},{72,... | collective-permute-start | bytes 122888 | tf_op jit(solution)/shard_map/ppermute | solution.py:492
  10.6 5.7 %collective-permute-start.4 = (f32[40,128]{1,0:T(8,128)S(1)}, f32[40,128]{1,0:T(8,128)S(1)}, u32[]{:S(2)}, u32[]{:S(2)}) collective-permute-start(f32[40,128]{1,0:T(8,128)S(1)} %get-tuple-element.24), channel_id=1, source_target_pairs={{1,2},{2,1},{3,4},{4,3},{5,6},{6,5},{9,10},{10,9},{11,12},{12,11},... | collective-permute-start | bytes 61448 | tf_op jit(solution)/shard_map/ppermute | solution.py:492
  14.9 1.5 %collective-permute-start.5 = (f32[40,128]{1,0:T(8,128)S(1)}, f32[40,128]{1,0:T(8,128)S(1)}, u32[]{:S(2)}, u32[]{:S(2)}) collective-permute-start(f32[40,128]{1,0:T(8,128)S(1)} %get-tuple-element.25), channel_id=1, source_target_pairs={{0,1},{1,0},{2,3},{3,2},{4,5},{5,4},{6,7},{7,6},{8,9},{9,8},{10,11... | collective-permute-start | bytes 61448 | tf_op jit(solution)/shard_map/ppermute | solution.py:492
  21.9 1.3 %collective-permute-start.6 = (f32[12,128]{1,0:T(8,128)S(1)}, f32[12,128]{1,0:T(8,128)S(1)}, u32[]{:S(2)}, u32[]{:S(2)}) collective-permute-start(f32[12,128]{1,0:T(8,128)S(1)} %get-tuple-element.27), channel_id=1, source_target_pairs={{0,1},{1,0},{2,3},{3,2},{4,5},{5,4},{6,7},{7,6},{8,9},{9,8},{10,11... | collective-permute-start | bytes 18440 | tf_op jit(solution)/shard_map/ppermute | solution.py:492
  23.1 3.8 %collective-permute-start.9 = (f32[12,128]{1,0:T(8,128)S(1)}, f32[12,128]{1,0:T(8,128)S(1)}, u32[]{:S(2)}, u32[]{:S(2)}) collective-permute-start(f32[12,128]{1,0:T(8,128)S(1)} %shard_map.78.own_ref), channel_id=1, source_target_pairs={{0,6},{1,7},{2,4},{3,5},{4,2},{5,3},{6,0},{7,1},{8,14},{9,15},{10,... | collective-permute-start | bytes 18440 | tf_op jit(solution)/shard_map/ppermute | solution.py:526
  25.9 4.0 %collective-permute-start.8 = (f32[12,128]{1,0:T(8,128)S(1)}, f32[12,128]{1,0:T(8,128)S(1)}, u32[]{:S(2)}, u32[]{:S(2)}) collective-permute-start(f32[12,128]{1,0:T(8,128)S(1)} %shard_map.78.own_ref), channel_id=1, source_target_pairs={{0,4},{1,5},{2,6},{3,7},{4,0},{5,1},{6,2},{7,3},{8,12},{9,13},{10,... | collective-permute-start | bytes 18440 | tf_op jit(solution)/shard_map/ppermute | solution.py:526
  26.4 3.5 %collective-permute-start.7 = (f32[12,128]{1,0:T(8,128)S(1)}, f32[12,128]{1,0:T(8,128)S(1)}, u32[]{:S(2)}, u32[]{:S(2)}) collective-permute-start(f32[12,128]{1,0:T(8,128)S(1)} %shard_map.78.own_ref), channel_id=1, source_target_pairs={{0,2},{1,3},{2,0},{3,1},{4,6},{5,7},{6,4},{7,5},{8,10},{9,11},{10,... | collective-permute-start | bytes 18440 | tf_op jit(solution)/shard_map/ppermute | solution.py:526
  55.0 4.4 %collective-permute-start.10 = (f32[3,4,128]{2,1,0:T(4,128)S(1)}, f32[3,4,128]{2,1,0:T(4,128)S(1)}, u32[]{:S(2)}, u32[]{:S(2)}) collective-permute-start(f32[3,4,128]{2,1,0:T(4,128)S(1)} %shard_map.80.refs_0_.own_ref), channel_id=1, source_target_pairs={{0,1},{1,0},{2,3},{3,2},{4,5},{5,4},{6,7},{7,6},{8,9},{9,8},{10,11... | collective-permute-start | bytes 18440 | tf_op jit(solution)/shard_map/ppermute | solution.py:492

commit v10 on v9

--- a/solution.py
+++ b/solution.py
@@ -292,8 +292,7 @@
     t2 = total([own(true_skel[z] * probs[z][0]) for z in range(4)])
     t3 = total([own(true_skel[z]) for z in range(4)])
 
-    weights = [labels, [inner] * 4]
-    running = [jnp.ones((24, 256), F32)] * 4
+    running = [inner] * 4
     deep = [None, None]
     for i in range(ITERS, -1, -1):
         coefs = []
@@ -304,7 +303,7 @@
         q_of = [q_last[z][8:32] if i == ITERS else qs_ref[i + 1, z] for z in range(4)]
         q_of = [(x * x) * inner for x in q_of]
         for f in range(2):
-            scaled = [coefs[z] * weights[f][z] for z in range(4)]
+            scaled = [coefs[z] * labels[z] for z in range(4)] if f == 0 else coefs
             spread = box([scaled[z] * ds_ref[i, z] for z in range(4)], 0.0, False)
             incoming = []
             for z in range(4):

time: 60.7 us -> 60.7 us (level)
  no operation moved by 1% of the time
where the time goes in v10:
time: 60.7 us; the launch traced here: 60.4 us
  blocking collectives  25 us (41%)
  starting transfers between devices  18.3 us (30%)
  Pallas kernels  9.08 us (15%)
  waiting for transfers between devices  6.68 us (11%)
  between operations  1.38 us (2%)
    all_to_all x1, blocking collectives, local(): sums = lax.all_to_all(sums, 'gx', 0, 0, tiled=True)  25 us
    ppermute x8, starting transfers between devices, swapped(): return lax.ppermute(x, axis, pairs)  14.9 us
    pallas_call x8, Pallas kernels, call(): pl.pallas_call(kernel, out_shape=[jax.ShapeDtypeStruct(shape, dtype) for...  9.08 us
    ppermute x3, waiting for transfers between devices, local(): lax.ppermute(half, 'gy', [(n, n ^ mask) for n in range(gy)])  3.43 us
    ppermute x3, starting transfers between devices, local(): lax.ppermute(half, 'gy', [(n, n ^ mask) for n in range(gy)])  3.36 us
    ppermute x8, waiting for transfers between devices, swapped(): return lax.ppermute(x, axis, pairs)  3.25 us
  transfers between devices with their start and end apart: 11, of which 5 were waited for; matrix products, arithmetic and copies ran while one was open for 0% of the time, Pallas kernels for 1%

profile of v10, /device:TPU:1, one launch (start us, length us, event | category | flops | bytes accessed | tf_op | source)
XLA Modules:
  0.0 60.4 jit_solution(3936236143986904482)
XLA Ops:
  0.6 1.4 %shard_map.75 = (bf16[144,256]{1,0:T(8,128)(2,1)S(1)}, f32[80,128]{1,0:T(8,128)S(1)}, f32[88,128]{1,0:T(8,128)S(1)}, bf16[32,4,8,128]{3,2,1,0:T(8,128)(2,1)S(1)}) custom-call(bf16[27,32]{1,0:T(8,128)(2,1)} %w_hbm.1, bf16[32,4,8,128]{3,2,1,0:T(8,128)(2,1)} %f_hbm.1, s32[4,8,128]{2,1,0:T(8,128)} %lab_hbm.1), custom_call_target="tpu_custom_call" | custom-call | tf_op jit(solution)/shard_map/pallas_call | solution.py:473
  2.1 3.9 %collective-permute-start.1 = (f32[88,128]{1,0:T(8,128)S(1)}, f32[88,128]{1,0:T(8,128)S(1)}, u32[]{:S(2)}, u32[]{:S(2)}) collective-permute-start(f32[88,128]{1,0:T(8,128)S(1)} %get-tuple-element.21), channel_id=1, source_target_pairs={{0,16},{16,0},{8,24},{24,8},{32,48},{48,32},{40,56},{56,40},{64,80... | collective-permute-start | bytes 135176 | tf_op jit(solution)/shard_map/ppermute | solution.py:491
  6.0 0.7 %collective-permute-start = (f32[88,128]{1,0:T(8,128)S(1)}, f32[88,128]{1,0:T(8,128)S(1)}, u32[]{:S(2)}, u32[]{:S(2)}) collective-permute-start(f32[88,128]{1,0:T(8,128)S(1)} %get-tuple-element.21), channel_id=1, source_target_pairs={{16,32},{32,16},{24,40},{40,24},{48,64},{64,48},{56,72},{72,56},{8... | collective-permute-start | bytes 135176 | tf_op jit(solution)/shard_map/ppermute | solution.py:491
  6.6 1.7 %collective-permute-start.3 = (f32[80,128]{1,0:T(8,128)S(1)}, f32[80,128]{1,0:T(8,128)S(1)}, u32[]{:S(2)}, u32[]{:S(2)}) collective-permute-start(f32[80,128]{1,0:T(8,128)S(1)} %get-tuple-element.20.own_ref), channel_id=1, source_target_pairs={{0,8},{8,0},{16,24},{24,16},{32,40},{40,32},{48,56},{56,48},{64,72... | collective-permute-start | bytes 122888 | tf_op jit(solution)/shard_map/ppermute | solution.py:491
  8.3 0.7 %collective-permute-start.2 = (f32[80,128]{1,0:T(8,128)S(1)}, f32[80,128]{1,0:T(8,128)S(1)}, u32[]{:S(2)}, u32[]{:S(2)}) collective-permute-start(f32[80,128]{1,0:T(8,128)S(1)} %get-tuple-element.20.own_ref), channel_id=1, source_target_pairs={{8,16},{16,8},{24,32},{32,24},{40,48},{48,40},{56,64},{64,56},{72,... | collective-permute-start | bytes 122888 | tf_op jit(solution)/shard_map/ppermute | solution.py:491
  9.0 1.4 %collective-permute-done.3.one_a_ref = f32[80,128]{1,0:T(8,128)S(1)} collective-permute-done((f32[80,128]{1,0:T(8,128)S(1)}, f32[80,128]{1,0:T(8,128)S(1)}, u32[]{:S(2)}, u32[]{:S(2)}) %collective-permute-start.3) | collective-permute-done | bytes 40992 | tf_op jit(solution)/shard_map/ppermute | solution.py:491
  10.4 0.0 collective-permute-done.2.one_b_ref
  10.4 0.0 collective-permute-done.1.two_a_ref
  10.4 0.0 collective-permute-done.two_b_ref
  10.4 0.2 shard_map.76
  10.6 4.3 %collective-permute-start.4 = (f32[40,128]{1,0:T(8,128)S(1)}, f32[40,128]{1,0:T(8,128)S(1)}, u32[]{:S(2)}, u32[]{:S(2)}) collective-permute-start(f32[40,128]{1,0:T(8,128)S(1)} %get-tuple-element.24), channel_id=1, source_target_pairs={{1,2},{2,1},{3,4},{4,3},{5,6},{6,5},{9,10},{10,9},{11,12},{12,11},... | collective-permute-start | bytes 61448 | tf_op jit(solution)/shard_map/ppermute | solution.py:491
  14.9 0.1 collective-permute-start.5
  15.6 0.7 %collective-permute-done.4.got_b_ref = f32[40,128]{1,0:T(8,128)S(1)} collective-permute-done((f32[40,128]{1,0:T(8,128)S(1)}, f32[40,128]{1,0:T(8,128)S(1)}, u32[]{:S(2)}, u32[]{:S(2)}) %collective-permute-start.4) | collective-permute-done | bytes 20512 | tf_op jit(solution)/shard_map/ppermute | solution.py:491
  16.3 0.0 collective-permute-done.5.got_a_ref
  16.3 5.6 %shard_map.77 = (f32[3,4,16,256]{3,2,1,0:T(8,128)S(1)}, f32[12,128]{1,0:T(8,128)S(1)}, f32[12,128]{1,0:T(8,128)S(1)}) custom-call(f32[1]{0:T(128)S(6)} %copy.8.bias_ref, bf16[32,4,8,128]{3,2,1,0:T(8,128)(2,1)S(1)} %get-tuple-element.19.f_ref, f32[5,40,128]{2,1,0:T(8,128)S(1)} %get-tuple-element.22.main_ref, f32[4,24,128]{2,1,0:T(8,128)S(1)} %get-tuple-element.23.lab_ref, ...), custom_call_target="tpu_custom_call" | custom-call | tf_op jit(solution)/shard_map/pallas_call | solution.py:473
  21.9 0.1 collective-permute-start.6
  22.0 1.2 %collective-permute-done.6.got_ref = f32[12,128]{1,0:T(8,128)S(1)} collective-permute-done((f32[12,128]{1,0:T(8,128)S(1)}, f32[12,128]{1,0:T(8,128)S(1)}, u32[]{:S(2)}, u32[]{:S(2)}) %collective-permute-start.6) | collective-permute-done | bytes 6176 | tf_op jit(solution)/shard_map/ppermute | solution.py:491
  23.2 2.8 %collective-permute-start.9 = (f32[12,128]{1,0:T(8,128)S(1)}, f32[12,128]{1,0:T(8,128)S(1)}, u32[]{:S(2)}, u32[]{:S(2)}) collective-permute-start(f32[12,128]{1,0:T(8,128)S(1)} %shard_map.78.own_ref), channel_id=1, source_target_pairs={{0,6},{1,7},{2,4},{3,5},{4,2},{5,3},{6,0},{7,1},{8,14},{9,15},{10,... | collective-permute-start | bytes 18440 | tf_op jit(solution)/shard_map/ppermute | solution.py:525
  25.9 0.5 collective-permute-start.8
  26.4 0.1 collective-permute-start.7
  26.5 0.5 collective-permute-done.9.three_ref
  27.0 3.0 %collective-permute-done.8.two_ref = f32[12,128]{1,0:T(8,128)S(1)} collective-permute-done((f32[12,128]{1,0:T(8,128)S(1)}, f32[12,128]{1,0:T(8,128)S(1)}, u32[]{:S(2)}, u32[]{:S(2)}) %collective-permute-start.8) | collective-permute-done | bytes 6176 | tf_op jit(solution)/shard_map/ppermute | solution.py:525
  29.9 0.0 collective-permute-done.7.one_ref
  30.0 25.0 %all_to_all.5.in_ref = f32[96,4,128]{2,1,0:T(4,128)S(1)} all-to-all(f32[96,4,128]{2,1,0:T(4,128)S(1)} %shard_map.79), channel_id=1, replica_groups=mesh['gx'=32,'gy'=8] {'gx'}, dimensions={0} | all-to-all | bytes 393216 | tf_op jit(solution)/shard_map/all_to_all | solution.py:527
  55.0 3.5 %collective-permute-start.10 = (f32[3,4,128]{2,1,0:T(4,128)S(1)}, f32[3,4,128]{2,1,0:T(4,128)S(1)}, u32[]{:S(2)}, u32[]{:S(2)}) collective-permute-start(f32[3,4,128]{2,1,0:T(4,128)S(1)} %shard_map.80.refs_0_.own_ref), channel_id=1, source_target_pairs={{0,1},{1,0},{2,3},{3,2},{4,5},{5,4},{6,7},{7,6},{8,9},{9,8},{10,11... | collective-permute-start | bytes 18440 | tf_op jit(solution)/shard_map/ppermute | solution.py:491
  58.5 0.8 %shard_map.81.feature_ref = bf16[32,4,8,128]{3,2,1,0:T(8,128)(2,1)S(1)} custom-call(f32[3,4,128]{2,1,0:T(4,128)S(1)} %shard_map.80.refs_0_.own_ref, f32[3,4,16,256]{3,2,1,0:T(8,128)S(1)} %get-tuple-element.28.refs_1_, bf16[144,256]{1,0:T(8,128)(2,1)S(1)} %get-tuple-element.29.refs_2_), custom_call_target="tpu_custom_call" | custom-call | tf_op jit(solution)/shard_map/pallas_call | solution.py:473
  59.3 0.0 collective-permute-done.10.got_ref
  59.3 1.0 %shard_map.82 = (f32[1,1]{1,0:T(1,128)}, f32[27,32]{1,0:T(8,128)}, f32[1,1]{1,0:T(1,128)}, bf16[32,4,8,128]{3,2,1,0:T(8,128)(2,1)}) custom-call(f32[3,4,128]{2,1,0:T(4,128)S(1)} %shard_map.80.refs_0_.own_ref, f32[3,4,128]{2,1,0:T(4,128)S(1)} %collective-permute-done.10.got_ref, bf16[32,4,8,128]{3,2,1,0:T(8,128)(2,1)S(1)} %shard_map.81.feature_ref), custom_call_target="tpu_custom_call" | custom-call | tf_op jit(solution)/shard_map/pallas_call | solution.py:473
  (3 shorter events, 0.1 us)
Async XLA Ops:
  2.1 8.3 %collective-permute-start.1 = (f32[88,128]{1,0:T(8,128)S(1)}, f32[88,128]{1,0:T(8,128)S(1)}, u32[]{:S(2)}, u32[]{:S(2)}) collective-permute-start(f32[88,128]{1,0:T(8,128)S(1)} %get-tuple-element.21), channel_id=1, source_target_pairs={{0,16},{16,0},{8,24},{24,8},{32,48},{48,32},{40,56},{56,40},{64,80... | collective-permute-start | bytes 135176 | tf_op jit(solution)/shard_map/ppermute | solution.py:491
  6.0 4.4 %collective-permute-start = (f32[88,128]{1,0:T(8,128)S(1)}, f32[88,128]{1,0:T(8,128)S(1)}, u32[]{:S(2)}, u32[]{:S(2)}) collective-permute-start(f32[88,128]{1,0:T(8,128)S(1)} %get-tuple-element.21), channel_id=1, source_target_pairs={{16,32},{32,16},{24,40},{40,24},{48,64},{64,48},{56,72},{72,56},{8... | collective-permute-start | bytes 135176 | tf_op jit(solution)/shard_map/ppermute | solution.py:491
  6.6 3.8 %collective-permute-start.3 = (f32[80,128]{1,0:T(8,128)S(1)}, f32[80,128]{1,0:T(8,128)S(1)}, u32[]{:S(2)}, u32[]{:S(2)}) collective-permute-start(f32[80,128]{1,0:T(8,128)S(1)} %get-tuple-element.20.own_ref), channel_id=1, source_target_pairs={{0,8},{8,0},{16,24},{24,16},{32,40},{40,32},{48,56},{56,48},{64,72... | collective-permute-start | bytes 122888 | tf_op jit(solution)/shard_map/ppermute | solution.py:491
  8.3 2.0 %collective-permute-start.2 = (f32[80,128]{1,0:T(8,128)S(1)}, f32[80,128]{1,0:T(8,128)S(1)}, u32[]{:S(2)}, u32[]{:S(2)}) collective-permute-start(f32[80,128]{1,0:T(8,128)S(1)} %get-tuple-element.20.own_ref), channel_id=1, source_target_pairs={{8,16},{16,8},{24,32},{32,24},{40,48},{48,40},{56,64},{64,56},{72,... | collective-permute-start | bytes 122888 | tf_op jit(solution)/shard_map/ppermute | solution.py:491
  10.6 5.7 %collective-permute-start.4 = (f32[40,128]{1,0:T(8,128)S(1)}, f32[40,128]{1,0:T(8,128)S(1)}, u32[]{:S(2)}, u32[]{:S(2)}) collective-permute-start(f32[40,128]{1,0:T(8,128)S(1)} %get-tuple-element.24), channel_id=1, source_target_pairs={{1,2},{2,1},{3,4},{4,3},{5,6},{6,5},{9,10},{10,9},{11,12},{12,11},... | collective-permute-start | bytes 61448 | tf_op jit(solution)/shard_map/ppermute | solution.py:491
  14.9 1.5 %collective-permute-start.5 = (f32[40,128]{1,0:T(8,128)S(1)}, f32[40,128]{1,0:T(8,128)S(1)}, u32[]{:S(2)}, u32[]{:S(2)}) collective-permute-start(f32[40,128]{1,0:T(8,128)S(1)} %get-tuple-element.25), channel_id=1, source_target_pairs={{0,1},{1,0},{2,3},{3,2},{4,5},{5,4},{6,7},{7,6},{8,9},{9,8},{10,11... | collective-permute-start | bytes 61448 | tf_op jit(solution)/shard_map/ppermute | solution.py:491
  21.9 1.3 %collective-permute-start.6 = (f32[12,128]{1,0:T(8,128)S(1)}, f32[12,128]{1,0:T(8,128)S(1)}, u32[]{:S(2)}, u32[]{:S(2)}) collective-permute-start(f32[12,128]{1,0:T(8,128)S(1)} %get-tuple-element.27), channel_id=1, source_target_pairs={{0,1},{1,0},{2,3},{3,2},{4,5},{5,4},{6,7},{7,6},{8,9},{9,8},{10,11... | collective-permute-start | bytes 18440 | tf_op jit(solution)/shard_map/ppermute | solution.py:491
  23.2 3.8 %collective-permute-start.9 = (f32[12,128]{1,0:T(8,128)S(1)}, f32[12,128]{1,0:T(8,128)S(1)}, u32[]{:S(2)}, u32[]{:S(2)}) collective-permute-start(f32[12,128]{1,0:T(8,128)S(1)} %shard_map.78.own_ref), channel_id=1, source_target_pairs={{0,6},{1,7},{2,4},{3,5},{4,2},{5,3},{6,0},{7,1},{8,14},{9,15},{10,... | collective-permute-start | bytes 18440 | tf_op jit(solution)/shard_map/ppermute | solution.py:525
  25.9 4.0 %collective-permute-start.8 = (f32[12,128]{1,0:T(8,128)S(1)}, f32[12,128]{1,0:T(8,128)S(1)}, u32[]{:S(2)}, u32[]{:S(2)}) collective-permute-start(f32[12,128]{1,0:T(8,128)S(1)} %shard_map.78.own_ref), channel_id=1, source_target_pairs={{0,4},{1,5},{2,6},{3,7},{4,0},{5,1},{6,2},{7,3},{8,12},{9,13},{10,... | collective-permute-start | bytes 18440 | tf_op jit(solution)/shard_map/ppermute | solution.py:525
  26.4 3.5 %collective-permute-start.7 = (f32[12,128]{1,0:T(8,128)S(1)}, f32[12,128]{1,0:T(8,128)S(1)}, u32[]{:S(2)}, u32[]{:S(2)}) collective-permute-start(f32[12,128]{1,0:T(8,128)S(1)} %shard_map.78.own_ref), channel_id=1, source_target_pairs={{0,2},{1,3},{2,0},{3,1},{4,6},{5,7},{6,4},{7,5},{8,10},{9,11},{10,... | collective-permute-start | bytes 18440 | tf_op jit(solution)/shard_map/ppermute | solution.py:525
  55.0 4.4 %collective-permute-start.10 = (f32[3,4,128]{2,1,0:T(4,128)S(1)}, f32[3,4,128]{2,1,0:T(4,128)S(1)}, u32[]{:S(2)}, u32[]{:S(2)}) collective-permute-start(f32[3,4,128]{2,1,0:T(4,128)S(1)} %shard_map.80.refs_0_.own_ref), channel_id=1, source_target_pairs={{0,1},{1,0},{2,3},{3,2},{4,5},{5,4},{6,7},{7,6},{8,9},{9,8},{10,11... | collective-permute-start | bytes 18440 | tf_op jit(solution)/shard_map/ppermute | solution.py:491
